TPU v7x, 128 devices: a whole 4x4x4 slice. The times are simulated.
128 devices in a mesh: seq: 8 (over z_lo, x), tp: 16 (over y, z_hi, core).
Axes of the slice: x: 4, y: 4, z: 4 (z_hi: 2, z_lo: 2; z = z_hi * 2 + z_lo), core: 2. Of those that a mesh axis runs over, the one named last changes fastest.
Arguments:
- tokens: bfloat16 [8192, 6144], P(('seq', 'tp')), may hold values from -6 to 6
- w_x: bfloat16 [6144, 8192], P(None, 'tp'), may hold values from -0.078125 to 0.078125
- w_z: bfloat16 [6144, 8192], P(None, 'tp'), may hold values from -0.078125 to 0.078125
- w_bc: bfloat16 [6144, 1024], P(None, 'tp'), may hold values from -0.078125 to 0.078125
- w_dt: bfloat16 [6144, 128], P(None, 'tp'), may hold values from -0.078125 to 0.078125
- conv_x: bfloat16 [4, 8192], P(None, 'tp'), may hold values from -3 to 3
- conv_bc: bfloat16 [4, 1024], P(None, 'tp'), may hold values from -3 to 3
- dt_bias: float32 [128], P('tp'), may hold values from -1.5 to 0.5
- decay_rate: float32 [128], P('tp'), may hold values from 6.1035156e-05 to 0.08
- skip: float32 [128], P('tp'), may hold values from 0 to 2.5
- norm_gain: bfloat16 [8192], P('tp'), may hold values from 0.5 to 1.5
- w_out: bfloat16 [8192, 6144], P('tp'), may hold values from -0.0625 to 0.0625
Outputs:
- mixed: bfloat16 [8192, 6144], P(('seq', 'tp'))
All inputs are finite; a program needn't handle non-finite values.
Results may differ from a plain program's by a relative error of at most 0.023.
Values may be sent and summed in bfloat16 or wider, within the bound.
A program may use at most 128 MiB of HBM per device.

v0:
```python
import jax
import jax.numpy as jnp
from jax import lax
from jax.sharding import PartitionSpec as P

HEAD_DIM = 64
STATE = 128
GROUPS = 4
BLOCK = 256


HIGH = lax.Precision.HIGHEST


def from_behind(value, axis, steps):
    count = lax.axis_size(axis)
    first, last = (max(0, -steps), min(count, count - steps))
    return lax.ppermute(value, axis, [(source, source + steps) for source in range(first, last)])


def from_partner(block, axis, stride):
    count = lax.axis_size(axis)
    route = []
    for low in range(count):
        high = low | 1 << stride
        if high != low and high < count:
            route += [(low, high), (high, low)]
    return lax.ppermute(block, axis, route)


def on_device(
    tokens, w_x, w_z, w_bc, w_dt, conv_x, conv_bc, dt_bias, decay_rate, skip, norm_gain, w_out
):
    col_x = w_x.shape[1]
    col_bc = w_bc.shape[1]
    heads_dev = w_dt.shape[1]
    taps = conv_x.shape[0]
    piece = lax.all_gather(tokens, "tp", axis=0, tiled=True)
    projected = jnp.concatenate(
        [
            jnp.dot(piece, w_x, preferred_element_type=jnp.float32),
            jnp.dot(piece, w_z, preferred_element_type=jnp.float32),
            jnp.dot(piece, w_bc, preferred_element_type=jnp.float32),
            jnp.dot(piece, w_dt, preferred_element_type=jnp.float32),
        ],
        axis=1,
    )
    span_len = projected.shape[0]
    x_in = projected[:, :col_x].astype(jnp.bfloat16)
    z_gate = projected[:, col_x : 2 * col_x].astype(jnp.bfloat16)
    bc_in = projected[:, 2 * col_x : 2 * col_x + col_bc].astype(jnp.bfloat16)
    dt_raw = projected[:, 2 * col_x + col_bc :]
    conv_input = jnp.concatenate([x_in, bc_in], axis=1)
    rim_rows = from_behind(conv_input[span_len - (taps - 1) :], "seq", 1)
    padded = jnp.concatenate([rim_rows, conv_input], axis=0)
    all_taps = jnp.concatenate([conv_x, conv_bc], axis=1).astype(jnp.float32)
    conv_acc = jnp.zeros(conv_input.shape, jnp.float32)
    for index_k in range(taps):
        conv_acc = conv_acc + all_taps[index_k][None, :] * padded[
            index_k : index_k + span_len
        ].astype(jnp.float32)
    conv_out = jax.nn.silu(conv_acc).astype(jnp.bfloat16)
    x_conv = conv_out[:, :col_x]
    own_maps = conv_out[:, col_x:]
    levels = (lax.axis_size("tp") // GROUPS).bit_length() - 1
    held = own_maps
    for level in range(levels):
        partner = from_partner(held, "tp", level)
        upper = lax.axis_index("tp") // 2**level % 2
        held = jnp.where(
            upper == 1,
            jnp.concatenate([partner, held], axis=1),
            jnp.concatenate([held, partner], axis=1),
        )
    b_mat = held[:, :STATE]
    c_mat = held[:, STATE : 2 * STATE]
    dt = jax.nn.softplus(dt_raw + dt_bias[None, :])
    nblocks = span_len // BLOCK
    x_blocks = x_conv.astype(jnp.float32).reshape(nblocks, BLOCK, heads_dev, HEAD_DIM)
    b_blocks = b_mat.astype(jnp.float32).reshape(nblocks, BLOCK, STATE)
    c_blocks = c_mat.astype(jnp.float32).reshape(nblocks, BLOCK, STATE)
    dt_heads = jnp.transpose(dt.reshape(nblocks, BLOCK, heads_dev), (0, 2, 1))
    accum = jnp.cumsum(dt_heads * decay_rate[None, :, None], axis=2)
    causal = (jnp.arange(BLOCK)[:, None] >= jnp.arange(BLOCK)[None, :])[None, None, :, :]
    affinity = jnp.einsum("btn,bsn->bts", c_blocks, b_blocks, precision=HIGH)
    expo = accum[:, :, :, None] - accum[:, :, None, :]
    decay = jnp.where(causal, jnp.exp(-jnp.where(causal, expo, 0.0)), 0.0)
    weights = affinity[:, None, :, :] * decay * dt_heads[:, :, None, :]
    y_intra = jnp.einsum("bhts,bshp->bthp", weights, x_blocks, precision=HIGH)
    tail = jnp.exp(-(accum[:, :, -1:] - accum)) * dt_heads
    contrib = jnp.einsum("bshp,bhs,bsn->bhpn", x_blocks, tail, b_blocks, precision=HIGH)
    block_decay = jnp.exp(-accum[:, :, -1])
    local_state = jnp.zeros((heads_dev, HEAD_DIM, STATE), jnp.float32)
    prefix_decay = jnp.ones((heads_dev,), jnp.float32)
    entry_local = []
    entry_decay = []
    for index_b in range(nblocks):
        entry_local.append(local_state)
        entry_decay.append(prefix_decay)
        local_state = block_decay[index_b][:, None, None] * local_state + contrib[index_b]
        prefix_decay = prefix_decay * block_decay[index_b]
    zero_state = jnp.zeros((heads_dev, HEAD_DIM, STATE), jnp.float32)

    def advance(count, incoming):
        return from_behind(
            (prefix_decay[:, None, None] * incoming + local_state).astype(jnp.bfloat16), "seq", 1
        ).astype(jnp.float32)

    state_in = lax.fori_loop(0, lax.axis_size("seq") - 1, advance, zero_state)
    entry_states = jnp.stack(
        [
            entry_decay[index_b][:, None, None] * state_in + entry_local[index_b]
            for index_b in range(nblocks)
        ],
        axis=0,
    )
    entry_scale = jnp.transpose(jnp.exp(-accum), (0, 2, 1))
    y_inter = entry_scale[..., None] * jnp.einsum(
        "btn,bhpn->bthp", c_blocks, entry_states, precision=HIGH
    )
    y_all = y_intra + y_inter + skip[None, None, :, None] * x_blocks
    y_flat = y_all.reshape(span_len, col_x)
    gated = y_flat * jax.nn.silu(z_gate.astype(jnp.float32))
    squares_sum = lax.psum(jnp.sum(gated * gated, axis=1), "tp")
    mean_sq = squares_sum / (col_x * lax.axis_size("tp")) + 1e-05
    normed = (gated * lax.rsqrt(mean_sq)[:, None] * norm_gain.astype(jnp.float32)[None, :]).astype(
        jnp.bfloat16
    )
    return lax.psum_scatter(
        jnp.dot(normed, w_out, preferred_element_type=jnp.float32).astype(jnp.bfloat16),
        "tp",
        scatter_dimension=0,
        tiled=True,
    )


def solution(mesh):
    placed = (
        P(("seq", "tp"), None),
        P(None, "tp"),
        P(None, "tp"),
        P(None, "tp"),
        P(None, "tp"),
        P(None, "tp"),
        P(None, "tp"),
        P("tp"),
        P("tp"),
        P("tp"),
        P("tp"),
        P("tp", None),
    )
    return jax.shard_map(
        on_device, mesh=mesh, in_specs=placed, out_specs=P(("seq", "tp"), None), check_vma=False
    )
```

profile of v0, /device:TPU:1, one launch (start us, length us, event | category | flops | bytes accessed | tf_op | source)
XLA Modules:
  0.0 419.0 jit_solution(13533606657815817851)
XLA Ops:
  10.0 94.4 %all-gather.2.cloned.1.call-done = bf16[1024,6144]{1,0:T(8,128)(2,1)} async-done(((bf16[64,6144]{1,0:T(8,128)(2,1)}), bf16[1024,6144]{1,0:T(8,128)(2,1)}) %all-gather.2.cloned.1.call-update) | async-done | bytes 12582928 | tf_op jit(solution)/shard_map/all_gather | solution.py:38
  104.4 8.0 %compare_select_fusion = f32[1024,8]{0,1:T(8,128)S(1)} fusion(bf16[1024,6144]{1,0:T(8,128)(2,1)} %all-gather.2.cloned.1.call-done, bf16[6144,8]{0,1:T(8,128)(2,1)} %param.18, f32[8]{0:T(128)} %param.21), kind=kOutput, calls=%fused_computation.76 | convolution fusion | flops 100720640 | bytes 12714016 | tf_op jit(solution)/shard_map/dot_general | solution.py:44
  112.5 2.3 reduce-window.6
  115.2 8.5 %convolution_convert_fusion.3 = bf16[1024,64]{0,1:T(8,128)(2,1)S(1)} fusion(bf16[1024,6144]{1,0:T(8,128)(2,1)} %all-gather.2.cloned.1.call-done, bf16[6144,64]{0,1:T(8,128)(2,1)S(1)} %copy-done), kind=kOutput, calls=%fused_computation.38 | convolution fusion | flops 805371904 | bytes 13500416 | tf_op jit(solution)/shard_map/dot_general | solution.py:43
  123.7 11.6 %convolution_convert_fusion.2 = bf16[1024,512]{0,1:T(8,128)(2,1)S(1)} fusion(bf16[1024,6144]{1,0:T(8,128)(2,1)} %all-gather.2.cloned.1.call-done, bf16[6144,512]{1,0:T(8,128)(2,1)} %param.15), kind=kOutput, calls=%fused_computation.36 | convolution fusion | flops 6442975232 | bytes 19922944 | tf_op jit(solution)/shard_map/dot_general | solution.py:41
  135.4 3.1 collective-permute-start.1
  138.5 3.0 collective-permute-done.1
  142.2 2.7 multiply_convert_fusion
  149.0 7.4 %collective-permute-done.3 = bf16[1024,128]{0,1:T(8,128)(2,1)S(1)} collective-permute-done((bf16[1024,128]{0,1:T(8,128)(2,1)S(1)}, bf16[1024,128]{0,1:T(8,128)(2,1)S(1)}, u32[]{:S(2)}, u32[]{:S(2)}) %collective-permute-start.3) | collective-permute-done | bytes 262176 | tf_op jit(solution)/shard_map/ppermute | solution.py:28
  160.4 46.6 %while.11 = (s32[]{:T(128)}, f32[8,64,128]{2,1,0:T(8,128)S(1)}, f32[8]{0:T(128)S(1)}, f32[8,64,128]{2,1,0:T(8,128)S(1)}, s32[]{:T(128)}, /*index=5*/s32[]{:T(128)}) while((s32[]{:T(128)}, f32[8,64,128]{2,1,0:T(8,128)S(1)}, f32[8]{0:T(128)S(1)}, f32[8,64,128]{2,1,0:T(8,128)S(1)}, s32[]{:T(128)}, /*index=5*/s32[]{:T(128)}) %tuple.37), condition=%wide.region_3.4_spmd.clone, body=%wide.region_2.3_spmd.clone.sunk | while | flops 327683 | bytes 1573015 | solution.py:109
  160.5 4.1 collective-permute-start
  164.6 1.9 collective-permute-done
  166.7 3.8 collective-permute-start
  170.5 1.9 collective-permute-done
  172.5 3.8 collective-permute-start
  178.4 3.8 collective-permute-start
  184.2 4.8 %collective-permute-start = (bf16[8,64,128]{2,1,0:T(8,128)(2,1)S(1)}, bf16[8,64,128]{2,1,0:T(8,128)(2,1)S(1)}, u32[]{:S(2)}, u32[]{:S(2)}) collective-permute-start(bf16[8,64,128]{2,1,0:T(8,128)(2,1)S(1)} %fusion.72), channel_id=1, source_target_pairs={{0,16},{16,32},{32,48},{48,64},{64,80},{80,96},{96,112},{1,17},{17... | collective-permute-start | bytes 393224 | tf_op jit(solution)/shard_map/while/body/eval_jaxpr/ppermute | solution.py:18
  191.1 5.9 %collective-permute-start = (bf16[8,64,128]{2,1,0:T(8,128)(2,1)S(1)}, bf16[8,64,128]{2,1,0:T(8,128)(2,1)S(1)}, u32[]{:S(2)}, u32[]{:S(2)}) collective-permute-start(bf16[8,64,128]{2,1,0:T(8,128)(2,1)S(1)} %fusion.72), channel_id=1, source_target_pairs={{0,16},{16,32},{32,48},{48,64},{64,80},{80,96},{96,112},{1,17},{17... | collective-permute-start | bytes 393224 | tf_op jit(solution)/shard_map/while/body/eval_jaxpr/ppermute | solution.py:18
  199.1 5.9 %collective-permute-start = (bf16[8,64,128]{2,1,0:T(8,128)(2,1)S(1)}, bf16[8,64,128]{2,1,0:T(8,128)(2,1)S(1)}, u32[]{:S(2)}, u32[]{:S(2)}) collective-permute-start(bf16[8,64,128]{2,1,0:T(8,128)(2,1)S(1)} %fusion.72), channel_id=1, source_target_pairs={{0,16},{16,32},{32,48},{48,64},{64,80},{80,96},{96,112},{1,17},{17... | collective-permute-start | bytes 393224 | tf_op jit(solution)/shard_map/while/body/eval_jaxpr/ppermute | solution.py:18
  208.2 6.5 %fusion.23 = f32[4,256,8,64]{1,3,2,0:T(8,128)S(1)} fusion(f32[4,256,8,64]{1,3,2,0:T(8,128)S(1)} %fusion.26, f32[4,8,256]{2,1,0:T(8,128)S(1)} %bitcast.115, f32[4,8,256]{2,1,0:T(8,128)S(1)} %get-tuple-element.56, f32[4,256,256]{2,1,0:T(8,128)S(1)} %copy-done.2, pred[256,256]{1,0:T(8,128)(4,1)S(1)} %copy-done.3, f32[8]{0:T(128)S(1)} %copy-done.8, ...), kind=kOutput, calls=%fused_computation.29 | convolution fusion | flops 1625817088 | bytes 6455328 | tf_op jit(solution)/shard_map/bhts,bshp->bthp/dot_general | solution.py:89
  216.6 12.2 %multiply_reduce_fusion = (f32[1024]{0:T(1024)S(1)}, f32[1024,512]{0,1:T(8,128)S(1)}) fusion(f32[1024,512]{0,1:T(8,128)S(1)} %bitcast.110, bf16[1024,6144]{1,0:T(8,128)(2,1)} %all-gather.2.cloned.1.call-done, bf16[6144,512]{1,0:T(8,128)(2,1)} %param.16), kind=kOutput, calls=%fused_computation.32 | convolution fusion | flops 6447168512 | bytes 23072768 | tf_op jit(solution)/shard_map/dot_general | solution.py:42
  228.8 40.8 %psum.7 = f32[1024]{0:T(1024)S(1)} all-reduce(f32[1024]{0:T(1024)S(1)} %get-tuple-element.72), channel_id=1, replica_groups=mesh['seq'=8,'tp'=16] {'tp'}, use_global_device_ids=true, to_apply=%region_5.6 | all-reduce | flops 1024 | bytes 8192 | tf_op jit(solution)/shard_map/psum | solution.py:124
  269.6 12.6 %convolution_convert_fusion = bf16[1024,6144]{1,0:T(8,128)(2,1)} fusion(bf16[512,6144]{1,0:T(8,128)(2,1)} %param.25, f32[1024,512]{0,1:T(8,128)S(1)} %get-tuple-element.73, f32[512]{0:T(512)S(1)} %copy-done.6, f32[1024]{0:T(1024)S(1)} %add_rsqrt_fusion), kind=kOutput, calls=%fused_computation.3 | convolution fusion | flops 6450315264 | bytes 20977664 | tf_op jit(solution)/shard_map/dot_general | solution.py:130
  282.2 129.9 %reduce-scatter.2.cloned.1.call-done = bf16[64,6144]{1,0:T(8,128)(2,1)} async-done(((bf16[1024,6144]{1,0:T(8,128)(2,1)}), bf16[64,6144]{1,0:T(8,128)(2,1)}) %reduce-scatter.2.cloned.1.call-update) | async-done | bytes 786448 | tf_op jit(solution)/shard_map/reduce_scatter | solution.py:129
  (79 shorter events, 26.3 us)
Async XLA Ops:
  6.5 108.7 %copy-start = (bf16[6144,64]{0,1:T(8,128)(2,1)S(1)}, bf16[6144,64]{0,1:T(8,128)(2,1)}, u32[]{:S(2)}) copy-start(bf16[6144,64]{0,1:T(8,128)(2,1)} %param.17) | copy-start | bytes 2359300
  6.5 97.9 %all-gather.2.cloned.1.call-start = ((), (), s32[]{:S(2)}) async-start(), calls=%async_computation.1 | async-start | bytes 13369344 | tf_op jit(solution)/shard_map/all_gather | solution.py:38
  7.3 404.9 %reduce-scatter.2.cloned.1.call-start = ((), (), s32[]{:S(2)}) async-start(), calls=%async_computation.2 | async-start | bytes 13369344 | tf_op jit(solution)/shard_map/reduce_scatter | solution.py:129
  10.0 102.4 %copy-start.7 = (f32[8]{0:T(128)S(1)}, f32[8]{0:T(128)}, u32[]{:S(2)}) copy-start(f32[8]{0:T(128)} %param.22) | copy-start | bytes 100
  135.4 6.1 %collective-permute-start.1 = (bf16[3,576]{0,1:T(8,128)(2,1)S(1)}, bf16[3,576]{0,1:T(8,128)(2,1)S(1)}, u32[]{:S(2)}, u32[]{:S(2)}) collective-permute-start(bf16[3,576]{0,1:T(8,128)(2,1)S(1)} %fusion.50), channel_id=1, source_target_pairs={{0,16},{16,32},{32,48},{48,64},{64,80},{80,96},{96,112},{1,17},{17... | collective-permute-start | bytes 10376 | tf_op jit(solution)/shard_map/ppermute | solution.py:18
  144.9 2.3 collective-permute-start.2
  147.3 9.1 %collective-permute-start.3 = (bf16[1024,128]{0,1:T(8,128)(2,1)S(1)}, bf16[1024,128]{0,1:T(8,128)(2,1)S(1)}, u32[]{:S(2)}, u32[]{:S(2)}) collective-permute-start(bf16[1024,128]{0,1:T(8,128)(2,1)S(1)} %maximum_select_fusion.1), channel_id=1, source_target_pairs={{0,2},{2,0},{1,3},{3,1},{4,6},{6,4},{5,7},{7,5},{8,10},{10,8},{9,1... | collective-permute-start | bytes 786440 | tf_op jit(solution)/shard_map/ppermute | solution.py:28
  160.3 46.6 %copy-start.4 = (f32[8]{0:T(128)S(1)}, f32[8]{0:T(128)}, u32[]{:S(2)}) copy-start(f32[8]{0:T(128)} %get-tuple-element.61) | copy-start | bytes 100
  160.3 46.6 %copy-start.5 = (f32[8]{0:T(128)S(1)}, f32[8]{0:T(128)}, u32[]{:S(2)}) copy-start(f32[8]{0:T(128)} %get-tuple-element.67) | copy-start | bytes 100
  160.5 6.1 %collective-permute-start = (bf16[8,64,128]{2,1,0:T(8,128)(2,1)S(1)}, bf16[8,64,128]{2,1,0:T(8,128)(2,1)S(1)}, u32[]{:S(2)}, u32[]{:S(2)}) collective-permute-start(bf16[8,64,128]{2,1,0:T(8,128)(2,1)S(1)} %fusion.72), channel_id=1, source_target_pairs={{0,16},{16,32},{32,48},{48,64},{64,80},{80,96},{96,112},{1,17},{17... | collective-permute-start | bytes 393224 | tf_op jit(solution)/shard_map/while/body/eval_jaxpr/ppermute | solution.py:18
  166.7 5.7 %collective-permute-start = (bf16[8,64,128]{2,1,0:T(8,128)(2,1)S(1)}, bf16[8,64,128]{2,1,0:T(8,128)(2,1)S(1)}, u32[]{:S(2)}, u32[]{:S(2)}) collective-permute-start(bf16[8,64,128]{2,1,0:T(8,128)(2,1)S(1)} %fusion.72), channel_id=1, source_target_pairs={{0,16},{16,32},{32,48},{48,64},{64,80},{80,96},{96,112},{1,17},{17... | collective-permute-start | bytes 393224 | tf_op jit(solution)/shard_map/while/body/eval_jaxpr/ppermute | solution.py:18
  172.5 5.7 %collective-permute-start = (bf16[8,64,128]{2,1,0:T(8,128)(2,1)S(1)}, bf16[8,64,128]{2,1,0:T(8,128)(2,1)S(1)}, u32[]{:S(2)}, u32[]{:S(2)}) collective-permute-start(bf16[8,64,128]{2,1,0:T(8,128)(2,1)S(1)} %fusion.72), channel_id=1, source_target_pairs={{0,16},{16,32},{32,48},{48,64},{64,80},{80,96},{96,112},{1,17},{17... | collective-permute-start | bytes 393224 | tf_op jit(solution)/shard_map/while/body/eval_jaxpr/ppermute | solution.py:18
  178.4 5.7 %collective-permute-start = (bf16[8,64,128]{2,1,0:T(8,128)(2,1)S(1)}, bf16[8,64,128]{2,1,0:T(8,128)(2,1)S(1)}, u32[]{:S(2)}, u32[]{:S(2)}) collective-permute-start(bf16[8,64,128]{2,1,0:T(8,128)(2,1)S(1)} %fusion.72), channel_id=1, source_target_pairs={{0,16},{16,32},{32,48},{48,64},{64,80},{80,96},{96,112},{1,17},{17... | collective-permute-start | bytes 393224 | tf_op jit(solution)/shard_map/while/body/eval_jaxpr/ppermute | solution.py:18
  184.2 6.8 %collective-permute-start = (bf16[8,64,128]{2,1,0:T(8,128)(2,1)S(1)}, bf16[8,64,128]{2,1,0:T(8,128)(2,1)S(1)}, u32[]{:S(2)}, u32[]{:S(2)}) collective-permute-start(bf16[8,64,128]{2,1,0:T(8,128)(2,1)S(1)} %fusion.72), channel_id=1, source_target_pairs={{0,16},{16,32},{32,48},{48,64},{64,80},{80,96},{96,112},{1,17},{17... | collective-permute-start | bytes 393224 | tf_op jit(solution)/shard_map/while/body/eval_jaxpr/ppermute | solution.py:18
  191.1 7.8 %collective-permute-start = (bf16[8,64,128]{2,1,0:T(8,128)(2,1)S(1)}, bf16[8,64,128]{2,1,0:T(8,128)(2,1)S(1)}, u32[]{:S(2)}, u32[]{:S(2)}) collective-permute-start(bf16[8,64,128]{2,1,0:T(8,128)(2,1)S(1)} %fusion.72), channel_id=1, source_target_pairs={{0,16},{16,32},{32,48},{48,64},{64,80},{80,96},{96,112},{1,17},{17... | collective-permute-start | bytes 393224 | tf_op jit(solution)/shard_map/while/body/eval_jaxpr/ppermute | solution.py:18
  199.1 7.8 %collective-permute-start = (bf16[8,64,128]{2,1,0:T(8,128)(2,1)S(1)}, bf16[8,64,128]{2,1,0:T(8,128)(2,1)S(1)}, u32[]{:S(2)}, u32[]{:S(2)}) collective-permute-start(bf16[8,64,128]{2,1,0:T(8,128)(2,1)S(1)} %fusion.72), channel_id=1, source_target_pairs={{0,16},{16,32},{32,48},{48,64},{64,80},{80,96},{96,112},{1,17},{17... | collective-permute-start | bytes 393224 | tf_op jit(solution)/shard_map/while/body/eval_jaxpr/ppermute | solution.py:18
  207.0 1.2 copy-start.2
  207.0 1.2 copy-start.3
  207.0 1.2 copy-start.8
  216.6 53.0 %copy-start.6 = (f32[512]{0:T(512)S(1)}, f32[512]{0:T(512)}, u32[]{:S(2)}) copy-start(f32[512]{0:T(512)} %convert_element_type.58) | copy-start | bytes 6148
  282.2 129.9 %copy-start.1 = (bf16[6144,64]{0,1:T(8,128)(2,1)S(1)}, bf16[6144,64]{0,1:T(8,128)(2,1)}, u32[]{:S(2)}) copy-start(bf16[6144,64]{0,1:T(8,128)(2,1)} %param.17) | copy-start | bytes 2359300
Sparse Core Ops, SparseCore 0:
  9.8 94.6 all-gather.1
  282.4 129.7 reduce-scatter.1
where the time goes:
time: 419 us
  waiting for transfers between devices  249 us (59%)
  matrix products  63 us (15%)
  blocking collectives  40.8 us (10%)
  starting transfers between devices  36.7 us (9%)
  between operations  13.7 us (3%)
  other arithmetic  11.1 us (3%)
    reduce_scatter x1, waiting for transfers between devices, on_device(): lax.psum_scatter(jnp.dot(normed, w_out, preferred_element_type=jnp.float3...  130 us
    all_gather x1, waiting for transfers between devices, on_device(): piece = lax.all_gather(tokens, 'tp', axis=0, tiled=True)  94.4 us
    psum x1, blocking collectives, on_device(): squares_sum = lax.psum(jnp.sum(gated * gated, axis=1), 'tp')  40.8 us
    ppermute x8, starting transfers between devices, from_behind(): lax.ppermute(value, axis, [(source, source + steps) for source in range(f...  35.2 us
    ppermute x8, waiting for transfers between devices, from_behind(): lax.ppermute(value, axis, [(source, source + steps) for source in range(f...  16.4 us
    dot_general x1, matrix products, on_device(): jnp.dot(normed, w_out, preferred_element_type=jnp.float32)  12.6 us
    dot_general x1, matrix products, on_device(): jnp.dot(piece, w_z, preferred_element_type=jnp.float32)  12.2 us
    dot_general x1, matrix products, on_device(): jnp.dot(piece, w_x, preferred_element_type=jnp.float32)  11.6 us
  transfers between devices with their start and end apart: 12, of which 12 were waited for; matrix products, arithmetic and copies ran while one was open for 1% of the time, Pallas kernels for 0%

commit v1 on v0

--- a/solution.py
+++ b/solution.py
@@ -1,15 +1,401 @@
+import functools
+
 import jax
 import jax.numpy as jnp
 from jax import lax
+from jax.experimental import pallas as pl
+from jax.experimental.pallas import tpu as pltpu
 from jax.sharding import PartitionSpec as P
 
 HEAD_DIM = 64
 STATE = 128
 GROUPS = 4
 BLOCK = 256
-
-
-HIGH = lax.Precision.HIGHEST
+MESH = pl.DeviceIdType.MESH
+F32 = jnp.float32
+BF16 = jnp.bfloat16
+
+D = 6144
+ROWS = 64
+SPAN = 1024
+COLS = 512
+SPLIT = 3584
+HALF_P = SPLIT // 2
+HALF_Q = 1280
+WIDE = D + 128
+
+
+def place():
+    tp = lax.axis_index("tp")
+    return lax.axis_index("seq"), tp // 4, tp // 2 % 2, tp % 2
+
+
+def greet(peers):
+    barrier = pltpu.get_barrier_semaphore()
+    for peer in peers:
+        pl.semaphore_signal(barrier, inc=1, device_id=peer, device_id_type=MESH)
+    pl.semaphore_wait(barrier, len(peers))
+
+
+def project_kernel(
+    tok, wx, wz, wbc, wdt, x_out, z_out, small_out, buf, w, w_small, st_bc, st_dt, sends, recvs, locs
+):
+    s, y, h, c = place()
+    up, down, far = (y + 1) % 4, (y + 3) % 4, (y + 2) % 4
+    dev = lambda yy, hh, cc: (s, yy * 4 + hh * 2 + cc)
+    dev_up, dev_down, dev_z, dev_sib = dev(up, h, c), dev(down, h, c), dev(y, 1 - h, c), dev(y, h, 1 - c)
+    part_p, part_q = (0, SPLIT), (SPLIT, D - SPLIT)
+    p_a, p_b = (0, HALF_P), (HALF_P, SPLIT - HALF_P)
+    q_a, q_b = (SPLIT, HALF_Q), (SPLIT + HALF_Q, D - SPLIT - HALF_Q)
+    whole = (0, D)
+
+    def at(yy, hh, cc, cols):
+        row = pl.multiple_of((yy * 4 + hh * 2 + cc) * ROWS, ROWS)
+        return buf.at[pl.ds(row, ROWS), pl.ds(cols[0], cols[1])]
+
+    started = []
+
+    def send(k, yy, hh, cols, to, own=False):
+        dst = at(yy, hh, c, cols)
+        src = tok.at[:, pl.ds(cols[0], cols[1])] if own else dst
+        copy = pltpu.make_async_remote_copy(
+            src_ref=src, dst_ref=dst, send_sem=sends.at[k], recv_sem=recvs.at[k],
+            device_id=to, device_id_type=MESH,
+        )
+        copy.start()
+        started.append(copy)
+
+    def arrive(k, yy, hh, cols, sib=False):
+        ref = at(yy, hh, 1 - c if sib else c, cols)
+        pltpu.make_async_remote_copy(
+            src_ref=ref, dst_ref=ref, send_sem=sends.at[k], recv_sem=recvs.at[k],
+            device_id=dev_sib, device_id_type=MESH,
+        ).wait_recv()
+
+    locals_ = [
+        pltpu.make_async_copy(tok, at(y, h, c, whole), locs.at[0]),
+        pltpu.make_async_copy(wbc, st_bc, locs.at[1]),
+        pltpu.make_async_copy(wdt, st_dt, locs.at[2]),
+        pltpu.make_async_copy(wx, w.at[:, pl.ds(0, COLS)], locs.at[3]),
+        pltpu.make_async_copy(wz, w.at[:, pl.ds(COLS, COLS)], locs.at[4]),
+    ]
+    for copy in locals_:
+        copy.start()
+    greet([dev_up, dev_down, dev_z, dev_sib])
+    send(0, y, h, part_p, dev_z, own=True)
+    send(1, y, h, part_q, dev_up, own=True)
+    send(2, y, h, part_q, dev_down, own=True)
+    send(3, y, h, whole, dev_sib, own=True)
+    send(4, y, h, part_q, dev_z, own=True)
+    send(5, y, h, part_p, dev_up, own=True)
+    send(6, y, h, part_p, dev_down, own=True)
+
+    def project(yy, hh):
+        row = pl.multiple_of((yy * 4 + hh * 2) * ROWS, 2 * ROWS)
+        rows = pl.ds(row, 2 * ROWS)
+        for out, base in ((x_out, 0), (z_out, COLS)):
+
+            @pl.loop(0, COLS // 256)
+            def _(j):
+                col = pl.multiple_of(j * 256, 256)
+                out[rows, pl.ds(col, 256)] = jnp.dot(
+                    buf[rows, :], w[:, pl.ds(base + col, 256)], preferred_element_type=F32
+                ).astype(BF16)
+
+        small_out[rows, :] = jnp.dot(buf[rows, :], w_small[...], preferred_element_type=F32)
+
+    locals_[1].wait()
+    locals_[2].wait()
+    w_small[...] = jnp.zeros_like(w_small)
+    w_small[:, 0:64] = st_bc[...]
+    w_small[:, 64:72] = st_dt[...]
+    locals_[0].wait()
+    locals_[3].wait()
+    locals_[4].wait()
+    arrive(3, y, h, whole, sib=True)
+    project(y, h)
+    arrive(1, down, h, part_q)
+    send(7, down, h, q_a, dev_up)
+    send(8, down, h, part_q, dev_z)
+    send(9, down, h, part_q, dev_sib)
+    arrive(2, up, h, part_q)
+    send(10, up, h, q_b, dev_down)
+    send(11, up, h, part_q, dev_z)
+    send(12, up, h, part_q, dev_sib)
+    arrive(0, y, 1 - h, part_p)
+    send(13, y, 1 - h, part_p, dev_up)
+    send(14, y, 1 - h, part_p, dev_down)
+    send(15, y, 1 - h, part_p, dev_sib)
+    arrive(7, far, h, q_a)
+    send(17, far, h, q_a, dev_z)
+    send(18, far, h, q_a, dev_sib)
+    arrive(10, far, h, q_b)
+    send(19, far, h, q_b, dev_z)
+    send(20, far, h, q_b, dev_sib)
+    arrive(4, y, 1 - h, part_q)
+    send(16, y, 1 - h, part_q, dev_sib)
+    arrive(5, down, h, part_p)
+    send(21, down, h, p_a, dev_up)
+    send(22, down, h, part_p, dev_sib)
+    arrive(6, up, h, part_p)
+    send(23, up, h, p_b, dev_down)
+    send(24, up, h, part_p, dev_sib)
+    arrive(15, y, 1 - h, part_p, sib=True)
+    arrive(16, y, 1 - h, part_q, sib=True)
+    project(y, 1 - h)
+    arrive(9, down, h, part_q, sib=True)
+    arrive(22, down, h, part_p, sib=True)
+    project(down, h)
+    arrive(13, down, 1 - h, part_p)
+    send(27, down, 1 - h, p_a, dev_up)
+    send(28, down, 1 - h, part_p, dev_sib)
+    arrive(14, up, 1 - h, part_p)
+    send(29, up, 1 - h, p_b, dev_down)
+    send(30, up, 1 - h, part_p, dev_sib)
+    arrive(12, up, h, part_q, sib=True)
+    arrive(24, up, h, part_p, sib=True)
+    project(up, h)
+    arrive(8, down, 1 - h, part_q)
+    send(25, down, 1 - h, part_q, dev_sib)
+    arrive(11, up, 1 - h, part_q)
+    send(26, up, 1 - h, part_q, dev_sib)
+    arrive(25, down, 1 - h, part_q, sib=True)
+    arrive(28, down, 1 - h, part_p, sib=True)
+    project(down, 1 - h)
+    arrive(21, far, h, p_a)
+    send(33, far, h, p_a, dev_sib)
+    arrive(23, far, h, p_b)
+    send(34, far, h, p_b, dev_sib)
+    arrive(26, up, 1 - h, part_q, sib=True)
+    arrive(30, up, 1 - h, part_p, sib=True)
+    project(up, 1 - h)
+    arrive(17, far, 1 - h, q_a)
+    send(31, far, 1 - h, q_a, dev_sib)
+    arrive(19, far, 1 - h, q_b)
+    send(32, far, 1 - h, q_b, dev_sib)
+    arrive(18, far, h, q_a, sib=True)
+    arrive(20, far, h, q_b, sib=True)
+    arrive(33, far, h, p_a, sib=True)
+    arrive(34, far, h, p_b, sib=True)
+    project(far, h)
+    arrive(27, far, 1 - h, p_a)
+    send(35, far, 1 - h, p_a, dev_sib)
+    arrive(29, far, 1 - h, p_b)
+    send(36, far, 1 - h, p_b, dev_sib)
+    arrive(31, far, 1 - h, q_a, sib=True)
+    arrive(32, far, 1 - h, q_b, sib=True)
+    arrive(35, far, 1 - h, p_a, sib=True)
+    arrive(36, far, 1 - h, p_b, sib=True)
+    project(far, 1 - h)
+    for copy in started:
+        copy.wait_send()
+
+
+def gather_project(tokens, w_x, w_z, w_bc, w_dt):
+    anywhere = pl.BlockSpec(memory_space=pl.ANY)
+    vmem = pl.BlockSpec(memory_space=pltpu.VMEM)
+    return pl.pallas_call(
+        project_kernel,
+        out_shape=(
+            jax.ShapeDtypeStruct((SPAN, COLS), BF16),
+            jax.ShapeDtypeStruct((SPAN, COLS), BF16),
+            jax.ShapeDtypeStruct((SPAN, 128), F32),
+        ),
+        in_specs=[anywhere] * 5,
+        out_specs=(vmem, vmem, vmem),
+        scratch_shapes=[
+            pltpu.VMEM((SPAN, D), BF16),
+            pltpu.VMEM((D, 2 * COLS), BF16),
+            pltpu.VMEM((D, 128), BF16),
+            pltpu.VMEM((D, 64), BF16),
+            pltpu.VMEM((D, 8), BF16),
+            pltpu.SemaphoreType.DMA((37,)),
+            pltpu.SemaphoreType.DMA((37,)),
+            pltpu.SemaphoreType.DMA((5,)),
+        ],
+        compiler_params=pltpu.CompilerParams(
+            collective_id=1, has_side_effects=True, vmem_limit_bytes=56 << 20
+        ),
+        name="gather_project",
+    )(tokens, w_x, w_z, w_bc, w_dt)
+
+
+def reduce_kernel(
+    g, sq, w_out, out, o, sib, zq, pa, pb, qa, qb, pf, qf, zp, sends, recvs
+):
+    s, y, h, c = place()
+    up, down, far = (y + 1) % 4, (y + 3) % 4, (y + 2) % 4
+    dev = lambda yy, hh, cc: (s, yy * 4 + hh * 2 + cc)
+    dev_up, dev_down, dev_z, dev_sib = dev(up, h, c), dev(down, h, c), dev(y, 1 - h, c), dev(y, h, 1 - c)
+    wide_q = WIDE - SPLIT
+    part_p, part_q = (0, SPLIT), (SPLIT, wide_q)
+    p_a, p_b = (0, HALF_P), (HALF_P, SPLIT - HALF_P)
+    q_a, q_b = (SPLIT, HALF_Q), (SPLIT + HALF_Q, wide_q - HALF_Q)
+    started = []
+
+    def at(yy, hh, cc, cols):
+        row = pl.multiple_of((yy * 4 + hh * 2 + cc) * ROWS, ROWS)
+        return o.at[pl.ds(row, ROWS), pl.ds(cols[0], cols[1])]
+
+    def copy_of(k, src, dst, to):
+        return pltpu.make_async_remote_copy(
+            src_ref=src, dst_ref=dst, send_sem=sends.at[k], recv_sem=recvs.at[k],
+            device_id=to, device_id_type=MESH,
+        )
+
+    def send(k, src, dst, to):
+        copy = copy_of(k, src, dst, to)
+        copy.start()
+        started.append(copy)
+
+    def arrive(k, ref):
+        copy_of(k, ref, ref, dev_sib).wait_recv()
+
+    def add(yy, hh, cols, ref):
+        target = at(yy, hh, c, cols)
+
+        @pl.loop(0, ROWS // 16)
+        def _(i):
+            rows = pl.ds(pl.multiple_of(i * 16, 16), 16)
+            target[rows, :] = (target[rows, :].astype(F32) + ref[rows, :].astype(F32)).astype(BF16)
+
+    def chip(yy, hh):
+        return yy * 2 + hh
+
+    def partial(yy, hh, k):
+        row = pl.multiple_of((yy * 4 + hh * 2) * ROWS, 2 * ROWS)
+        rows = pl.ds(row, 2 * ROWS)
+        left = g[rows, :]
+
+        @pl.loop(0, D // 512)
+        def _(j):
+            cols = pl.ds(pl.multiple_of(j * 512, 512), 512)
+            o[rows, cols] = jnp.dot(left, w_out[:, cols], preferred_element_type=F32).astype(BF16)
+
+        o[rows, pl.ds(D, 128)] = sq[rows, :]
+        send(k, at(yy, hh, 1 - c, (0, WIDE)), sib.at[chip(yy, hh)], dev_sib)
+
+    def joined(yy, hh, k):
+        ref = sib.at[chip(yy, hh)]
+        arrive(k, ref)
+        add(yy, hh, (0, WIDE), ref)
+
+    greet([dev_up, dev_down, dev_z, dev_sib])
+    n = 1 - h
+    partial(far, n, 0)
+    partial(far, h, 1)
+    joined(far, n, 0)
+    send(8, at(far, n, c, p_a), pa.at[n], dev_up)
+    send(9, at(far, n, c, p_b), pb.at[n], dev_down)
+    send(10, at(far, n, c, part_q), zq.at[far], dev_z)
+    partial(up, n, 2)
+    joined(far, h, 1)
+    send(11, at(far, h, c, p_a), pa.at[h], dev_up)
+    send(12, at(far, h, c, p_b), pb.at[h], dev_down)
+    partial(down, n, 3)
+    joined(up, n, 2)
+    send(13, at(up, n, c, part_q), zq.at[up], dev_z)
+    partial(up, h, 4)
+    joined(down, n, 3)
+    send(14, at(down, n, c, part_q), zq.at[down], dev_z)
+    arrive(8, pa.at[n])
+    add(up, n, p_a, pa.at[n])
+    send(15, at(up, n, c, part_p), pf.at[0, n], dev_up)
+    arrive(9, pb.at[n])
+    add(down, n, p_b, pb.at[n])
+    send(16, at(down, n, c, part_p), pf.at[1, n], dev_down)
+    partial(down, h, 5)
+    joined(up, h, 4)
+    arrive(11, pa.at[h])
+    add(up, h, p_a, pa.at[h])
+    send(17, at(up, h, c, part_p), pf.at[0, h], dev_up)
+    partial(y, n, 6)
+    joined(down, h, 5)
+    arrive(12, pb.at[h])
+    add(down, h, p_b, pb.at[h])
+    send(18, at(down, h, c, part_p), pf.at[1, h], dev_down)
+    joined(y, n, 6)
+    send(19, at(y, n, c, part_q), zq.at[y], dev_z)
+    partial(y, h, 7)
+    arrive(10, zq.at[far])
+    add(far, h, part_q, zq.at[far])
+    send(20, at(far, h, c, q_a), qa, dev_up)
+    send(21, at(far, h, c, q_b), qb, dev_down)
+    joined(y, h, 7)
+    arrive(13, zq.at[up])
+    add(up, h, part_q, zq.at[up])
+    arrive(20, qa)
+    add(up, h, q_a, qa)
+    send(22, at(up, h, c, part_q), qf.at[0], dev_up)
+    arrive(14, zq.at[down])
+    add(down, h, part_q, zq.at[down])
+    arrive(21, qb)
+    add(down, h, q_b, qb)
+    send(23, at(down, h, c, part_q), qf.at[1], dev_down)
+    arrive(15, pf.at[0, n])
+    add(y, n, part_p, pf.at[0, n])
+    arrive(16, pf.at[1, n])
+    add(y, n, part_p, pf.at[1, n])
+    send(24, at(y, n, c, part_p), zp, dev_z)
+    arrive(17, pf.at[0, h])
+    add(y, h, part_p, pf.at[0, h])
+    arrive(18, pf.at[1, h])
+    add(y, h, part_p, pf.at[1, h])
+    arrive(19, zq.at[y])
+    arrive(22, qf.at[0])
+    arrive(23, qf.at[1])
+    mine_q = at(y, h, c, part_q)
+    mine_p = at(y, h, c, part_p)
+    terms = (mine_q, zq.at[y], qf.at[0], qf.at[1])
+    lane = pl.ds(D - SPLIT, 128)
+    squares = sum(t[:, lane].astype(F32) for t in terms)
+    scale = lax.rsqrt(squares / (COLS * 16) + 1e-05)
+
+    @pl.loop(0, (D - SPLIT) // 128)
+    def _(j):
+        cols = pl.ds(pl.multiple_of(j * 128, 128), 128)
+        total = sum(t[:, cols].astype(F32) for t in terms)
+        out[:, pl.ds(pl.multiple_of(SPLIT + j * 128, 128), 128)] = (total * scale).astype(BF16)
+
+    arrive(24, zp)
+
+    @pl.loop(0, SPLIT // 128)
+    def _(j):
+        cols = pl.ds(pl.multiple_of(j * 128, 128), 128)
+        total = mine_p[:, cols].astype(F32) + zp[:, cols].astype(F32)
+        out[:, cols] = (total * scale).astype(BF16)
+
+    for copy in started:
+        copy.wait_send()
+
+
+def project_reduce(g, sq, w_out):
+    vmem = pl.BlockSpec(memory_space=pltpu.VMEM)
+    wide_q = WIDE - SPLIT
+    return pl.pallas_call(
+        reduce_kernel,
+        out_shape=jax.ShapeDtypeStruct((ROWS, D), BF16),
+        in_specs=[vmem] * 3,
+        out_specs=vmem,
+        scratch_shapes=[
+            pltpu.VMEM((SPAN, WIDE), BF16),
+            pltpu.VMEM((8, ROWS, WIDE), BF16),
+            pltpu.VMEM((4, ROWS, wide_q), BF16),
+            pltpu.VMEM((2, ROWS, HALF_P), BF16),
+            pltpu.VMEM((2, ROWS, SPLIT - HALF_P), BF16),
+            pltpu.VMEM((ROWS, HALF_Q), BF16),
+            pltpu.VMEM((ROWS, wide_q - HALF_Q), BF16),
+            pltpu.VMEM((2, 2, ROWS, SPLIT), BF16),
+            pltpu.VMEM((2, ROWS, wide_q), BF16),
+            pltpu.VMEM((ROWS, SPLIT), BF16),
+            pltpu.SemaphoreType.DMA((25,)),
+            pltpu.SemaphoreType.DMA((25,)),
+        ],
+        compiler_params=pltpu.CompilerParams(
+            collective_id=2, has_side_effects=True, vmem_limit_bytes=56 << 20
+        ),
+        name="project_reduce",
+    )(g, sq, w_out)
 
 
 def from_behind(value, axis, steps):
@@ -35,21 +421,10 @@
     col_bc = w_bc.shape[1]
     heads_dev = w_dt.shape[1]
     taps = conv_x.shape[0]
-    piece = lax.all_gather(tokens, "tp", axis=0, tiled=True)
-    projected = jnp.concatenate(
-        [
-            jnp.dot(piece, w_x, preferred_element_type=jnp.float32),
-            jnp.dot(piece, w_z, preferred_element_type=jnp.float32),
-            jnp.dot(piece, w_bc, preferred_element_type=jnp.float32),
-            jnp.dot(piece, w_dt, preferred_element_type=jnp.float32),
-        ],
-        axis=1,
-    )
-    span_len = projected.shape[0]
-    x_in = projected[:, :col_x].astype(jnp.bfloat16)
-    z_gate = projected[:, col_x : 2 * col_x].astype(jnp.bfloat16)
-    bc_in = projected[:, 2 * col_x : 2 * col_x + col_bc].astype(jnp.bfloat16)
-    dt_raw = projected[:, 2 * col_x + col_bc :]
+    x_in, z_gate, small = gather_project(tokens, w_x, w_z, w_bc, w_dt)
+    span_len = x_in.shape[0]
+    bc_in = small[:, :col_bc].astype(jnp.bfloat16)
+    dt_raw = small[:, col_bc : col_bc + heads_dev]
     conv_input = jnp.concatenate([x_in, bc_in], axis=1)
     rim_rows = from_behind(conv_input[span_len - (taps - 1) :], "seq", 1)
     padded = jnp.concatenate([rim_rows, conv_input], axis=0)
@@ -82,13 +457,13 @@
     dt_heads = jnp.transpose(dt.reshape(nblocks, BLOCK, heads_dev), (0, 2, 1))
     accum = jnp.cumsum(dt_heads * decay_rate[None, :, None], axis=2)
     causal = (jnp.arange(BLOCK)[:, None] >= jnp.arange(BLOCK)[None, :])[None, None, :, :]
-    affinity = jnp.einsum("btn,bsn->bts", c_blocks, b_blocks, precision=HIGH)
+    affinity = jnp.einsum("btn,bsn->bts", c_blocks, b_blocks, precision=lax.Precision.DEFAULT)
     expo = accum[:, :, :, None] - accum[:, :, None, :]
     decay = jnp.where(causal, jnp.exp(-jnp.where(causal, expo, 0.0)), 0.0)
     weights = affinity[:, None, :, :] * decay * dt_heads[:, :, None, :]
-    y_intra = jnp.einsum("bhts,bshp->bthp", weights, x_blocks, precision=HIGH)
+    y_intra = jnp.einsum("bhts,bshp->bthp", weights, x_blocks, precision=lax.Precision.DEFAULT)
     tail = jnp.exp(-(accum[:, :, -1:] - accum)) * dt_heads
-    contrib = jnp.einsum("bshp,bhs,bsn->bhpn", x_blocks, tail, b_blocks, precision=HIGH)
+    contrib = jnp.einsum("bshp,bhs,bsn->bhpn", x_blocks, tail, b_blocks, precision=lax.Precision.DEFAULT)
     block_decay = jnp.exp(-accum[:, :, -1])
     local_state = jnp.zeros((heads_dev, HEAD_DIM, STATE), jnp.float32)
     prefix_decay = jnp.ones((heads_dev,), jnp.float32)
@@ -116,22 +491,15 @@
     )
     entry_scale = jnp.transpose(jnp.exp(-accum), (0, 2, 1))
     y_inter = entry_scale[..., None] * jnp.einsum(
-        "btn,bhpn->bthp", c_blocks, entry_states, precision=HIGH
+        "btn,bhpn->bthp", c_blocks, entry_states, precision=lax.Precision.DEFAULT
     )
     y_all = y_intra + y_inter + skip[None, None, :, None] * x_blocks
     y_flat = y_all.reshape(span_len, col_x)
     gated = y_flat * jax.nn.silu(z_gate.astype(jnp.float32))
-    squares_sum = lax.psum(jnp.sum(gated * gated, axis=1), "tp")
-    mean_sq = squares_sum / (col_x * lax.axis_size("tp")) + 1e-05
-    normed = (gated * lax.rsqrt(mean_sq)[:, None] * norm_gain.astype(jnp.float32)[None, :]).astype(
-        jnp.bfloat16
-    )
-    return lax.psum_scatter(
-        jnp.dot(normed, w_out, preferred_element_type=jnp.float32).astype(jnp.bfloat16),
-        "tp",
-        scatter_dimension=0,
-        tiled=True,
-    )
+    squares = jnp.sum(gated * gated, axis=1, keepdims=True)
+    scaled = (gated * norm_gain.astype(jnp.float32)[None, :]).astype(jnp.bfloat16)
+    spread = jnp.broadcast_to(squares, (span_len, 128)).astype(jnp.bfloat16)
+    return project_reduce(scaled, spread, w_out)
 
 
 def solution(mesh):

time: 419 us -> 231 us (0.55)
  the two profiles are of different devices: /device:TPU:1 before, /device:TPU:32 now
where the time goes in v1:
time: 231 us; the launch traced here: 230 us
  Pallas kernels  119 us (52%)
  waiting for transfers between devices  56.3 us (24%)
  starting transfers between devices  19 us (8%)
  local copies, waits for them, and re-layouts  18.6 us (8%)
  other arithmetic  12.1 us (5%)
  matrix products  5.01 us (2%)
    pallas_call x1, Pallas kernels, gather_project(): pl.pallas_call(project_kernel, out_shape=(jax.ShapeDtypeStruct((SPAN, COL...  59.5 us
    pallas_call x1, Pallas kernels, project_reduce(): pl.pallas_call(reduce_kernel, out_shape=jax.ShapeDtypeStruct((ROWS, D), B...  59 us
    ppermute x8, waiting for transfers between devices, from_behind(): lax.ppermute(value, axis, [(source, source + steps) for source in range(f...  49 us
    ppermute x8, starting transfers between devices, from_behind(): lax.ppermute(value, axis, [(source, source + steps) for source in range(f...  18.2 us
    ppermute x2, waiting for transfers between devices, from_partner(): return lax.ppermute(block, axis, route)  7.28 us
    unnamed x37, local copies, waits for them, and re-layouts  6.68 us
    reshape x2, local copies, waits for them, and re-layouts, on_device(): y_flat = y_all.reshape(span_len, col_x)  6.26 us
  transfers between devices with their start and end apart: 10, of which 10 were waited for; matrix products, arithmetic and copies ran while one was open for 3% of the time, Pallas kernels for 0%

profile of v1, /device:TPU:32, one launch (start us, length us, event | category | flops | bytes accessed | tf_op | source)
XLA Modules:
  0.0 230.1 jit_solution(5100073175909110269)
XLA Ops:
  0.0 2.5 %copy.47.wbc = bf16[6144,64]{1,0:T(8,128)(2,1)} copy(bf16[6144,64]{0,1:T(8,128)(2,1)} %param.17) | data formatting | bytes 1572864 | tf_op args[3]
  4.0 59.5 %gather_project.1 = (bf16[1024,512]{1,0:T(8,128)(2,1)}, bf16[1024,512]{1,0:T(8,128)(2,1)}, f32[1024,128]{1,0:T(8,128)}) custom-call(bf16[64,6144]{1,0:T(8,128)(2,1)} %tok.1, bf16[6144,512]{1,0:T(8,128)(2,1)} %wx.1, bf16[6144,512]{1,0:T(8,128)(2,1)} %wz.1, bf16[6144,64]{1,0:T(8,128)(2,1)} %copy.47.wbc, bf16[6144,8]{1,0:T(8,128)(2,1)} %copy.48.wdt), custom_call_target="tpu_custom_call" | custom-call | tf_op jit(solution)/shard_map/gather_project/pallas_call | solution.py:197
  65.4 3.4 %collective-permute-start.1 = (bf16[3,576]{1,0:T(4,128)(2,1)S(1)}, bf16[3,576]{1,0:T(4,128)(2,1)S(1)}, u32[]{:S(2)}, u32[]{:S(2)}) collective-permute-start(bf16[3,576]{1,0:T(4,128)(2,1)S(1)} %fusion.39), channel_id=1, source_target_pairs={{0,16},{16,32},{32,48},{48,64},{64,80},{80,96},{96,112},{1,17},{17... | collective-permute-start | bytes 10376 | tf_op jit(solution)/shard_map/ppermute | solution.py:404
  69.4 2.3 reduce-window.6
  81.5 6.4 %collective-permute-done.3 = bf16[1024,128]{1,0:T(8,128)(2,1)} collective-permute-done((bf16[1024,128]{1,0:T(8,128)(2,1)}, bf16[1024,128]{1,0:T(8,128)(2,1)}, u32[]{:S(2)}, u32[]{:S(2)}) %collective-permute-start.3) | collective-permute-done | bytes 262176 | tf_op jit(solution)/shard_map/ppermute | solution.py:414
  91.2 64.7 %while.11 = (s32[]{:T(128)}, f32[8,64,128]{2,1,0:T(8,128)S(1)}, f32[8]{0:T(128)S(1)}, f32[8,64,128]{2,1,0:T(8,128)S(1)}, s32[]{:T(128)}, /*index=5*/s32[]{:T(128)}) while((s32[]{:T(128)}, f32[8,64,128]{2,1,0:T(8,128)S(1)}, f32[8]{0:T(128)S(1)}, f32[8,64,128]{2,1,0:T(8,128)S(1)}, s32[]{:T(128)}, /*index=5*/s32[]{:T(128)}) %tuple.37), condition=%wide.region_3.4_spmd.clone, body=%wide.region_2.3_spmd.clone.sunk | while | flops 327683 | bytes 1573015 | solution.py:484
  91.3 3.3 %collective-permute-start = (bf16[8,64,128]{2,1,0:T(8,128)(2,1)S(1)}, bf16[8,64,128]{2,1,0:T(8,128)(2,1)S(1)}, u32[]{:S(2)}, u32[]{:S(2)}) collective-permute-start(bf16[8,64,128]{2,1,0:T(8,128)(2,1)S(1)} %fusion.58), channel_id=1, source_target_pairs={{0,16},{16,32},{32,48},{48,64},{64,80},{80,96},{96,112},{1,17},{17... | collective-permute-start | bytes 393224 | tf_op jit(solution)/shard_map/while/body/eval_jaxpr/ppermute | solution.py:404
  94.6 5.7 %collective-permute-done = bf16[8,64,128]{2,1,0:T(8,128)(2,1)S(1)} collective-permute-done((bf16[8,64,128]{2,1,0:T(8,128)(2,1)S(1)}, bf16[8,64,128]{2,1,0:T(8,128)(2,1)S(1)}, u32[]{:S(2)}, u32[]{:S(2)}) %collective-permute-start) | collective-permute-done | bytes 131104 | tf_op jit(solution)/shard_map/while/body/eval_jaxpr/ppermute | solution.py:404
  100.4 1.9 collective-permute-start
  102.4 7.0 %collective-permute-done = bf16[8,64,128]{2,1,0:T(8,128)(2,1)S(1)} collective-permute-done((bf16[8,64,128]{2,1,0:T(8,128)(2,1)S(1)}, bf16[8,64,128]{2,1,0:T(8,128)(2,1)S(1)}, u32[]{:S(2)}, u32[]{:S(2)}) %collective-permute-start) | collective-permute-done | bytes 131104 | tf_op jit(solution)/shard_map/while/body/eval_jaxpr/ppermute | solution.py:404
  109.5 1.9 collective-permute-start
  111.5 7.0 %collective-permute-done = bf16[8,64,128]{2,1,0:T(8,128)(2,1)S(1)} collective-permute-done((bf16[8,64,128]{2,1,0:T(8,128)(2,1)S(1)}, bf16[8,64,128]{2,1,0:T(8,128)(2,1)S(1)}, u32[]{:S(2)}, u32[]{:S(2)}) %collective-permute-start) | collective-permute-done | bytes 131104 | tf_op jit(solution)/shard_map/while/body/eval_jaxpr/ppermute | solution.py:404
  118.7 1.9 collective-permute-start
  120.6 7.0 %collective-permute-done = bf16[8,64,128]{2,1,0:T(8,128)(2,1)S(1)} collective-permute-done((bf16[8,64,128]{2,1,0:T(8,128)(2,1)S(1)}, bf16[8,64,128]{2,1,0:T(8,128)(2,1)S(1)}, u32[]{:S(2)}, u32[]{:S(2)}) %collective-permute-start) | collective-permute-done | bytes 131104 | tf_op jit(solution)/shard_map/while/body/eval_jaxpr/ppermute | solution.py:404
  127.8 1.9 collective-permute-start
  129.7 7.0 %collective-permute-done = bf16[8,64,128]{2,1,0:T(8,128)(2,1)S(1)} collective-permute-done((bf16[8,64,128]{2,1,0:T(8,128)(2,1)S(1)}, bf16[8,64,128]{2,1,0:T(8,128)(2,1)S(1)}, u32[]{:S(2)}, u32[]{:S(2)}) %collective-permute-start) | collective-permute-done | bytes 131104 | tf_op jit(solution)/shard_map/while/body/eval_jaxpr/ppermute | solution.py:404
  136.9 1.9 collective-permute-start
  138.8 7.9 %collective-permute-done = bf16[8,64,128]{2,1,0:T(8,128)(2,1)S(1)} collective-permute-done((bf16[8,64,128]{2,1,0:T(8,128)(2,1)S(1)}, bf16[8,64,128]{2,1,0:T(8,128)(2,1)S(1)}, u32[]{:S(2)}, u32[]{:S(2)}) %collective-permute-start) | collective-permute-done | bytes 131104 | tf_op jit(solution)/shard_map/while/body/eval_jaxpr/ppermute | solution.py:404
  148.8 7.0 %collective-permute-done = bf16[8,64,128]{2,1,0:T(8,128)(2,1)S(1)} collective-permute-done((bf16[8,64,128]{2,1,0:T(8,128)(2,1)S(1)}, bf16[8,64,128]{2,1,0:T(8,128)(2,1)S(1)}, u32[]{:S(2)}, u32[]{:S(2)}) %collective-permute-start) | collective-permute-done | bytes 131104 | tf_op jit(solution)/shard_map/while/body/eval_jaxpr/ppermute | solution.py:404
  157.2 2.9 %fusion.23 = f32[4,256,8,64]{1,3,2,0:T(8,128)S(1)} fusion(bf16[4,256,8,64]{1,3,2,0:T(8,128)(2,1)S(1)} %copy.54, f32[4,256,8,64]{1,3,2,0:T(8,128)S(1)} %fusion.26, f32[4,8,256]{2,1,0:T(8,128)S(1)} %bitcast.100, f32[4,8,256]{2,1,0:T(8,128)S(1)} %get-tuple-element.62, f32[4,256,256]{2,1,0:T(8,128)S(1)} %copy-done.3, pred[256,256]{1,0:T(8,128)(4,1)S(1)} %copy-done.5, ...), kind=kOutput, calls=%fused_computation.28 | convolution fusion | flops 283639808 | bytes 6455328 | tf_op jit(solution)/shard_map/bhts,bshp->bthp/dot_general | solution.py:464
  160.0 2.7 %copy.60 = f32[4,256,8,64]{3,2,1,0:T(8,128)} copy(f32[4,256,8,64]{1,3,2,0:T(8,128)S(1)} %fusion.23) | data formatting | bytes 4194304 | tf_op jit(solution)/shard_map/reshape | solution.py:497
  162.8 3.5 %reshape.107 = f32[1024,512]{1,0:T(8,128)S(1)} reshape(f32[4,256,8,64]{3,2,1,0:T(8,128)} %copy.60) | data formatting | bytes 4194304 | tf_op jit(solution)/shard_map/reshape | solution.py:497
  169.0 59.0 %project_reduce.1 = bf16[64,6144]{1,0:T(8,128)(2,1)} custom-call(bf16[1024,512]{1,0:T(8,128)(2,1)} %get-tuple-element.69.g, bf16[1024,128]{1,0:T(8,128)(2,1)} %broadcast_in_dim.23.sq, bf16[512,6144]{1,0:T(8,128)(2,1)} %w_out.1), custom_call_target="tpu_custom_call" | custom-call | tf_op jit(solution)/shard_map/project_reduce/pallas_call | solution.py:375
  228.1 2.1 copy.71
  (91 shorter events, 23.6 us)
Async XLA Ops:
  0.0 2.5 %copy-start.4 = (bf16[6144,8]{0,1:T(8,128)(2,1)S(1)}, bf16[6144,8]{0,1:T(8,128)(2,1)}, u32[]{:S(2)}) copy-start(bf16[6144,8]{0,1:T(8,128)(2,1)} %param.18) | copy-start | bytes 294916
  4.0 64.8 %copy-start.14 = (f32[8]{0:T(128)S(1)}, f32[8]{0:T(128)}, u32[]{:S(2)}) copy-start(f32[8]{0:T(128)} %param.21) | copy-start | bytes 100
  63.5 5.3 %copy-start.1 = (f32[1024,128]{1,0:T(8,128)S(1)}, f32[1024,128]{1,0:T(8,128)}, u32[]{:S(2)}) copy-start(f32[1024,128]{1,0:T(8,128)} %get-tuple-element.31) | copy-start | bytes 1572868
  63.5 5.9 %copy-start.15 = (f32[8]{0:T(128)S(1)}, f32[8]{0:T(128)}, u32[]{:S(2)}) copy-start(f32[8]{0:T(128)} %param.22) | copy-start | bytes 100
  63.5 9.3 %copy-start.6 = (bf16[4,512]{1,0:T(4,128)(2,1)S(1)}, bf16[4,512]{1,0:T(4,128)(2,1)}, u32[]{:S(2)}) copy-start(bf16[4,512]{1,0:T(4,128)(2,1)} %param.19) | copy-start | bytes 12292
  63.5 9.3 %copy-start.13 = (bf16[4,64]{1,0:T(4,128)(2,1)S(1)}, bf16[4,64]{1,0:T(4,128)(2,1)}, u32[]{:S(2)}) copy-start(bf16[4,64]{1,0:T(4,128)(2,1)} %param.20) | copy-start | bytes 1540
  63.5 9.5 %copy-start = (bf16[1024,512]{1,0:T(8,128)(2,1)S(1)}, bf16[1024,512]{1,0:T(8,128)(2,1)}, u32[]{:S(2)}) copy-start(bf16[1024,512]{1,0:T(8,128)(2,1)} %get-tuple-element.30) | copy-start | bytes 3145732
  65.4 7.6 %collective-permute-start.1 = (bf16[3,576]{1,0:T(4,128)(2,1)S(1)}, bf16[3,576]{1,0:T(4,128)(2,1)S(1)}, u32[]{:S(2)}, u32[]{:S(2)}) collective-permute-start(bf16[3,576]{1,0:T(4,128)(2,1)S(1)} %fusion.39), channel_id=1, source_target_pairs={{0,16},{16,32},{32,48},{48,64},{64,80},{80,96},{96,112},{1,17},{17... | collective-permute-start | bytes 10376 | tf_op jit(solution)/shard_map/ppermute | solution.py:404
  73.4 5.7 %copy-start.12 = (bf16[512]{0:T(512)(128)(2,1)S(1)}, bf16[512]{0:T(512)(128)(2,1)}, u32[]{:S(2)}) copy-start(bf16[512]{0:T(512)(128)(2,1)} %param.24) | copy-start | bytes 3076
  75.1 1.6 collective-permute-start.2
  77.7 10.2 %collective-permute-start.3 = (bf16[1024,128]{1,0:T(8,128)(2,1)}, bf16[1024,128]{1,0:T(8,128)(2,1)}, u32[]{:S(2)}, u32[]{:S(2)}) collective-permute-start(bf16[1024,128]{1,0:T(8,128)(2,1)} %maximum_select_fusion.1), channel_id=1, source_target_pairs={{0,2},{2,0},{1,3},{3,1},{4,6},{6,4},{5,7},{7,5},{8,10},{10,8},{9,1... | collective-permute-start | bytes 786440 | tf_op jit(solution)/shard_map/ppermute | solution.py:414
  89.3 1.7 copy-start.10
  89.3 1.7 copy-start.11
  91.2 64.8 %copy-start.7 = (f32[8]{0:T(128)S(1)}, f32[8]{0:T(128)}, u32[]{:S(2)}) copy-start(f32[8]{0:T(128)} %get-tuple-element.75) | copy-start | bytes 100
  91.2 64.8 %copy-start.8 = (f32[8]{0:T(128)S(1)}, f32[8]{0:T(128)}, u32[]{:S(2)}) copy-start(f32[8]{0:T(128)} %get-tuple-element.66) | copy-start | bytes 100
  91.2 64.8 %copy-start.9 = (f32[8]{0:T(128)S(1)}, f32[8]{0:T(128)}, u32[]{:S(2)}) copy-start(f32[8]{0:T(128)} %get-tuple-element.67) | copy-start | bytes 100
  91.3 9.0 %collective-permute-start = (bf16[8,64,128]{2,1,0:T(8,128)(2,1)S(1)}, bf16[8,64,128]{2,1,0:T(8,128)(2,1)S(1)}, u32[]{:S(2)}, u32[]{:S(2)}) collective-permute-start(bf16[8,64,128]{2,1,0:T(8,128)(2,1)S(1)} %fusion.58), channel_id=1, source_target_pairs={{0,16},{16,32},{32,48},{48,64},{64,80},{80,96},{96,112},{1,17},{17... | collective-permute-start | bytes 393224 | tf_op jit(solution)/shard_map/while/body/eval_jaxpr/ppermute | solution.py:404
  100.4 9.0 %collective-permute-start = (bf16[8,64,128]{2,1,0:T(8,128)(2,1)S(1)}, bf16[8,64,128]{2,1,0:T(8,128)(2,1)S(1)}, u32[]{:S(2)}, u32[]{:S(2)}) collective-permute-start(bf16[8,64,128]{2,1,0:T(8,128)(2,1)S(1)} %fusion.58), channel_id=1, source_target_pairs={{0,16},{16,32},{32,48},{48,64},{64,80},{80,96},{96,112},{1,17},{17... | collective-permute-start | bytes 393224 | tf_op jit(solution)/shard_map/while/body/eval_jaxpr/ppermute | solution.py:404
  109.5 9.0 %collective-permute-start = (bf16[8,64,128]{2,1,0:T(8,128)(2,1)S(1)}, bf16[8,64,128]{2,1,0:T(8,128)(2,1)S(1)}, u32[]{:S(2)}, u32[]{:S(2)}) collective-permute-start(bf16[8,64,128]{2,1,0:T(8,128)(2,1)S(1)} %fusion.58), channel_id=1, source_target_pairs={{0,16},{16,32},{32,48},{48,64},{64,80},{80,96},{96,112},{1,17},{17... | collective-permute-start | bytes 393224 | tf_op jit(solution)/shard_map/while/body/eval_jaxpr/ppermute | solution.py:404
  118.7 9.0 %collective-permute-start = (bf16[8,64,128]{2,1,0:T(8,128)(2,1)S(1)}, bf16[8,64,128]{2,1,0:T(8,128)(2,1)S(1)}, u32[]{:S(2)}, u32[]{:S(2)}) collective-permute-start(bf16[8,64,128]{2,1,0:T(8,128)(2,1)S(1)} %fusion.58), channel_id=1, source_target_pairs={{0,16},{16,32},{32,48},{48,64},{64,80},{80,96},{96,112},{1,17},{17... | collective-permute-start | bytes 393224 | tf_op jit(solution)/shard_map/while/body/eval_jaxpr/ppermute | solution.py:404
  127.8 9.0 %collective-permute-start = (bf16[8,64,128]{2,1,0:T(8,128)(2,1)S(1)}, bf16[8,64,128]{2,1,0:T(8,128)(2,1)S(1)}, u32[]{:S(2)}, u32[]{:S(2)}) collective-permute-start(bf16[8,64,128]{2,1,0:T(8,128)(2,1)S(1)} %fusion.58), channel_id=1, source_target_pairs={{0,16},{16,32},{32,48},{48,64},{64,80},{80,96},{96,112},{1,17},{17... | collective-permute-start | bytes 393224 | tf_op jit(solution)/shard_map/while/body/eval_jaxpr/ppermute | solution.py:404
  136.9 9.9 %collective-permute-start = (bf16[8,64,128]{2,1,0:T(8,128)(2,1)S(1)}, bf16[8,64,128]{2,1,0:T(8,128)(2,1)S(1)}, u32[]{:S(2)}, u32[]{:S(2)}) collective-permute-start(bf16[8,64,128]{2,1,0:T(8,128)(2,1)S(1)} %fusion.58), channel_id=1, source_target_pairs={{0,16},{16,32},{32,48},{48,64},{64,80},{80,96},{96,112},{1,17},{17... | collective-permute-start | bytes 393224 | tf_op jit(solution)/shard_map/while/body/eval_jaxpr/ppermute | solution.py:404
  146.9 9.0 %collective-permute-start = (bf16[8,64,128]{2,1,0:T(8,128)(2,1)S(1)}, bf16[8,64,128]{2,1,0:T(8,128)(2,1)S(1)}, u32[]{:S(2)}, u32[]{:S(2)}) collective-permute-start(bf16[8,64,128]{2,1,0:T(8,128)(2,1)S(1)} %fusion.58), channel_id=1, source_target_pairs={{0,16},{16,32},{32,48},{48,64},{64,80},{80,96},{96,112},{1,17},{17... | collective-permute-start | bytes 393224 | tf_op jit(solution)/shard_map/while/body/eval_jaxpr/ppermute | solution.py:404
  162.8 3.5 %copy-start.2 = (bf16[1024,512]{1,0:T(8,128)(2,1)S(1)}, bf16[1024,512]{1,0:T(8,128)(2,1)}, u32[]{:S(2)}) copy-start(bf16[1024,512]{1,0:T(8,128)(2,1)} %get-tuple-element.33) | copy-start | bytes 3145732
  (3 other events, 3.7 us)

commit v2 on v1

v2 whole, which is shorter than its diff:
```python
import jax
import jax.numpy as jnp
from jax import lax
from jax.experimental import pallas as pl
from jax.experimental.pallas import tpu as pltpu
from jax.sharding import PartitionSpec as P

HEAD_DIM = 64
STATE = 128
BLOCK = 256
MESH = pl.DeviceIdType.MESH
F32 = jnp.float32
BF16 = jnp.bfloat16

D = 6144
ROWS = 64
SPAN = 1024
COLS = 512
SPLIT = 3584
HALF_P = SPLIT // 2
HALF_Q = 1280
WIDE = D + 128


def place():
    tp = lax.axis_index("tp")
    return lax.axis_index("seq"), tp // 4, tp // 2 % 2, tp % 2


def greet(peers):
    barrier = pltpu.get_barrier_semaphore()
    for peer in peers:
        pl.semaphore_signal(barrier, inc=1, device_id=peer, device_id_type=MESH)
    pl.semaphore_wait(barrier, len(peers))


def silu(v):
    return v / (1.0 + jnp.exp(-v))


def mixer_kernel(
    tok, wx, wz, wbc, wdt, cx, cbc, bias, rate, skip, gain, g_out, sq_out,
    buf, w, w_small, st_w, st_dt, xp, zs, small, bco, bcs, own, oth, maps, b_t, xc, dtx, xt,
    ea_x, yloc, cols, rows_a, a_x, spread, aff, entry, state, states, decays, t_out, t_in,
    sends, recvs, locs, sib_s, sib_r, z_s, z_r, halo_s, halo_r, line_s, line_r, t_s, t_r,
):
    s, y, h, c = place()
    up, down, far = (y + 1) % 4, (y + 3) % 4, (y + 2) % 4
    n = 1 - h
    line, x = s // 4, s % 4
    dev = lambda yy, hh, cc: (s, yy * 4 + hh * 2 + cc)
    span = lambda ss, hh: (ss, y * 4 + hh * 2 + c)
    dev_up, dev_down, dev_z, dev_sib = dev(up, h, c), dev(down, h, c), dev(y, n, c), dev(y, h, 1 - c)
    dev_zsib = dev(y, n, 1 - c)
    later, before = (s + 1) % 8, (s + 7) % 8
    on_line = [span(line * 4 + (x + d) % 4, h) for d in (1, 2, 3)]
    across = span((1 - line) * 4 + x, h)
    part_p, part_q = (0, SPLIT), (SPLIT, D - SPLIT)
    p_a, p_b = (0, HALF_P), (HALF_P, SPLIT - HALF_P)
    q_a, q_b = (SPLIT, HALF_Q), (SPLIT + HALF_Q, D - SPLIT - HALF_Q)
    whole = (0, D)

    def at(yy, hh, cc, cols_):
        row = pl.multiple_of((yy * 4 + hh * 2 + cc) * ROWS, ROWS)
        return buf.at[pl.ds(row, ROWS), pl.ds(cols_[0], cols_[1])]

    started = []

    def remote(src, dst, send_sem, recv_sem, to):
        return pltpu.make_async_remote_copy(
            src_ref=src, dst_ref=dst, send_sem=send_sem, recv_sem=recv_sem,
            device_id=to, device_id_type=MESH,
        )

    def push(src, dst, send_sem, recv_sem, to):
        copy = remote(src, dst, send_sem, recv_sem, to)
        copy.start()
        started.append(copy)

    def landed(ref, send_sem, recv_sem):
        remote(ref, ref, send_sem, recv_sem, dev_sib).wait_recv()

    def send(k, yy, hh, cols_, to, own=False):
        dst = at(yy, hh, c, cols_)
        src = tok.at[:, pl.ds(cols_[0], cols_[1])] if own else dst
        push(src, dst, sends.at[k], recvs.at[k], to)

    def arrive(k, yy, hh, cols_, sib=False):
        landed(at(yy, hh, 1 - c if sib else c, cols_), sends.at[k], recvs.at[k])

    tall = pl.ds(pl.multiple_of(c * 64, 64), 64)
    locals_ = [
        pltpu.make_async_copy(tok, at(y, h, c, whole), locs.at[0]),
        pltpu.make_async_copy(wbc, st_w.at[tall], locs.at[1]),
        pltpu.make_async_copy(wdt, st_dt, locs.at[2]),
        pltpu.make_async_copy(wx, w.at[:, pl.ds(0, COLS)], locs.at[3]),
        pltpu.make_async_copy(wz, w.at[:, pl.ds(COLS, COLS)], locs.at[4]),
    ]
    st_w[...] = jnp.zeros_like(st_w)
    for copy in locals_:
        copy.start()
    greet(
        [dev_up, dev_down, dev_z, dev_sib, dev_zsib, across]
        + on_line
        + [span(later, h), span(later, n), span(before, h), span(before, n)]
    )
    send(0, y, h, part_p, dev_z, own=True)
    send(1, y, h, part_q, dev_up, own=True)
    send(2, y, h, part_q, dev_down, own=True)
    send(3, y, h, whole, dev_sib, own=True)
    send(4, y, h, part_q, dev_z, own=True)
    send(5, y, h, part_p, dev_up, own=True)
    send(6, y, h, part_p, dev_down, own=True)

    units = [(y, h), (y, n), (down, h), (up, h), (down, n), (up, n), (far, h), (far, n)]

    def unit_row(k, flip=False):
        yy, hh = units[k]
        return pl.multiple_of((yy * 4 + (1 - hh if flip else hh) * 2) * ROWS, 2 * ROWS)

    def share(k, row, count):
        rows = pl.ds(row, count)
        push(bco.at[rows], bcs.at[rows], sib_s.at[k], sib_r.at[k], dev_sib)

    def merge(k):
        row = unit_row(k)
        rows = pl.ds(row, 2 * ROWS)
        landed(bcs.at[rows], sib_s.at[k], sib_r.at[k])
        own[pl.ds(pl.multiple_of(row + 16, 16), 2 * ROWS), :] = bco[rows, :] + bcs[rows, :]
        half = pl.ds(pl.multiple_of(row + 16 + c * ROWS, 16), ROWS)
        push(own.at[half], oth.at[half], z_s.at[k, 0], z_r.at[k, 0], dev_z)
        push(own.at[half], oth.at[half], z_s.at[k, 1], z_r.at[k, 1], dev_zsib)

    def merged_there(k):
        row = unit_row(k, flip=True)
        for rel, core in ((0, c), (1, 1 - c)):
            ref = oth.at[pl.ds(pl.multiple_of(row + 16 + core * ROWS, 16), ROWS)]
            landed(ref, z_s.at[k, rel], z_r.at[k, rel])

    def project(k):
        row = unit_row(k)
        rows = pl.ds(row, 2 * ROWS)
        part = jnp.dot(buf[rows, :], w_small[...], preferred_element_type=F32)
        small[rows, :] = part
        lane = lax.broadcasted_iota(jnp.int32, part.shape, 1)
        bco[rows, :] = jnp.where(lane // 64 == c, part, 0.0).astype(BF16)
        share(k, row, 2 * ROWS)
        past = pl.ds(pl.multiple_of(row + 16, 16), 2 * ROWS)
        for out, base, target in ((xp, 0, past), (zs, COLS, rows)):

            @pl.loop(0, COLS // 256)
            def _(j):
                col = pl.multiple_of(j * 256, 256)
                out[target, pl.ds(col, 256)] = jnp.dot(
                    buf[rows, :], w[:, pl.ds(base + col, 256)], preferred_element_type=F32
                ).astype(BF16)

    tap_rows = pl.ds(SPAN, 16)
    tap_own = pl.ds(SPAN + 16, 16)
    tap = jnp.concatenate([cbc[...].astype(F32), jnp.zeros((12, 64), F32)], axis=0)
    none = jnp.zeros_like(tap)
    bco[tap_rows, :] = jnp.where(
        c == 0, jnp.concatenate([tap, none], axis=1), jnp.concatenate([none, tap], axis=1)
    ).astype(BF16)
    share(8, SPAN, 16)

    lane_i = lax.broadcasted_iota(jnp.int32, (256, 3 * COLS), 1)
    deep_i = lax.broadcasted_iota(jnp.int32, (256, 3 * COLS), 0)
    spread[...] = jnp.where(
        deep_i % 128 == (lane_i // COLS + 1) * 8 + lane_i % COLS // HEAD_DIM, 1.0, 0.0
    ).astype(BF16)
    head_lane = lax.broadcasted_iota(jnp.int32, (8, COLS), 1) // HEAD_DIM
    head_sub = lax.broadcasted_iota(jnp.int32, (8, COLS), 0)
    skip_x = sum(jnp.where(head_lane[0:1] == i, skip[i], 0.0) for i in range(8))
    sub256 = lax.broadcasted_iota(jnp.int32, (8, BLOCK), 0)
    bias_r = sum(jnp.where(sub256 == i, bias[i], 0.0) for i in range(8))
    rate_r = sum(jnp.where(sub256 == i, rate[i], 0.0) for i in range(8))

    locals_[1].wait()
    locals_[2].wait()
    st_w[pl.ds(pl.multiple_of((1 - c) * 64, 64), 16), :] = st_dt[...]

    @pl.loop(0, D // 128)
    def _(j):
        part = pl.ds(pl.multiple_of(j * 128, 128), 128)
        w_small[part, :] = st_w[:, part].T

    landed(bcs.at[tap_rows], sib_s.at[8], sib_r.at[8])
    own[tap_own, :] = bco[tap_rows, :] + bcs[tap_rows, :]
    push(own.at[tap_own], oth.at[tap_own], z_s.at[8, 0], z_r.at[8, 0], dev_z)
    locals_[0].wait()
    locals_[3].wait()
    locals_[4].wait()
    arrive(3, y, h, whole, sib=True)
    project(0)
    arrive(1, down, h, part_q)
    send(7, down, h, q_a, dev_up)
    send(8, down, h, part_q, dev_z)
    send(9, down, h, part_q, dev_sib)
    arrive(2, up, h, part_q)
    send(10, up, h, q_b, dev_down)
    send(11, up, h, part_q, dev_z)
    send(12, up, h, part_q, dev_sib)
    merge(0)
    arrive(0, y, n, part_p)
    send(13, y, n, part_p, dev_up)
    send(14, y, n, part_p, dev_down)
    send(15, y, n, part_p, dev_sib)
    arrive(7, far, h, q_a)
    send(17, far, h, q_a, dev_z)
    send(18, far, h, q_a, dev_sib)
    arrive(10, far, h, q_b)
    send(19, far, h, q_b, dev_z)
    send(20, far, h, q_b, dev_sib)
    arrive(4, y, n, part_q)
    send(16, y, n, part_q, dev_sib)
    arrive(5, down, h, part_p)
    send(21, down, h, p_a, dev_up)
    send(22, down, h, part_p, dev_sib)
    arrive(6, up, h, part_p)
    send(23, up, h, p_b, dev_down)
    send(24, up, h, part_p, dev_sib)
    arrive(15, y, n, part_p, sib=True)
    arrive(16, y, n, part_q, sib=True)
    project(1)
    arrive(9, down, h, part_q, sib=True)
    arrive(22, down, h, part_p, sib=True)
    project(2)
    merge(1)
    arrive(13, down, n, part_p)
    send(27, down, n, p_a, dev_up)
    send(28, down, n, part_p, dev_sib)
    arrive(14, up, n, part_p)
    send(29, up, n, p_b, dev_down)
    send(30, up, n, part_p, dev_sib)
    arrive(12, up, h, part_q, sib=True)
    arrive(24, up, h, part_p, sib=True)
    project(3)
    merge(2)
    arrive(8, down, n, part_q)
    send(25, down, n, part_q, dev_sib)
    arrive(11, up, n, part_q)
    send(26, up, n, part_q, dev_sib)
    arrive(25, down, n, part_q, sib=True)
    arrive(28, down, n, part_p, sib=True)
    project(4)
    merge(3)
    arrive(21, far, h, p_a)
    send(33, far, h, p_a, dev_sib)
    arrive(23, far, h, p_b)
    send(34, far, h, p_b, dev_sib)
    arrive(26, up, n, part_q, sib=True)
    arrive(30, up, n, part_p, sib=True)
    project(5)
    merge(4)
    arrive(17, far, n, q_a)
    send(31, far, n, q_a, dev_sib)
    arrive(19, far, n, q_b)
    send(32, far, n, q_b, dev_sib)
    arrive(18, far, h, q_a, sib=True)
    arrive(20, far, h, q_b, sib=True)
    arrive(33, far, h, p_a, sib=True)
    arrive(34, far, h, p_b, sib=True)
    project(6)
    merge(5)
    arrive(27, far, n, p_a)
    send(35, far, n, p_a, dev_sib)
    arrive(29, far, n, p_b)
    send(36, far, n, p_b, dev_sib)
    arrive(31, far, n, q_a, sib=True)
    arrive(32, far, n, q_b, sib=True)
    arrive(35, far, n, p_a, sib=True)
    arrive(36, far, n, p_b, sib=True)
    project(7)
    merge(6)
    merge(7)

    last, first = pl.ds(SPAN, 16), pl.ds(0, 16)
    push(xp.at[last], xp.at[first], halo_s.at[0], halo_r.at[0], span(later, h))
    push(own.at[last], own.at[first], halo_s.at[1], halo_r.at[1], span(later, h))
    push(own.at[last], oth.at[first], halo_s.at[2], halo_r.at[2], span(later, n))

    causal = lax.broadcasted_iota(jnp.int32, (BLOCK, BLOCK), 0)
    summing = jnp.where(causal <= lax.broadcasted_iota(jnp.int32, (BLOCK, BLOCK), 1), 1.0, 0.0)

    @pl.loop(0, 4)
    def _(b):
        rows = pl.ds(pl.multiple_of(b * BLOCK, BLOCK), BLOCK)
        turned = small[rows, :].T
        raw = jnp.where(c == 0, turned[64:72], turned[0:8]) + bias_r
        dt = jnp.maximum(raw, 0.0) + jnp.log1p(jnp.exp(-jnp.abs(raw)))
        accum = jnp.dot(
            dt * rate_r, summing, preferred_element_type=F32, precision=lax.Precision.HIGHEST
        )
        end = accum[:, BLOCK - 1 : BLOCK]
        stack = jnp.concatenate(
            [accum, dt, jnp.exp(accum - end) * dt, jnp.exp(-accum), jnp.zeros((96, BLOCK), F32)], axis=0
        )
        cols[rows, :] = stack.T
        rows_a[b] = accum
        total = jnp.sum(jnp.where(head_sub == head_lane, end, 0.0), axis=0, keepdims=True)
        a_x[b] = jnp.broadcast_to(total, (8, COLS))

    decays[x] = a_x[0] + a_x[1] + a_x[2] + a_x[3]
    for d in (1, 2, 3):
        push(decays.at[x], decays.at[x], line_s.at[3 + d], line_r.at[3 + d], on_line[d - 1])

    taps_x = cx[...].astype(F32)
    step = 64

    def convolve(src, row, lanes, taps):
        v = src[pl.ds(row, step + 16), lanes].astype(F32)
        acc = taps[0:1] * v[13 : 13 + step]
        for k in (1, 2, 3):
            acc = acc + taps[k : k + 1] * v[13 + k : 13 + k + step]
        return silu(acc).astype(BF16)

    def conv_x(low, high):
        @pl.loop(low // step, high // step)
        def _(i):
            row = pl.multiple_of(i * step, step)
            for j in range(4):
                lanes = slice(128 * j, 128 * j + 128)
                xc[pl.ds(row, step), lanes] = convolve(xp, row, lanes, taps_x[:, lanes])

    def conv_maps(src, index, taps, low, high):
        @pl.loop(low // step, high // step)
        def _(i):
            row = pl.multiple_of(i * step, step)
            maps[index, pl.ds(row, step), :] = convolve(src, row, slice(0, 128), taps)

    conv_x(step, SPAN)
    landed(xp.at[first], halo_s.at[0], halo_r.at[0])

    @pl.when(s == 0)
    def _():
        xp[first, :] = jnp.zeros((16, COLS), BF16)

    conv_x(0, step)

    @pl.loop(0, 4)
    def _(b):
        rows = pl.ds(pl.multiple_of(b * BLOCK, BLOCK), BLOCK)
        exact = cols[rows, :]
        high = exact.astype(BF16)
        both = jnp.concatenate([high, (exact - high.astype(F32)).astype(BF16)], axis=1)
        for j in range(4):
            lanes = slice(128 * j, 128 * j + 128)
            value = xc[rows, lanes].astype(F32)
            grown = [
                jnp.dot(both, spread[:, q * COLS + 128 * j : q * COLS + 128 * j + 128], preferred_element_type=F32)
                for q in range(3)
            ]
            dtx[rows, lanes] = (value * grown[0]).astype(BF16)
            xt[rows, lanes] = (value * grown[1]).astype(BF16)
            ea_x[rows, lanes] = grown[2]

    tap_o = own[tap_own, :][0:4].astype(F32)
    conv_maps(own, h, tap_o, step, SPAN)
    landed(oth.at[tap_own], z_s.at[8, 0], z_r.at[8, 0])
    for k in range(8):
        merged_there(k)
    tap_t = oth[tap_own, :][0:4].astype(F32)
    conv_maps(oth, n, tap_t, step, SPAN)
    landed(own.at[first], halo_s.at[1], halo_r.at[1])
    landed(oth.at[first], halo_s.at[2], halo_r.at[2])

    @pl.when(s == 0)
    def _():
        own[first, :] = jnp.zeros((16, 128), BF16)
        oth[first, :] = jnp.zeros((16, 128), BF16)

    conv_maps(own, h, tap_o, 0, step)
    conv_maps(oth, n, tap_t, 0, step)

    state[...] = jnp.zeros_like(state)

    @pl.loop(0, 4)
    def _(b):
        rows = pl.ds(pl.multiple_of(b * BLOCK, BLOCK), BLOCK)
        turned = maps[0, rows, :].T
        b_t[:, rows] = turned
        entry[b] = state[...]
        state[...] = jnp.exp(-a_x[b][0:1]) * state[...] + jnp.dot(
            turned, xt[rows, :], preferred_element_type=F32
        )

    states[x] = state[...].astype(BF16)
    for d in (1, 2, 3):
        push(states.at[x], states.at[x], line_s.at[d - 1], line_r.at[d - 1], on_line[d - 1])

    pair_lane = lax.broadcasted_iota(jnp.int32, (128, 128), 1)

    @pl.loop(0, 4)
    def _(b):
        start = pl.multiple_of(b * BLOCK, BLOCK)
        rows = pl.ds(start, BLOCK)
        aff[...] = jnp.dot(maps[1, rows, :], b_t[:, rows], preferred_element_type=F32)
        accum = rows_a[b]
        for t in (0, 1):
            reach = 128 * (t + 1)
            here = pl.ds(pl.multiple_of(start + 128 * t, 128), 128)
            near = pl.ds(start, reach)
            keep = (
                lax.broadcasted_iota(jnp.int32, (128, reach), 0) + 128 * t
                >= lax.broadcasted_iota(jnp.int32, (128, reach), 1)
            )
            column = cols[here, :]
            for j in range(4):
                lanes = slice(128 * j, 128 * j + 128)
                weights = [
                    jnp.where(
                        keep,
                        aff[128 * t : 128 * t + 128, 0:reach]
                        * jnp.exp(accum[i : i + 1, 0:reach] - column[:, i : i + 1]),
                        0.0,
                    ).astype(BF16)
                    for i in (2 * j, 2 * j + 1)
                ]
                both = jnp.dot(
                    jnp.concatenate(weights, axis=0), dtx[near, lanes], preferred_element_type=F32
                )
                yloc[here, lanes] = (
                    jnp.where(pair_lane < HEAD_DIM, both[0:128], both[128:256])
                    + skip_x[:, lanes] * xc[here, lanes].astype(F32)
                )

    for d in (1, 2, 3):
        index = (x + 4 - d) % 4
        landed(decays.at[index], line_s.at[3 + d], line_r.at[3 + d])
        landed(states.at[index], line_s.at[d - 1], line_r.at[d - 1])
    total = jnp.zeros((STATE, COLS), F32)
    for j in range(4):
        total = jnp.exp(-decays[j][0:1]) * total + states[j].astype(F32)
    t_out[...] = total.astype(BF16)
    push(t_out, t_in, t_s.at[0], t_r.at[0], across)
    total = jnp.zeros((STATE, COLS), F32)
    passed = jnp.zeros((1, COLS), F32)
    for j in range(4):
        taken = jnp.where(j < x, 1.0, 0.0)
        through = jnp.where(j < x, jnp.exp(-decays[j][0:1]), 1.0)
        total = through * total + taken * states[j].astype(F32)
        passed = passed + taken * decays[j][0:1]
    landed(t_in, t_s.at[0], t_r.at[0])
    state[...] = total + jnp.where(line == 1, jnp.exp(-passed), 0.0) * t_in[...].astype(F32)

    @pl.loop(0, 4)
    def _(b):
        rows = pl.ds(pl.multiple_of(b * BLOCK, BLOCK), BLOCK)
        ahead = sum(jnp.where(i < b, 1.0, 0.0) * a_x[i][0:1] for i in range(3))
        squares = jnp.zeros((BLOCK, 128), F32)
        for j in range(4):
            lanes = slice(128 * j, 128 * j + 128)
            entering = entry[b, :, lanes] + jnp.exp(-ahead[:, lanes]) * state[:, lanes]
            far_y = jnp.dot(maps[1, rows, :], entering.astype(BF16), preferred_element_type=F32)
            value = yloc[rows, lanes] + far_y * ea_x[rows, lanes]
            value = value * silu(zs[rows, lanes].astype(F32))
            squares = squares + value * value
            g_out[rows, lanes] = (value * gain[:, lanes].astype(F32)).astype(BF16)
        sq_out[rows, :] = jnp.broadcast_to(
            jnp.sum(squares, axis=1, keepdims=True), (BLOCK, 128)
        ).astype(BF16)

    for copy in started:
        copy.wait_send()


def mix(tokens, w_x, w_z, w_bc, w_dt, conv_x, conv_bc, dt_bias, decay_rate, skip, norm_gain):
    anywhere = pl.BlockSpec(memory_space=pl.ANY)
    vmem = pl.BlockSpec(memory_space=pltpu.VMEM)
    smem = pl.BlockSpec(memory_space=pltpu.SMEM)
    dma = pltpu.SemaphoreType.DMA
    return pl.pallas_call(
        mixer_kernel,
        out_shape=(
            jax.ShapeDtypeStruct((SPAN, COLS), BF16),
            jax.ShapeDtypeStruct((SPAN, 128), BF16),
        ),
        in_specs=[anywhere] * 5 + [vmem, vmem, smem, smem, smem, vmem],
        out_specs=(vmem, vmem),
        scratch_shapes=[
            pltpu.VMEM((SPAN, D), BF16),
            pltpu.VMEM((D, 2 * COLS), BF16),
            pltpu.VMEM((D, 128), BF16),
            pltpu.VMEM((128, D), BF16),
            pltpu.VMEM((16, D), BF16),
            pltpu.VMEM((SPAN + 16, COLS), BF16),
            pltpu.VMEM((SPAN, COLS), BF16),
            pltpu.VMEM((SPAN, 128), F32),
            pltpu.VMEM((SPAN + 16, 128), BF16),
            pltpu.VMEM((SPAN + 16, 128), BF16),
            pltpu.VMEM((SPAN + 32, 128), BF16),
            pltpu.VMEM((SPAN + 32, 128), BF16),
            pltpu.VMEM((2, SPAN, 128), BF16),
            pltpu.VMEM((STATE, SPAN), BF16),
            pltpu.VMEM((SPAN, COLS), BF16),
            pltpu.VMEM((SPAN, COLS), BF16),
            pltpu.VMEM((SPAN, COLS), BF16),
            pltpu.VMEM((SPAN, COLS), F32),
            pltpu.VMEM((SPAN, COLS), F32),
            pltpu.VMEM((SPAN, 128), F32),
            pltpu.VMEM((4, 8, BLOCK), F32),
            pltpu.VMEM((4, 8, COLS), F32),
            pltpu.VMEM((256, 3 * COLS), BF16),
            pltpu.VMEM((BLOCK, BLOCK), F32),
            pltpu.VMEM((4, STATE, COLS), F32),
            pltpu.VMEM((STATE, COLS), F32),
            pltpu.VMEM((4, STATE, COLS), BF16),
            pltpu.VMEM((4, 8, COLS), F32),
            pltpu.VMEM((STATE, COLS), BF16),
            pltpu.VMEM((STATE, COLS), BF16),
            dma((37,)), dma((37,)), dma((5,)), dma((9,)), dma((9,)), dma((9, 2)), dma((9, 2)),
            dma((3,)), dma((3,)), dma((7,)), dma((7,)), dma((1,)), dma((1,)),
        ],
        compiler_params=pltpu.CompilerParams(
            collective_id=1, has_side_effects=True, vmem_limit_bytes=58 << 20
        ),
        name="mix",
    )(
        tokens, w_x, w_z, w_bc.T, jnp.pad(w_dt.T, ((0, 8), (0, 0))), conv_x, conv_bc, dt_bias,
        decay_rate, skip, norm_gain.reshape(1, COLS),
    )


def reduce_kernel(
    g, sq, w_out, out, o, sib, zq, pa, pb, qa, qb, pf, qf, zp, sends, recvs
):
    s, y, h, c = place()
    up, down, far = (y + 1) % 4, (y + 3) % 4, (y + 2) % 4
    dev = lambda yy, hh, cc: (s, yy * 4 + hh * 2 + cc)
    dev_up, dev_down, dev_z, dev_sib = dev(up, h, c), dev(down, h, c), dev(y, 1 - h, c), dev(y, h, 1 - c)
    wide_q = WIDE - SPLIT
    part_p, part_q = (0, SPLIT), (SPLIT, wide_q)
    p_a, p_b = (0, HALF_P), (HALF_P, SPLIT - HALF_P)
    q_a, q_b = (SPLIT, HALF_Q), (SPLIT + HALF_Q, wide_q - HALF_Q)
    started = []

    def at(yy, hh, cc, cols):
        row = pl.multiple_of((yy * 4 + hh * 2 + cc) * ROWS, ROWS)
        return o.at[pl.ds(row, ROWS), pl.ds(cols[0], cols[1])]

    def copy_of(k, src, dst, to):
        return pltpu.make_async_remote_copy(
            src_ref=src, dst_ref=dst, send_sem=sends.at[k], recv_sem=recvs.at[k],
            device_id=to, device_id_type=MESH,
        )

    def send(k, src, dst, to):
        copy = copy_of(k, src, dst, to)
        copy.start()
        started.append(copy)

    def arrive(k, ref):
        copy_of(k, ref, ref, dev_sib).wait_recv()

    def add(yy, hh, cols, ref):
        target = at(yy, hh, c, cols)

        @pl.loop(0, ROWS // 16)
        def _(i):
            rows = pl.ds(pl.multiple_of(i * 16, 16), 16)
            target[rows, :] = (target[rows, :].astype(F32) + ref[rows, :].astype(F32)).astype(BF16)

    def chip(yy, hh):
        return yy * 2 + hh

    def partial(yy, hh, k):
        row = pl.multiple_of((yy * 4 + hh * 2) * ROWS, 2 * ROWS)
        rows = pl.ds(row, 2 * ROWS)
        left = g[rows, :]

        @pl.loop(0, D // 512)
        def _(j):
            cols = pl.ds(pl.multiple_of(j * 512, 512), 512)
            o[rows, cols] = jnp.dot(left, w_out[:, cols], preferred_element_type=F32).astype(BF16)

        o[rows, pl.ds(D, 128)] = sq[rows, :]
        send(k, at(yy, hh, 1 - c, (0, WIDE)), sib.at[chip(yy, hh)], dev_sib)

    def joined(yy, hh, k):
        ref = sib.at[chip(yy, hh)]
        arrive(k, ref)
        add(yy, hh, (0, WIDE), ref)

    greet([dev_up, dev_down, dev_z, dev_sib])
    n = 1 - h
    partial(far, n, 0)
    partial(far, h, 1)
    joined(far, n, 0)
    send(8, at(far, n, c, p_a), pa.at[n], dev_up)
    send(9, at(far, n, c, p_b), pb.at[n], dev_down)
    send(10, at(far, n, c, part_q), zq.at[far], dev_z)
    partial(up, n, 2)
    joined(far, h, 1)
    send(11, at(far, h, c, p_a), pa.at[h], dev_up)
    send(12, at(far, h, c, p_b), pb.at[h], dev_down)
    partial(down, n, 3)
    joined(up, n, 2)
    send(13, at(up, n, c, part_q), zq.at[up], dev_z)
    partial(up, h, 4)
    joined(down, n, 3)
    send(14, at(down, n, c, part_q), zq.at[down], dev_z)
    arrive(8, pa.at[n])
    add(up, n, p_a, pa.at[n])
    send(15, at(up, n, c, part_p), pf.at[0, n], dev_up)
    arrive(9, pb.at[n])
    add(down, n, p_b, pb.at[n])
    send(16, at(down, n, c, part_p), pf.at[1, n], dev_down)
    partial(down, h, 5)
    joined(up, h, 4)
    arrive(11, pa.at[h])
    add(up, h, p_a, pa.at[h])
    send(17, at(up, h, c, part_p), pf.at[0, h], dev_up)
    partial(y, n, 6)
    joined(down, h, 5)
    arrive(12, pb.at[h])
    add(down, h, p_b, pb.at[h])
    send(18, at(down, h, c, part_p), pf.at[1, h], dev_down)
    joined(y, n, 6)
    send(19, at(y, n, c, part_q), zq.at[y], dev_z)
    partial(y, h, 7)
    arrive(10, zq.at[far])
    add(far, h, part_q, zq.at[far])
    send(20, at(far, h, c, q_a), qa, dev_up)
    send(21, at(far, h, c, q_b), qb, dev_down)
    joined(y, h, 7)
    arrive(13, zq.at[up])
    add(up, h, part_q, zq.at[up])
    arrive(20, qa)
    add(up, h, q_a, qa)
    send(22, at(up, h, c, part_q), qf.at[0], dev_up)
    arrive(14, zq.at[down])
    add(down, h, part_q, zq.at[down])
    arrive(21, qb)
    add(down, h, q_b, qb)
    send(23, at(down, h, c, part_q), qf.at[1], dev_down)
    arrive(15, pf.at[0, n])
    add(y, n, part_p, pf.at[0, n])
    arrive(16, pf.at[1, n])
    add(y, n, part_p, pf.at[1, n])
    send(24, at(y, n, c, part_p), zp, dev_z)
    arrive(17, pf.at[0, h])
    add(y, h, part_p, pf.at[0, h])
    arrive(18, pf.at[1, h])
    add(y, h, part_p, pf.at[1, h])
    arrive(19, zq.at[y])
    arrive(22, qf.at[0])
    arrive(23, qf.at[1])
    mine_q = at(y, h, c, part_q)
    mine_p = at(y, h, c, part_p)
    terms = (mine_q, zq.at[y], qf.at[0], qf.at[1])
    lane = pl.ds(D - SPLIT, 128)
    squares = sum(t[:, lane].astype(F32) for t in terms)
    scale = lax.rsqrt(squares / (COLS * 16) + 1e-05)

    @pl.loop(0, (D - SPLIT) // 128)
    def _(j):
        cols = pl.ds(pl.multiple_of(j * 128, 128), 128)
        total = sum(t[:, cols].astype(F32) for t in terms)
        out[:, pl.ds(pl.multiple_of(SPLIT + j * 128, 128), 128)] = (total * scale).astype(BF16)

    arrive(24, zp)

    @pl.loop(0, SPLIT // 128)
    def _(j):
        cols = pl.ds(pl.multiple_of(j * 128, 128), 128)
        total = mine_p[:, cols].astype(F32) + zp[:, cols].astype(F32)
        out[:, cols] = (total * scale).astype(BF16)

    for copy in started:
        copy.wait_send()


def project_reduce(g, sq, w_out):
    vmem = pl.BlockSpec(memory_space=pltpu.VMEM)
    wide_q = WIDE - SPLIT
    return pl.pallas_call(
        reduce_kernel,
        out_shape=jax.ShapeDtypeStruct((ROWS, D), BF16),
        in_specs=[vmem] * 3,
        out_specs=vmem,
        scratch_shapes=[
            pltpu.VMEM((SPAN, WIDE), BF16),
            pltpu.VMEM((8, ROWS, WIDE), BF16),
            pltpu.VMEM((4, ROWS, wide_q), BF16),
            pltpu.VMEM((2, ROWS, HALF_P), BF16),
            pltpu.VMEM((2, ROWS, SPLIT - HALF_P), BF16),
            pltpu.VMEM((ROWS, HALF_Q), BF16),
            pltpu.VMEM((ROWS, wide_q - HALF_Q), BF16),
            pltpu.VMEM((2, 2, ROWS, SPLIT), BF16),
            pltpu.VMEM((2, ROWS, wide_q), BF16),
            pltpu.VMEM((ROWS, SPLIT), BF16),
            pltpu.SemaphoreType.DMA((25,)),
            pltpu.SemaphoreType.DMA((25,)),
        ],
        compiler_params=pltpu.CompilerParams(
            collective_id=2, has_side_effects=True, vmem_limit_bytes=56 << 20
        ),
        name="project_reduce",
    )(g, sq, w_out)


def on_device(
    tokens, w_x, w_z, w_bc, w_dt, conv_x, conv_bc, dt_bias, decay_rate, skip, norm_gain, w_out
):
    gated, squares = mix(
        tokens, w_x, w_z, w_bc, w_dt, conv_x, conv_bc, dt_bias, decay_rate, skip, norm_gain
    )
    return project_reduce(gated, squares, w_out)


def solution(mesh):
    placed = (
        P(("seq", "tp"), None),
        P(None, "tp"),
        P(None, "tp"),
        P(None, "tp"),
        P(None, "tp"),
        P(None, "tp"),
        P(None, "tp"),
        P("tp"),
        P("tp"),
        P("tp"),
        P("tp"),
        P("tp", None),
    )
    return jax.shard_map(
        on_device, mesh=mesh, in_specs=placed, out_specs=P(("seq", "tp"), None), check_vma=False
    )
```

time: 231 us -> 150 us (0.65)
  the two profiles are of different devices: /device:TPU:32 before, /device:TPU:1 now
where the time goes in v2:
time: 150 us
  Pallas kernels  145 us (97%)
  local copies, waits for them, and re-layouts  4.92 us (3%)
    pallas_call x1, Pallas kernels, mix(): pl.pallas_call(mixer_kernel, out_shape=(jax.ShapeDtypeStruct((SPAN, COLS)...  84.1 us
    pallas_call x1, Pallas kernels, project_reduce(): pl.pallas_call(reduce_kernel, out_shape=jax.ShapeDtypeStruct((ROWS, D), B...  60.7 us

profile of v2, /device:TPU:1, one launch (start us, length us, event | category | flops | bytes accessed | tf_op | source)
XLA Modules:
  0.0 149.7 jit_solution(13891682263460914921)
XLA Ops:
  0.0 1.3 reshape.3.gain
  1.3 1.6 %pad.4.wdt = bf16[16,6144]{1,0:T(8,128)(2,1)} pad(bf16[8,6144]{1,0:T(8,128)(2,1)} %bitcast.3, bf16[]{:T(256)} %constant.2.clone.1), padding=0_8x0_0 | pad | bytes 294914 | tf_op jit(solution)/shard_map/jit(_pad)/pad | solution.py:520
  2.9 84.1 %mix.1 = (bf16[1024,512]{1,0:T(8,128)(2,1)}, bf16[1024,128]{1,0:T(8,128)(2,1)}) custom-call(bf16[64,6144]{1,0:T(8,128)(2,1)} %tok.1, bf16[6144,512]{1,0:T(8,128)(2,1)} %wx.1, bf16[6144,512]{1,0:T(8,128)(2,1)} %wz.1, bf16[64,6144]{1,0:T(8,128)(2,1)} %bitcast.2, bf16[16,6144]{1,0:T(8,128)(2,1)} %pad.4.wdt, bf16[4,512]{1,0:T(4,128)(2,1)} %cx.1, ...), custom_call_target="tpu_custom_call" | custom-call | tf_op jit(solution)/shard_map/mix/pallas_call | solution.py:473
  87.0 60.7 %project_reduce.1 = bf16[64,6144]{1,0:T(8,128)(2,1)} custom-call(bf16[1024,512]{1,0:T(8,128)(2,1)} %get-tuple-element.7.g, bf16[1024,128]{1,0:T(8,128)(2,1)} %get-tuple-element.8.sq, bf16[512,6144]{1,0:T(8,128)(2,1)} %w_out.1), custom_call_target="tpu_custom_call" | custom-call | tf_op jit(solution)/shard_map/project_reduce/pallas_call | solution.py:677
  147.7 2.1 %copy.14 = bf16[64,6144]{1,0:T(8,128)(2,1)} copy(bf16[64,6144]{1,0:T(8,128)(2,1)} %project_reduce.1) | data formatting | bytes 1572864

commit v3 on v2

--- a/solution.py
+++ b/solution.py
@@ -40,7 +40,7 @@
 
 def mixer_kernel(
     tok, wx, wz, wbc, wdt, cx, cbc, bias, rate, skip, gain, g_out, sq_out,
-    buf, w, w_small, st_w, st_dt, xp, zs, small, bco, bcs, own, oth, maps, b_t, xc, dtx, xt,
+    buf, partials, w, w_small, st_w, st_dt, xp, zs, small, bco, bcs, own, oth, maps, b_t, xc, dtx, xt,
     ea_x, yloc, cols, rows_a, a_x, spread, aff, entry, state, states, decays, t_out, t_in,
     sends, recvs, locs, sib_s, sib_r, z_s, z_r, halo_s, halo_r, line_s, line_r, t_s, t_r,
 ):
@@ -76,6 +76,12 @@
         copy = remote(src, dst, send_sem, recv_sem, to)
         copy.start()
         started.append(copy)
+        return copy
+
+    def sent(*copies):
+        for copy in copies:
+            copy.wait_send()
+            started[:] = [other for other in started if other is not copy]
 
     def landed(ref, send_sem, recv_sem):
         remote(ref, ref, send_sem, recv_sem, dev_sib).wait_recv()
@@ -83,7 +89,7 @@
     def send(k, yy, hh, cols_, to, own=False):
         dst = at(yy, hh, c, cols_)
         src = tok.at[:, pl.ds(cols_[0], cols_[1])] if own else dst
-        push(src, dst, sends.at[k], recvs.at[k], to)
+        return push(src, dst, sends.at[k], recvs.at[k], to)
 
     def arrive(k, yy, hh, cols_, sib=False):
         landed(at(yy, hh, 1 - c if sib else c, cols_), sends.at[k], recvs.at[k])
@@ -108,9 +114,6 @@
     send(1, y, h, part_q, dev_up, own=True)
     send(2, y, h, part_q, dev_down, own=True)
     send(3, y, h, whole, dev_sib, own=True)
-    send(4, y, h, part_q, dev_z, own=True)
-    send(5, y, h, part_p, dev_up, own=True)
-    send(6, y, h, part_p, dev_down, own=True)
 
     units = [(y, h), (y, n), (down, h), (up, h), (down, n), (up, n), (far, h), (far, n)]
 
@@ -137,23 +140,31 @@
             ref = oth.at[pl.ds(pl.multiple_of(row + 16 + core * ROWS, 16), ROWS)]
             landed(ref, z_s.at[k, rel], z_r.at[k, rel])
 
-    def project(k):
+    def project(k, cols_=(0, D), keep=None, add=None):
         row = unit_row(k)
         rows = pl.ds(row, 2 * ROWS)
-        part = jnp.dot(buf[rows, :], w_small[...], preferred_element_type=F32)
-        small[rows, :] = part
-        lane = lax.broadcasted_iota(jnp.int32, part.shape, 1)
-        bco[rows, :] = jnp.where(lane // 64 == c, part, 0.0).astype(BF16)
-        share(k, row, 2 * ROWS)
+        inner = pl.ds(cols_[0], cols_[1])
+        part = jnp.dot(buf[rows, inner], w_small[inner, :], preferred_element_type=F32)
+        if add is not None:
+            part = part + partials[add, :, 2 * COLS : 2 * COLS + 128]
+        if keep is not None:
+            partials[keep, :, 2 * COLS : 2 * COLS + 128] = part
+        else:
+            small[rows, :] = part
+            lane = lax.broadcasted_iota(jnp.int32, part.shape, 1)
+            bco[rows, :] = jnp.where(lane // 64 == c, part, 0.0).astype(BF16)
+            share(k, row, 2 * ROWS)
         past = pl.ds(pl.multiple_of(row + 16, 16), 2 * ROWS)
         for out, base, target in ((xp, 0, past), (zs, COLS, rows)):
 
-            @pl.loop(0, COLS // 256)
-            def _(j):
-                col = pl.multiple_of(j * 256, 256)
-                out[target, pl.ds(col, 256)] = jnp.dot(
-                    buf[rows, :], w[:, pl.ds(base + col, 256)], preferred_element_type=F32
-                ).astype(BF16)
+            lanes = pl.ds(base, COLS)
+            part = jnp.dot(buf[rows, inner], w[inner, lanes], preferred_element_type=F32)
+            if add is not None:
+                part = part + partials[add, :, lanes]
+            if keep is not None:
+                partials[keep, :, lanes] = part
+            else:
+                out[target, :] = part.astype(BF16)
 
     tap_rows = pl.ds(SPAN, 16)
     tap_own = pl.ds(SPAN + 16, 16)
@@ -178,7 +189,9 @@
 
     locals_[1].wait()
     locals_[2].wait()
-    st_w[pl.ds(pl.multiple_of((1 - c) * 64, 64), 16), :] = st_dt[...]
+    st_w[pl.ds(pl.multiple_of((1 - c) * 64, 64), 16), :] = (
+        jnp.concatenate([st_dt[...].astype(F32), jnp.zeros((8, D), F32)], axis=0).astype(BF16)
+    )
 
     @pl.loop(0, D // 128)
     def _(j):
@@ -193,6 +206,9 @@
     locals_[4].wait()
     arrive(3, y, h, whole, sib=True)
     project(0)
+    send(5, y, h, part_p, dev_up, own=True)
+    send(6, y, h, part_p, dev_down, own=True)
+    send(4, y, h, part_q, dev_z, own=True)
     arrive(1, down, h, part_q)
     send(7, down, h, q_a, dev_up)
     send(8, down, h, part_q, dev_z)
@@ -206,12 +222,6 @@
     send(13, y, n, part_p, dev_up)
     send(14, y, n, part_p, dev_down)
     send(15, y, n, part_p, dev_sib)
-    arrive(7, far, h, q_a)
-    send(17, far, h, q_a, dev_z)
-    send(18, far, h, q_a, dev_sib)
-    arrive(10, far, h, q_b)
-    send(19, far, h, q_b, dev_z)
-    send(20, far, h, q_b, dev_sib)
     arrive(4, y, n, part_q)
     send(16, y, n, part_q, dev_sib)
     arrive(5, down, h, part_p)
@@ -223,56 +233,64 @@
     arrive(15, y, n, part_p, sib=True)
     arrive(16, y, n, part_q, sib=True)
     project(1)
+    arrive(7, far, h, q_a)
+    send(17, far, h, q_a, dev_z)
+    send(18, far, h, q_a, dev_sib)
+    arrive(10, far, h, q_b)
+    send(19, far, h, q_b, dev_z)
+    send(20, far, h, q_b, dev_sib)
     arrive(9, down, h, part_q, sib=True)
     arrive(22, down, h, part_p, sib=True)
     project(2)
     merge(1)
+    arrive(8, down, n, part_q)
+    send(25, down, n, part_q, dev_sib)
+    arrive(12, up, h, part_q, sib=True)
+    arrive(24, up, h, part_p, sib=True)
+    project(3)
+    arrive(18, far, h, q_a, sib=True)
+    arrive(20, far, h, q_b, sib=True)
+    project(6, part_q, keep=0)
+    merge(2)
     arrive(13, down, n, part_p)
     send(27, down, n, p_a, dev_up)
     send(28, down, n, part_p, dev_sib)
     arrive(14, up, n, part_p)
     send(29, up, n, p_b, dev_down)
     send(30, up, n, part_p, dev_sib)
-    arrive(12, up, h, part_q, sib=True)
-    arrive(24, up, h, part_p, sib=True)
-    project(3)
-    merge(2)
-    arrive(8, down, n, part_q)
-    send(25, down, n, part_q, dev_sib)
+    merge(3)
     arrive(11, up, n, part_q)
     send(26, up, n, part_q, dev_sib)
-    arrive(25, down, n, part_q, sib=True)
-    arrive(28, down, n, part_p, sib=True)
-    project(4)
-    merge(3)
     arrive(21, far, h, p_a)
     send(33, far, h, p_a, dev_sib)
     arrive(23, far, h, p_b)
     send(34, far, h, p_b, dev_sib)
+    arrive(25, down, n, part_q, sib=True)
+    arrive(28, down, n, part_p, sib=True)
+    project(4)
     arrive(26, up, n, part_q, sib=True)
     arrive(30, up, n, part_p, sib=True)
     project(5)
     merge(4)
+    arrive(33, far, h, p_a, sib=True)
+    arrive(34, far, h, p_b, sib=True)
+    project(6, part_p, add=0)
+    merge(5)
     arrive(17, far, n, q_a)
     send(31, far, n, q_a, dev_sib)
     arrive(19, far, n, q_b)
     send(32, far, n, q_b, dev_sib)
-    arrive(18, far, h, q_a, sib=True)
-    arrive(20, far, h, q_b, sib=True)
-    arrive(33, far, h, p_a, sib=True)
-    arrive(34, far, h, p_b, sib=True)
-    project(6)
-    merge(5)
     arrive(27, far, n, p_a)
     send(35, far, n, p_a, dev_sib)
     arrive(29, far, n, p_b)
     send(36, far, n, p_b, dev_sib)
     arrive(31, far, n, q_a, sib=True)
     arrive(32, far, n, q_b, sib=True)
+    project(7, part_q, keep=1)
+    merge(6)
     arrive(35, far, n, p_a, sib=True)
     arrive(36, far, n, p_b, sib=True)
-    project(7)
-    merge(6)
+    project(7, part_p, add=1)
     merge(7)
 
     last, first = pl.ds(SPAN, 16), pl.ds(0, 16)
@@ -303,7 +321,7 @@
 
     decays[x] = a_x[0] + a_x[1] + a_x[2] + a_x[3]
     for d in (1, 2, 3):
-        push(decays.at[x], decays.at[x], line_s.at[3 + d], line_r.at[3 + d], on_line[d - 1])
+        push(decays.at[x], decays.at[x], line_s.at[5 + d], line_r.at[5 + d], on_line[d - 1])
 
     taps_x = cx[...].astype(F32)
     step = 64
@@ -386,8 +404,11 @@
         )
 
     states[x] = state[...].astype(BF16)
-    for d in (1, 2, 3):
-        push(states.at[x], states.at[x], line_s.at[d - 1], line_r.at[d - 1], on_line[d - 1])
+    halves = [pl.ds(0, COLS // 2), pl.ds(COLS // 2, COLS // 2)]
+    for part, lanes in enumerate(halves):
+        for d in (1, 3, 2):
+            ref = states.at[x, :, lanes]
+            push(ref, ref, line_s.at[part * 3 + d - 1], line_r.at[part * 3 + d - 1], on_line[d - 1])
 
     pair_lane = lax.broadcasted_iota(jnp.int32, (128, 128), 1)
 
@@ -427,22 +448,29 @@
 
     for d in (1, 2, 3):
         index = (x + 4 - d) % 4
-        landed(decays.at[index], line_s.at[3 + d], line_r.at[3 + d])
-        landed(states.at[index], line_s.at[d - 1], line_r.at[d - 1])
-    total = jnp.zeros((STATE, COLS), F32)
-    for j in range(4):
-        total = jnp.exp(-decays[j][0:1]) * total + states[j].astype(F32)
-    t_out[...] = total.astype(BF16)
-    push(t_out, t_in, t_s.at[0], t_r.at[0], across)
-    total = jnp.zeros((STATE, COLS), F32)
-    passed = jnp.zeros((1, COLS), F32)
-    for j in range(4):
-        taken = jnp.where(j < x, 1.0, 0.0)
-        through = jnp.where(j < x, jnp.exp(-decays[j][0:1]), 1.0)
-        total = through * total + taken * states[j].astype(F32)
-        passed = passed + taken * decays[j][0:1]
-    landed(t_in, t_s.at[0], t_r.at[0])
-    state[...] = total + jnp.where(line == 1, jnp.exp(-passed), 0.0) * t_in[...].astype(F32)
+        landed(decays.at[index], line_s.at[5 + d], line_r.at[5 + d])
+    for part, lanes in enumerate(halves):
+        for d in (1, 3, 2):
+            landed(
+                states.at[(x + 4 - d) % 4, :, lanes], line_s.at[part * 3 + d - 1], line_r.at[part * 3 + d - 1]
+            )
+        total = jnp.zeros((STATE, COLS // 2), F32)
+        for j in range(4):
+            total = jnp.exp(-decays[j, 0:1, lanes]) * total + states[j, :, lanes].astype(F32)
+        t_out[:, lanes] = total.astype(BF16)
+        push(t_out.at[:, lanes], t_in.at[:, lanes], t_s.at[part], t_r.at[part], across)
+    for part, lanes in enumerate(halves):
+        total = jnp.zeros((STATE, COLS // 2), F32)
+        passed = jnp.zeros((1, COLS // 2), F32)
+        for j in range(4):
+            taken = jnp.where(j < x, 1.0, 0.0)
+            through = jnp.where(j < x, jnp.exp(-decays[j, 0:1, lanes]), 1.0)
+            total = through * total + taken * states[j, :, lanes].astype(F32)
+            passed = passed + taken * decays[j, 0:1, lanes]
+        landed(t_in.at[:, lanes], t_s.at[part], t_r.at[part])
+        state[:, lanes] = total + jnp.where(line == 1, jnp.exp(-passed), 0.0) * t_in[:, lanes].astype(F32)
+
+    gain_r = gain[...].astype(F32).reshape(1, COLS)
 
     @pl.loop(0, 4)
     def _(b):
@@ -456,7 +484,7 @@
             value = yloc[rows, lanes] + far_y * ea_x[rows, lanes]
             value = value * silu(zs[rows, lanes].astype(F32))
             squares = squares + value * value
-            g_out[rows, lanes] = (value * gain[:, lanes].astype(F32)).astype(BF16)
+            g_out[rows, lanes] = (value * gain_r[:, lanes]).astype(BF16)
         sq_out[rows, :] = jnp.broadcast_to(
             jnp.sum(squares, axis=1, keepdims=True), (BLOCK, 128)
         ).astype(BF16)
@@ -480,10 +508,11 @@
         out_specs=(vmem, vmem),
         scratch_shapes=[
             pltpu.VMEM((SPAN, D), BF16),
+            pltpu.VMEM((2, 2 * ROWS, 2 * COLS + 128), F32),
             pltpu.VMEM((D, 2 * COLS), BF16),
             pltpu.VMEM((D, 128), BF16),
             pltpu.VMEM((128, D), BF16),
-            pltpu.VMEM((16, D), BF16),
+            pltpu.VMEM((8, D), BF16),
             pltpu.VMEM((SPAN + 16, COLS), BF16),
             pltpu.VMEM((SPAN, COLS), BF16),
             pltpu.VMEM((SPAN, 128), F32),
@@ -510,15 +539,15 @@
             pltpu.VMEM((STATE, COLS), BF16),
             pltpu.VMEM((STATE, COLS), BF16),
             dma((37,)), dma((37,)), dma((5,)), dma((9,)), dma((9,)), dma((9, 2)), dma((9, 2)),
-            dma((3,)), dma((3,)), dma((7,)), dma((7,)), dma((1,)), dma((1,)),
+            dma((3,)), dma((3,)), dma((9,)), dma((9,)), dma((2,)), dma((2,)),
         ],
         compiler_params=pltpu.CompilerParams(
             collective_id=1, has_side_effects=True, vmem_limit_bytes=58 << 20
         ),
         name="mix",
     )(
-        tokens, w_x, w_z, w_bc.T, jnp.pad(w_dt.T, ((0, 8), (0, 0))), conv_x, conv_bc, dt_bias,
-        decay_rate, skip, norm_gain.reshape(1, COLS),
+        tokens, w_x, w_z, w_bc.T, w_dt.T, conv_x, conv_bc, dt_bias,
+        decay_rate, skip, norm_gain,
     )
 
 
@@ -549,6 +578,7 @@
         copy = copy_of(k, src, dst, to)
         copy.start()
         started.append(copy)
+        return copy
 
     def arrive(k, ref):
         copy_of(k, ref, ref, dev_sib).wait_recv()
@@ -569,9 +599,8 @@
         rows = pl.ds(row, 2 * ROWS)
         left = g[rows, :]
 
-        @pl.loop(0, D // 512)
-        def _(j):
-            cols = pl.ds(pl.multiple_of(j * 512, 512), 512)
+        for j in range(D // 1536):
+            cols = pl.ds(j * 1536, 1536)
             o[rows, cols] = jnp.dot(left, w_out[:, cols], preferred_element_type=F32).astype(BF16)
 
         o[rows, pl.ds(D, 128)] = sq[rows, :]
@@ -582,70 +611,88 @@
         arrive(k, ref)
         add(yy, hh, (0, WIDE), ref)
 
+    def in_q(cols):
+        return pl.ds(cols[0] - SPLIT, cols[1])
+
+    def in_p(cols):
+        return pl.ds(cols[0], cols[1])
+
     greet([dev_up, dev_down, dev_z, dev_sib])
     n = 1 - h
     partial(far, n, 0)
-    partial(far, h, 1)
+    partial(up, n, 2)
     joined(far, n, 0)
     send(8, at(far, n, c, p_a), pa.at[n], dev_up)
     send(9, at(far, n, c, p_b), pb.at[n], dev_down)
     send(10, at(far, n, c, part_q), zq.at[far], dev_z)
-    partial(up, n, 2)
-    joined(far, h, 1)
-    send(11, at(far, h, c, p_a), pa.at[h], dev_up)
-    send(12, at(far, h, c, p_b), pb.at[h], dev_down)
     partial(down, n, 3)
     joined(up, n, 2)
+    send(11, at(up, n, c, p_b), pf.at[0, n, :, in_p(p_b)], dev_up)
     send(13, at(up, n, c, part_q), zq.at[up], dev_z)
+    partial(far, h, 1)
+    joined(down, n, 3)
+    send(12, at(down, n, c, p_a), pf.at[1, n, :, in_p(p_a)], dev_down)
+    send(14, at(down, n, c, part_q), zq.at[down], dev_z)
     partial(up, h, 4)
-    joined(down, n, 3)
-    send(14, at(down, n, c, part_q), zq.at[down], dev_z)
+    joined(far, h, 1)
     arrive(8, pa.at[n])
     add(up, n, p_a, pa.at[n])
-    send(15, at(up, n, c, part_p), pf.at[0, n], dev_up)
+    send(15, at(up, n, c, p_a), pf.at[0, n, :, in_p(p_a)], dev_up)
     arrive(9, pb.at[n])
     add(down, n, p_b, pb.at[n])
-    send(16, at(down, n, c, part_p), pf.at[1, n], dev_down)
+    send(16, at(down, n, c, p_b), pf.at[1, n, :, in_p(p_b)], dev_down)
+    send(17, at(far, h, c, p_a), pa.at[h], dev_up)
+    send(18, at(far, h, c, p_b), pb.at[h], dev_down)
     partial(down, h, 5)
     joined(up, h, 4)
-    arrive(11, pa.at[h])
-    add(up, h, p_a, pa.at[h])
-    send(17, at(up, h, c, part_p), pf.at[0, h], dev_up)
+    send(19, at(up, h, c, p_b), pf.at[0, h, :, in_p(p_b)], dev_up)
     partial(y, n, 6)
     joined(down, h, 5)
-    arrive(12, pb.at[h])
-    add(down, h, p_b, pb.at[h])
-    send(18, at(down, h, c, part_p), pf.at[1, h], dev_down)
+    send(20, at(down, h, c, p_a), pf.at[1, h, :, in_p(p_a)], dev_down)
+    partial(y, h, 7)
     joined(y, n, 6)
-    send(19, at(y, n, c, part_q), zq.at[y], dev_z)
-    partial(y, h, 7)
+    send(21, at(y, n, c, part_q), zq.at[y], dev_z)
     arrive(10, zq.at[far])
     add(far, h, part_q, zq.at[far])
-    send(20, at(far, h, c, q_a), qa, dev_up)
-    send(21, at(far, h, c, q_b), qb, dev_down)
     joined(y, h, 7)
+    arrive(11, pf.at[0, n, :, in_p(p_b)])
+    arrive(15, pf.at[0, n, :, in_p(p_a)])
+    add(y, n, part_p, pf.at[0, n])
+    arrive(12, pf.at[1, n, :, in_p(p_a)])
+    arrive(16, pf.at[1, n, :, in_p(p_b)])
+    add(y, n, part_p, pf.at[1, n])
+    send(24, at(y, n, c, part_p), zp, dev_z)
+    arrive(17, pa.at[h])
+    add(up, h, p_a, pa.at[h])
+    send(22, at(up, h, c, p_a), pf.at[0, h, :, in_p(p_a)], dev_up)
+    arrive(18, pb.at[h])
+    add(down, h, p_b, pb.at[h])
+    send(23, at(down, h, c, p_b), pf.at[1, h, :, in_p(p_b)], dev_down)
+    send(25, at(far, h, c, q_a), qa, dev_up)
+    send(26, at(far, h, c, q_b), qb, dev_down)
     arrive(13, zq.at[up])
     add(up, h, part_q, zq.at[up])
-    arrive(20, qa)
-    add(up, h, q_a, qa)
-    send(22, at(up, h, c, part_q), qf.at[0], dev_up)
+    send(27, at(up, h, c, q_b), qf.at[0, :, in_q(q_b)], dev_up)
     arrive(14, zq.at[down])
     add(down, h, part_q, zq.at[down])
-    arrive(21, qb)
+    send(28, at(down, h, c, q_a), qf.at[1, :, in_q(q_a)], dev_down)
+    arrive(19, pf.at[0, h, :, in_p(p_b)])
+    arrive(22, pf.at[0, h, :, in_p(p_a)])
+    add(y, h, part_p, pf.at[0, h])
+    arrive(20, pf.at[1, h, :, in_p(p_a)])
+    arrive(23, pf.at[1, h, :, in_p(p_b)])
+    add(y, h, part_p, pf.at[1, h])
+    arrive(25, qa)
+    add(up, h, q_a, qa)
+    send(29, at(up, h, c, q_a), qf.at[0, :, in_q(q_a)], dev_up)
+    arrive(26, qb)
     add(down, h, q_b, qb)
-    send(23, at(down, h, c, part_q), qf.at[1], dev_down)
-    arrive(15, pf.at[0, n])
-    add(y, n, part_p, pf.at[0, n])
-    arrive(16, pf.at[1, n])
-    add(y, n, part_p, pf.at[1, n])
-    send(24, at(y, n, c, part_p), zp, dev_z)
-    arrive(17, pf.at[0, h])
-    add(y, h, part_p, pf.at[0, h])
-    arrive(18, pf.at[1, h])
-    add(y, h, part_p, pf.at[1, h])
-    arrive(19, zq.at[y])
-    arrive(22, qf.at[0])
-    arrive(23, qf.at[1])
+    send(30, at(down, h, c, q_b), qf.at[1, :, in_q(q_b)], dev_down)
+    arrive(21, zq.at[y])
+    arrive(27, qf.at[0, :, in_q(q_b)])
+    arrive(28, qf.at[1, :, in_q(q_a)])
+    arrive(29, qf.at[0, :, in_q(q_a)])
+    arrive(30, qf.at[1, :, in_q(q_b)])
     mine_q = at(y, h, c, part_q)
     mine_p = at(y, h, c, part_p)
     terms = (mine_q, zq.at[y], qf.at[0], qf.at[1])
@@ -690,8 +737,8 @@
             pltpu.VMEM((2, 2, ROWS, SPLIT), BF16),
             pltpu.VMEM((2, ROWS, wide_q), BF16),
             pltpu.VMEM((ROWS, SPLIT), BF16),
-            pltpu.SemaphoreType.DMA((25,)),
-            pltpu.SemaphoreType.DMA((25,)),
+            pltpu.SemaphoreType.DMA((31,)),
+            pltpu.SemaphoreType.DMA((31,)),
         ],
         compiler_params=pltpu.CompilerParams(
             collective_id=2, has_side_effects=True, vmem_limit_bytes=56 << 20

time: 150 us -> 138 us (0.920)
  Pallas kernels: 145 us -> 136 us
  local copies, waits for them, and re-layouts: 4.92 us -> 2.06 us
    pallas_call x1, Pallas kernels: 60.7 us -> 53.6 us  [project_reduce(): pl.pallas_call(reduce_kernel, out_shape=jax.ShapeDtypeStruct((ROWS, D), B...]
    pallas_call x1, Pallas kernels: 84.1 us -> 82.4 us  [mix(): pl.pallas_call(mixer_kernel, out_shape=(jax.ShapeDtypeStruct((SPAN, COLS)...]
    pad x1 -> x0, local copies, waits for them, and re-layouts: 1.58 us -> none  [mix(): jnp.pad(w_dt.T, ((0, 8), (0, 0)))]
where the time goes in v3:
time: 138 us
  Pallas kernels  136 us (99%)
  local copies, waits for them, and re-layouts  2.06 us (1%)
    pallas_call x1, Pallas kernels, mix(): pl.pallas_call(mixer_kernel, out_shape=(jax.ShapeDtypeStruct((SPAN, COLS)...  82.4 us
    pallas_call x1, Pallas kernels, project_reduce(): pl.pallas_call(reduce_kernel, out_shape=jax.ShapeDtypeStruct((ROWS, D), B...  53.6 us

profile of v3, /device:TPU:1, one launch (start us, length us, event | category | flops | bytes accessed | tf_op | source)
XLA Modules:
  0.0 138.1 jit_solution(10648032946211129879)
XLA Ops:
  0.0 82.4 %mix.1 = (bf16[1024,512]{1,0:T(8,128)(2,1)}, bf16[1024,128]{1,0:T(8,128)(2,1)}) custom-call(bf16[64,6144]{1,0:T(8,128)(2,1)} %tok.1, bf16[6144,512]{1,0:T(8,128)(2,1)} %wx.1, bf16[6144,512]{1,0:T(8,128)(2,1)} %wz.1, bf16[64,6144]{1,0:T(8,128)(2,1)} %bitcast.2, bf16[8,6144]{1,0:T(8,128)(2,1)} %bitcast.3, bf16[4,512]{1,0:T(4,128)(2,1)} %cx.1, ...), custom_call_target="tpu_custom_call" | custom-call | tf_op jit(solution)/shard_map/mix/pallas_call | solution.py:501
  82.4 53.6 %project_reduce.1 = bf16[64,6144]{1,0:T(8,128)(2,1)} custom-call(bf16[1024,512]{1,0:T(8,128)(2,1)} %get-tuple-element.7.g, bf16[1024,128]{1,0:T(8,128)(2,1)} %get-tuple-element.8.sq, bf16[512,6144]{1,0:T(8,128)(2,1)} %w_out.1), custom_call_target="tpu_custom_call" | custom-call | tf_op jit(solution)/shard_map/project_reduce/pallas_call | solution.py:724
  136.0 2.1 %copy.14 = bf16[64,6144]{1,0:T(8,128)(2,1)} copy(bf16[64,6144]{1,0:T(8,128)(2,1)} %project_reduce.1) | data formatting | bytes 1572864

commit v4 on v3

--- a/solution.py
+++ b/solution.py
@@ -39,10 +39,11 @@
 
 
 def mixer_kernel(
-    tok, wx, wz, wbc, wdt, cx, cbc, bias, rate, skip, gain, g_out, sq_out,
+    tok, wx, wz, wbc, wdt, cx, cbc, bias, rate, skip, gain, w_out, out,
     buf, partials, w, w_small, st_w, st_dt, xp, zs, small, bco, bcs, own, oth, maps, b_t, xc, dtx, xt,
-    ea_x, yloc, cols, rows_a, a_x, spread, aff, entry, state, states, decays, t_out, t_in,
+    yloc, cols, rows_a, a_x, spread, aff, entry, state, states, decays, t_out, t_in,
     sends, recvs, locs, sib_s, sib_r, z_s, z_r, halo_s, halo_r, line_s, line_r, t_s, t_r,
+    g, w_o, *reduce_refs,
 ):
     s, y, h, c = place()
     up, down, far = (y + 1) % 4, (y + 3) % 4, (y + 2) % 4
@@ -101,6 +102,7 @@
         pltpu.make_async_copy(wdt, st_dt, locs.at[2]),
         pltpu.make_async_copy(wx, w.at[:, pl.ds(0, COLS)], locs.at[3]),
         pltpu.make_async_copy(wz, w.at[:, pl.ds(COLS, COLS)], locs.at[4]),
+        pltpu.make_async_copy(w_out, w_o, locs.at[5]),
     ]
     st_w[...] = jnp.zeros_like(st_w)
     for copy in locals_:
@@ -114,6 +116,9 @@
     send(1, y, h, part_q, dev_up, own=True)
     send(2, y, h, part_q, dev_down, own=True)
     send(3, y, h, whole, dev_sib, own=True)
+    send(5, y, h, part_p, dev_up, own=True)
+    send(6, y, h, part_p, dev_down, own=True)
+    send(4, y, h, part_q, dev_z, own=True)
 
     units = [(y, h), (y, n), (down, h), (up, h), (down, n), (up, n), (far, h), (far, n)]
 
@@ -206,21 +211,18 @@
     locals_[4].wait()
     arrive(3, y, h, whole, sib=True)
     project(0)
-    send(5, y, h, part_p, dev_up, own=True)
-    send(6, y, h, part_p, dev_down, own=True)
-    send(4, y, h, part_q, dev_z, own=True)
     arrive(1, down, h, part_q)
-    send(7, down, h, q_a, dev_up)
     send(8, down, h, part_q, dev_z)
     send(9, down, h, part_q, dev_sib)
     arrive(2, up, h, part_q)
-    send(10, up, h, q_b, dev_down)
     send(11, up, h, part_q, dev_z)
     send(12, up, h, part_q, dev_sib)
     merge(0)
     arrive(0, y, n, part_p)
     send(13, y, n, part_p, dev_up)
     send(14, y, n, part_p, dev_down)
+    send(7, down, h, q_a, dev_up)
+    send(10, up, h, q_b, dev_down)
     send(15, y, n, part_p, dev_sib)
     arrive(4, y, n, part_q)
     send(16, y, n, part_q, dev_sib)
@@ -333,6 +335,10 @@
             acc = acc + taps[k : k + 1] * v[13 + k : 13 + k + step]
         return silu(acc).astype(BF16)
 
+    def split(exact):
+        high = exact.astype(BF16)
+        return jnp.concatenate([high, (exact - high.astype(F32)).astype(BF16)], axis=1)
+
     def conv_x(low, high):
         @pl.loop(low // step, high // step)
         def _(i):
@@ -359,19 +365,16 @@
     @pl.loop(0, 4)
     def _(b):
         rows = pl.ds(pl.multiple_of(b * BLOCK, BLOCK), BLOCK)
-        exact = cols[rows, :]
-        high = exact.astype(BF16)
-        both = jnp.concatenate([high, (exact - high.astype(F32)).astype(BF16)], axis=1)
+        both = split(cols[rows, :])
         for j in range(4):
             lanes = slice(128 * j, 128 * j + 128)
             value = xc[rows, lanes].astype(F32)
             grown = [
                 jnp.dot(both, spread[:, q * COLS + 128 * j : q * COLS + 128 * j + 128], preferred_element_type=F32)
-                for q in range(3)
+                for q in range(2)
             ]
             dtx[rows, lanes] = (value * grown[0]).astype(BF16)
             xt[rows, lanes] = (value * grown[1]).astype(BF16)
-            ea_x[rows, lanes] = grown[2]
 
     tap_o = own[tap_own, :][0:4].astype(F32)
     conv_maps(own, h, tap_o, step, SPAN)
@@ -446,6 +449,8 @@
                     + skip_x[:, lanes] * xc[here, lanes].astype(F32)
                 )
 
+    sent(*list(started))
+
     for d in (1, 2, 3):
         index = (x + 4 - d) % 4
         landed(decays.at[index], line_s.at[5 + d], line_r.at[5 + d])
@@ -470,6 +475,7 @@
         landed(t_in.at[:, lanes], t_s.at[part], t_r.at[part])
         state[:, lanes] = total + jnp.where(line == 1, jnp.exp(-passed), 0.0) * t_in[:, lanes].astype(F32)
 
+    sent(*list(started))
     gain_r = gain[...].astype(F32).reshape(1, COLS)
 
     @pl.loop(0, 4)
@@ -477,82 +483,28 @@
         rows = pl.ds(pl.multiple_of(b * BLOCK, BLOCK), BLOCK)
         ahead = sum(jnp.where(i < b, 1.0, 0.0) * a_x[i][0:1] for i in range(3))
         squares = jnp.zeros((BLOCK, 128), F32)
+        both = split(cols[rows, :])
         for j in range(4):
             lanes = slice(128 * j, 128 * j + 128)
             entering = entry[b, :, lanes] + jnp.exp(-ahead[:, lanes]) * state[:, lanes]
             far_y = jnp.dot(maps[1, rows, :], entering.astype(BF16), preferred_element_type=F32)
-            value = yloc[rows, lanes] + far_y * ea_x[rows, lanes]
+            shrink = jnp.dot(
+                both, spread[:, 2 * COLS + 128 * j : 2 * COLS + 128 * j + 128], preferred_element_type=F32
+            )
+            value = yloc[rows, lanes] + far_y * shrink
             value = value * silu(zs[rows, lanes].astype(F32))
             squares = squares + value * value
-            g_out[rows, lanes] = (value * gain_r[:, lanes]).astype(BF16)
-        sq_out[rows, :] = jnp.broadcast_to(
+            g[rows, lanes] = (value * gain_r[:, lanes]).astype(BF16)
+        buf[rows, pl.ds(D, 128)] = jnp.broadcast_to(
             jnp.sum(squares, axis=1, keepdims=True), (BLOCK, 128)
         ).astype(BF16)
 
-    for copy in started:
-        copy.wait_send()
-
-
-def mix(tokens, w_x, w_z, w_bc, w_dt, conv_x, conv_bc, dt_bias, decay_rate, skip, norm_gain):
-    anywhere = pl.BlockSpec(memory_space=pl.ANY)
-    vmem = pl.BlockSpec(memory_space=pltpu.VMEM)
-    smem = pl.BlockSpec(memory_space=pltpu.SMEM)
-    dma = pltpu.SemaphoreType.DMA
-    return pl.pallas_call(
-        mixer_kernel,
-        out_shape=(
-            jax.ShapeDtypeStruct((SPAN, COLS), BF16),
-            jax.ShapeDtypeStruct((SPAN, 128), BF16),
-        ),
-        in_specs=[anywhere] * 5 + [vmem, vmem, smem, smem, smem, vmem],
-        out_specs=(vmem, vmem),
-        scratch_shapes=[
-            pltpu.VMEM((SPAN, D), BF16),
-            pltpu.VMEM((2, 2 * ROWS, 2 * COLS + 128), F32),
-            pltpu.VMEM((D, 2 * COLS), BF16),
-            pltpu.VMEM((D, 128), BF16),
-            pltpu.VMEM((128, D), BF16),
-            pltpu.VMEM((8, D), BF16),
-            pltpu.VMEM((SPAN + 16, COLS), BF16),
-            pltpu.VMEM((SPAN, COLS), BF16),
-            pltpu.VMEM((SPAN, 128), F32),
-            pltpu.VMEM((SPAN + 16, 128), BF16),
-            pltpu.VMEM((SPAN + 16, 128), BF16),
-            pltpu.VMEM((SPAN + 32, 128), BF16),
-            pltpu.VMEM((SPAN + 32, 128), BF16),
-            pltpu.VMEM((2, SPAN, 128), BF16),
-            pltpu.VMEM((STATE, SPAN), BF16),
-            pltpu.VMEM((SPAN, COLS), BF16),
-            pltpu.VMEM((SPAN, COLS), BF16),
-            pltpu.VMEM((SPAN, COLS), BF16),
-            pltpu.VMEM((SPAN, COLS), F32),
-            pltpu.VMEM((SPAN, COLS), F32),
-            pltpu.VMEM((SPAN, 128), F32),
-            pltpu.VMEM((4, 8, BLOCK), F32),
-            pltpu.VMEM((4, 8, COLS), F32),
-            pltpu.VMEM((256, 3 * COLS), BF16),
-            pltpu.VMEM((BLOCK, BLOCK), F32),
-            pltpu.VMEM((4, STATE, COLS), F32),
-            pltpu.VMEM((STATE, COLS), F32),
-            pltpu.VMEM((4, STATE, COLS), BF16),
-            pltpu.VMEM((4, 8, COLS), F32),
-            pltpu.VMEM((STATE, COLS), BF16),
-            pltpu.VMEM((STATE, COLS), BF16),
-            dma((37,)), dma((37,)), dma((5,)), dma((9,)), dma((9,)), dma((9, 2)), dma((9, 2)),
-            dma((3,)), dma((3,)), dma((9,)), dma((9,)), dma((2,)), dma((2,)),
-        ],
-        compiler_params=pltpu.CompilerParams(
-            collective_id=1, has_side_effects=True, vmem_limit_bytes=58 << 20
-        ),
-        name="mix",
-    )(
-        tokens, w_x, w_z, w_bc.T, w_dt.T, conv_x, conv_bc, dt_bias,
-        decay_rate, skip, norm_gain,
-    )
-
-
-def reduce_kernel(
-    g, sq, w_out, out, o, sib, zq, pa, pb, qa, qb, pf, qf, zp, sends, recvs
+    locals_[5].wait()
+    reduce_stage(g, w_o, out, buf, *reduce_refs)
+
+
+def reduce_stage(
+    g, w_out, out, o, sib, zq, pa, pb, qa, qb, pf, qf, zp, sends, recvs
 ):
     s, y, h, c = place()
     up, down, far = (y + 1) % 4, (y + 3) % 4, (y + 2) % 4
@@ -603,7 +555,6 @@
             cols = pl.ds(j * 1536, 1536)
             o[rows, cols] = jnp.dot(left, w_out[:, cols], preferred_element_type=F32).astype(BF16)
 
-        o[rows, pl.ds(D, 128)] = sq[rows, :]
         send(k, at(yy, hh, 1 - c, (0, WIDE)), sib.at[chip(yy, hh)], dev_sib)
 
     def joined(yy, hh, k):
@@ -617,7 +568,6 @@
     def in_p(cols):
         return pl.ds(cols[0], cols[1])
 
-    greet([dev_up, dev_down, dev_z, dev_sib])
     n = 1 - h
     partial(far, n, 0)
     partial(up, n, 2)
@@ -718,16 +668,52 @@
         copy.wait_send()
 
 
-def project_reduce(g, sq, w_out):
+def mix(tokens, w_x, w_z, w_bc, w_dt, conv_x, conv_bc, dt_bias, decay_rate, skip, norm_gain, w_out):
+    anywhere = pl.BlockSpec(memory_space=pl.ANY)
     vmem = pl.BlockSpec(memory_space=pltpu.VMEM)
+    smem = pl.BlockSpec(memory_space=pltpu.SMEM)
     wide_q = WIDE - SPLIT
+    dma = pltpu.SemaphoreType.DMA
     return pl.pallas_call(
-        reduce_kernel,
+        mixer_kernel,
         out_shape=jax.ShapeDtypeStruct((ROWS, D), BF16),
-        in_specs=[vmem] * 3,
+        in_specs=[anywhere] * 5 + [vmem, vmem, smem, smem, smem, vmem, anywhere],
         out_specs=vmem,
         scratch_shapes=[
             pltpu.VMEM((SPAN, WIDE), BF16),
+            pltpu.VMEM((2, 2 * ROWS, 2 * COLS + 128), F32),
+            pltpu.VMEM((D, 2 * COLS), BF16),
+            pltpu.VMEM((D, 128), BF16),
+            pltpu.VMEM((128, D), BF16),
+            pltpu.VMEM((8, D), BF16),
+            pltpu.VMEM((SPAN + 16, COLS), BF16),
+            pltpu.VMEM((SPAN, COLS), BF16),
+            pltpu.VMEM((SPAN, 128), F32),
+            pltpu.VMEM((SPAN + 16, 128), BF16),
+            pltpu.VMEM((SPAN + 16, 128), BF16),
+            pltpu.VMEM((SPAN + 32, 128), BF16),
+            pltpu.VMEM((SPAN + 32, 128), BF16),
+            pltpu.VMEM((2, SPAN, 128), BF16),
+            pltpu.VMEM((STATE, SPAN), BF16),
+            pltpu.VMEM((SPAN, COLS), BF16),
+            pltpu.VMEM((SPAN, COLS), BF16),
+            pltpu.VMEM((SPAN, COLS), BF16),
+            pltpu.VMEM((SPAN, COLS), F32),
+            pltpu.VMEM((SPAN, 128), F32),
+            pltpu.VMEM((4, 8, BLOCK), F32),
+            pltpu.VMEM((4, 8, COLS), F32),
+            pltpu.VMEM((256, 3 * COLS), BF16),
+            pltpu.VMEM((BLOCK, BLOCK), F32),
+            pltpu.VMEM((4, STATE, COLS), F32),
+            pltpu.VMEM((STATE, COLS), F32),
+            pltpu.VMEM((4, STATE, COLS), BF16),
+            pltpu.VMEM((4, 8, COLS), F32),
+            pltpu.VMEM((STATE, COLS), BF16),
+            pltpu.VMEM((STATE, COLS), BF16),
+            dma((37,)), dma((37,)), dma((6,)), dma((9,)), dma((9,)), dma((9, 2)), dma((9, 2)),
+            dma((3,)), dma((3,)), dma((9,)), dma((9,)), dma((2,)), dma((2,)),
+            pltpu.VMEM((SPAN, COLS), BF16),
+            pltpu.VMEM((COLS, D), BF16),
             pltpu.VMEM((8, ROWS, WIDE), BF16),
             pltpu.VMEM((4, ROWS, wide_q), BF16),
             pltpu.VMEM((2, ROWS, HALF_P), BF16),
@@ -741,19 +727,21 @@
             pltpu.SemaphoreType.DMA((31,)),
         ],
         compiler_params=pltpu.CompilerParams(
-            collective_id=2, has_side_effects=True, vmem_limit_bytes=56 << 20
+            collective_id=1, has_side_effects=True, vmem_limit_bytes=63 << 20
         ),
-        name="project_reduce",
-    )(g, sq, w_out)
+        name="mix",
+    )(
+        tokens, w_x, w_z, w_bc.T, w_dt.T, conv_x, conv_bc, dt_bias,
+        decay_rate, skip, norm_gain, w_out,
+    )
 
 
 def on_device(
     tokens, w_x, w_z, w_bc, w_dt, conv_x, conv_bc, dt_bias, decay_rate, skip, norm_gain, w_out
 ):
-    gated, squares = mix(
-        tokens, w_x, w_z, w_bc, w_dt, conv_x, conv_bc, dt_bias, decay_rate, skip, norm_gain
+    return mix(
+        tokens, w_x, w_z, w_bc, w_dt, conv_x, conv_bc, dt_bias, decay_rate, skip, norm_gain, w_out
     )
-    return project_reduce(gated, squares, w_out)
 
 
 def solution(mesh):

time: 138 us -> 133 us (0.964)
  Pallas kernels: 136 us -> 131 us
    pallas_call x2 -> x1, Pallas kernels: 136 us -> 131 us  [mix(): pl.pallas_call(mixer_kernel, out_shape=jax.ShapeDtypeStruct((ROWS, D), BF...]
where the time goes in v4:
time: 133 us
  Pallas kernels  131 us (98%)
  local copies, waits for them, and re-layouts  2.06 us (2%)
    pallas_call x1, Pallas kernels, mix(): pl.pallas_call(mixer_kernel, out_shape=jax.ShapeDtypeStruct((ROWS, D), BF...  131 us

profile of v4, /device:TPU:1, one launch (start us, length us, event | category | flops | bytes accessed | tf_op | source)
XLA Modules:
  0.0 133.1 jit_solution(140293347004669467)
XLA Ops:
  0.0 131.0 %mix.1 = bf16[64,6144]{1,0:T(8,128)(2,1)} custom-call(bf16[64,6144]{1,0:T(8,128)(2,1)} %tok.1, bf16[6144,512]{1,0:T(8,128)(2,1)} %wx.1, bf16[6144,512]{1,0:T(8,128)(2,1)} %wz.1, bf16[64,6144]{1,0:T(8,128)(2,1)} %bitcast.2, bf16[8,6144]{1,0:T(8,128)(2,1)} %bitcast.3, bf16[4,512]{1,0:T(4,128)(2,1)} %cx.1, bf16[4,64]{1,0:T(4,128)(2,1)} %cbc.1, f32[8]{0:T(128)} %bias.1, ...), custom_call_target="tpu_custom_call" | custom-call | tf_op jit(solution)/shard_map/mix/pallas_call | solution.py:677
  131.0 2.1 %copy.14 = bf16[64,6144]{1,0:T(8,128)(2,1)} copy(bf16[64,6144]{1,0:T(8,128)(2,1)} %mix.1) | data formatting | bytes 1572864

commit v5 on v4

--- a/solution.py
+++ b/solution.py
@@ -40,8 +40,8 @@
 
 def mixer_kernel(
     tok, wx, wz, wbc, wdt, cx, cbc, bias, rate, skip, gain, w_out, out,
-    buf, partials, w, w_small, st_w, st_dt, xp, zs, small, bco, bcs, own, oth, maps, b_t, xc, dtx, xt,
-    yloc, cols, rows_a, a_x, spread, aff, entry, state, states, decays, t_out, t_in,
+    buf, partials, w, w_small, st_w, st_dt, xp, zs, small, bco, bcs, mp, direct, halo_in, maps, b_t, xc, dtx, xt,
+    yloc, cols, rows_a, a_x, aff, entry, state, states, decays, t_out, t_in,
     sends, recvs, locs, sib_s, sib_r, z_s, z_r, halo_s, halo_r, line_s, line_r, t_s, t_r,
     g, w_o, *reduce_refs,
 ):
@@ -50,12 +50,12 @@
     n = 1 - h
     line, x = s // 4, s % 4
     dev = lambda yy, hh, cc: (s, yy * 4 + hh * 2 + cc)
-    span = lambda ss, hh: (ss, y * 4 + hh * 2 + c)
+    span = lambda ss, hh, cc: (ss, y * 4 + hh * 2 + cc)
     dev_up, dev_down, dev_z, dev_sib = dev(up, h, c), dev(down, h, c), dev(y, n, c), dev(y, h, 1 - c)
     dev_zsib = dev(y, n, 1 - c)
     later, before = (s + 1) % 8, (s + 7) % 8
-    on_line = [span(line * 4 + (x + d) % 4, h) for d in (1, 2, 3)]
-    across = span((1 - line) * 4 + x, h)
+    on_line = [span(line * 4 + (x + d) % 4, h, c) for d in (1, 2, 3)]
+    across = span((1 - line) * 4 + x, h, c)
     part_p, part_q = (0, SPLIT), (SPLIT, D - SPLIT)
     p_a, p_b = (0, HALF_P), (HALF_P, SPLIT - HALF_P)
     q_a, q_b = (SPLIT, HALF_Q), (SPLIT + HALF_Q, D - SPLIT - HALF_Q)
@@ -110,7 +110,8 @@
     greet(
         [dev_up, dev_down, dev_z, dev_sib, dev_zsib, across]
         + on_line
-        + [span(later, h), span(later, n), span(before, h), span(before, n)]
+        + [span(later, hh, cc) for hh in (h, n) for cc in (c, 1 - c)]
+        + [span(before, hh, cc) for hh in (h, n) for cc in (c, 1 - c)]
     )
     send(0, y, h, part_p, dev_z, own=True)
     send(1, y, h, part_q, dev_up, own=True)
@@ -134,21 +135,20 @@
         row = unit_row(k)
         rows = pl.ds(row, 2 * ROWS)
         landed(bcs.at[rows], sib_s.at[k], sib_r.at[k])
-        own[pl.ds(pl.multiple_of(row + 16, 16), 2 * ROWS), :] = bco[rows, :] + bcs[rows, :]
+        mp[h, pl.ds(pl.multiple_of(row + 16, 16), 2 * ROWS), :] = bco[rows, :] + bcs[rows, :]
         half = pl.ds(pl.multiple_of(row + 16 + c * ROWS, 16), ROWS)
-        push(own.at[half], oth.at[half], z_s.at[k, 0], z_r.at[k, 0], dev_z)
-        push(own.at[half], oth.at[half], z_s.at[k, 1], z_r.at[k, 1], dev_zsib)
+        push(mp.at[h, half], mp.at[h, half], z_s.at[k, 0], z_r.at[k, 0], dev_z)
+        push(mp.at[h, half], mp.at[h, half], z_s.at[k, 1], z_r.at[k, 1], dev_zsib)
 
     def merged_there(k):
         row = unit_row(k, flip=True)
         for rel, core in ((0, c), (1, 1 - c)):
-            ref = oth.at[pl.ds(pl.multiple_of(row + 16 + core * ROWS, 16), ROWS)]
+            ref = mp.at[n, pl.ds(pl.multiple_of(row + 16 + core * ROWS, 16), ROWS)]
             landed(ref, z_s.at[k, rel], z_r.at[k, rel])
 
-    def project(k, cols_=(0, D), keep=None, add=None):
+    def project_small(k, cols_=(0, D), keep=None, add=None):
         row = unit_row(k)
-        rows = pl.ds(row, 2 * ROWS)
-        inner = pl.ds(cols_[0], cols_[1])
+        rows, inner = pl.ds(row, 2 * ROWS), pl.ds(cols_[0], cols_[1])
         part = jnp.dot(buf[rows, inner], w_small[inner, :], preferred_element_type=F32)
         if add is not None:
             part = part + partials[add, :, 2 * COLS : 2 * COLS + 128]
@@ -158,18 +158,27 @@
             small[rows, :] = part
             lane = lax.broadcasted_iota(jnp.int32, part.shape, 1)
             bco[rows, :] = jnp.where(lane // 64 == c, part, 0.0).astype(BF16)
-            share(k, row, 2 * ROWS)
-        past = pl.ds(pl.multiple_of(row + 16, 16), 2 * ROWS)
-        for out, base, target in ((xp, 0, past), (zs, COLS, rows)):
-
-            lanes = pl.ds(base, COLS)
-            part = jnp.dot(buf[rows, inner], w[inner, lanes], preferred_element_type=F32)
-            if add is not None:
-                part = part + partials[add, :, lanes]
-            if keep is not None:
-                partials[keep, :, lanes] = part
-            else:
-                out[target, :] = part.astype(BF16)
+
+    def project_wide(k, which, cols_=(0, D), keep=None, add=None):
+        row = unit_row(k)
+        rows, inner = pl.ds(row, 2 * ROWS), pl.ds(cols_[0], cols_[1])
+        lanes = pl.ds(which * COLS, COLS)
+        part = jnp.dot(buf[rows, inner], w[inner, lanes], preferred_element_type=F32)
+        if add is not None:
+            part = part + partials[add, :, lanes]
+        if keep is not None:
+            partials[keep, :, lanes] = part
+        elif which == 0:
+            xp[pl.ds(pl.multiple_of(row + 16, 16), 2 * ROWS), :] = part.astype(BF16)
+        else:
+            zs[rows, :] = part.astype(BF16)
+
+    def project(k, cols_=(0, D), keep=None, add=None):
+        project_small(k, cols_, keep, add)
+        if keep is None:
+            share(k, unit_row(k), 2 * ROWS)
+        project_wide(k, 0, cols_, keep, add)
+        project_wide(k, 1, cols_, keep, add)
 
     tap_rows = pl.ds(SPAN, 16)
     tap_own = pl.ds(SPAN + 16, 16)
@@ -180,11 +189,6 @@
     ).astype(BF16)
     share(8, SPAN, 16)
 
-    lane_i = lax.broadcasted_iota(jnp.int32, (256, 3 * COLS), 1)
-    deep_i = lax.broadcasted_iota(jnp.int32, (256, 3 * COLS), 0)
-    spread[...] = jnp.where(
-        deep_i % 128 == (lane_i // COLS + 1) * 8 + lane_i % COLS // HEAD_DIM, 1.0, 0.0
-    ).astype(BF16)
     head_lane = lax.broadcasted_iota(jnp.int32, (8, COLS), 1) // HEAD_DIM
     head_sub = lax.broadcasted_iota(jnp.int32, (8, COLS), 0)
     skip_x = sum(jnp.where(head_lane[0:1] == i, skip[i], 0.0) for i in range(8))
@@ -192,119 +196,10 @@
     bias_r = sum(jnp.where(sub256 == i, bias[i], 0.0) for i in range(8))
     rate_r = sum(jnp.where(sub256 == i, rate[i], 0.0) for i in range(8))
 
-    locals_[1].wait()
-    locals_[2].wait()
-    st_w[pl.ds(pl.multiple_of((1 - c) * 64, 64), 16), :] = (
-        jnp.concatenate([st_dt[...].astype(F32), jnp.zeros((8, D), F32)], axis=0).astype(BF16)
-    )
-
-    @pl.loop(0, D // 128)
-    def _(j):
-        part = pl.ds(pl.multiple_of(j * 128, 128), 128)
-        w_small[part, :] = st_w[:, part].T
-
-    landed(bcs.at[tap_rows], sib_s.at[8], sib_r.at[8])
-    own[tap_own, :] = bco[tap_rows, :] + bcs[tap_rows, :]
-    push(own.at[tap_own], oth.at[tap_own], z_s.at[8, 0], z_r.at[8, 0], dev_z)
-    locals_[0].wait()
-    locals_[3].wait()
-    locals_[4].wait()
-    arrive(3, y, h, whole, sib=True)
-    project(0)
-    arrive(1, down, h, part_q)
-    send(8, down, h, part_q, dev_z)
-    send(9, down, h, part_q, dev_sib)
-    arrive(2, up, h, part_q)
-    send(11, up, h, part_q, dev_z)
-    send(12, up, h, part_q, dev_sib)
-    merge(0)
-    arrive(0, y, n, part_p)
-    send(13, y, n, part_p, dev_up)
-    send(14, y, n, part_p, dev_down)
-    send(7, down, h, q_a, dev_up)
-    send(10, up, h, q_b, dev_down)
-    send(15, y, n, part_p, dev_sib)
-    arrive(4, y, n, part_q)
-    send(16, y, n, part_q, dev_sib)
-    arrive(5, down, h, part_p)
-    send(21, down, h, p_a, dev_up)
-    send(22, down, h, part_p, dev_sib)
-    arrive(6, up, h, part_p)
-    send(23, up, h, p_b, dev_down)
-    send(24, up, h, part_p, dev_sib)
-    arrive(15, y, n, part_p, sib=True)
-    arrive(16, y, n, part_q, sib=True)
-    project(1)
-    arrive(7, far, h, q_a)
-    send(17, far, h, q_a, dev_z)
-    send(18, far, h, q_a, dev_sib)
-    arrive(10, far, h, q_b)
-    send(19, far, h, q_b, dev_z)
-    send(20, far, h, q_b, dev_sib)
-    arrive(9, down, h, part_q, sib=True)
-    arrive(22, down, h, part_p, sib=True)
-    project(2)
-    merge(1)
-    arrive(8, down, n, part_q)
-    send(25, down, n, part_q, dev_sib)
-    arrive(12, up, h, part_q, sib=True)
-    arrive(24, up, h, part_p, sib=True)
-    project(3)
-    arrive(18, far, h, q_a, sib=True)
-    arrive(20, far, h, q_b, sib=True)
-    project(6, part_q, keep=0)
-    merge(2)
-    arrive(13, down, n, part_p)
-    send(27, down, n, p_a, dev_up)
-    send(28, down, n, part_p, dev_sib)
-    arrive(14, up, n, part_p)
-    send(29, up, n, p_b, dev_down)
-    send(30, up, n, part_p, dev_sib)
-    merge(3)
-    arrive(11, up, n, part_q)
-    send(26, up, n, part_q, dev_sib)
-    arrive(21, far, h, p_a)
-    send(33, far, h, p_a, dev_sib)
-    arrive(23, far, h, p_b)
-    send(34, far, h, p_b, dev_sib)
-    arrive(25, down, n, part_q, sib=True)
-    arrive(28, down, n, part_p, sib=True)
-    project(4)
-    arrive(26, up, n, part_q, sib=True)
-    arrive(30, up, n, part_p, sib=True)
-    project(5)
-    merge(4)
-    arrive(33, far, h, p_a, sib=True)
-    arrive(34, far, h, p_b, sib=True)
-    project(6, part_p, add=0)
-    merge(5)
-    arrive(17, far, n, q_a)
-    send(31, far, n, q_a, dev_sib)
-    arrive(19, far, n, q_b)
-    send(32, far, n, q_b, dev_sib)
-    arrive(27, far, n, p_a)
-    send(35, far, n, p_a, dev_sib)
-    arrive(29, far, n, p_b)
-    send(36, far, n, p_b, dev_sib)
-    arrive(31, far, n, q_a, sib=True)
-    arrive(32, far, n, q_b, sib=True)
-    project(7, part_q, keep=1)
-    merge(6)
-    arrive(35, far, n, p_a, sib=True)
-    arrive(36, far, n, p_b, sib=True)
-    project(7, part_p, add=1)
-    merge(7)
-
-    last, first = pl.ds(SPAN, 16), pl.ds(0, 16)
-    push(xp.at[last], xp.at[first], halo_s.at[0], halo_r.at[0], span(later, h))
-    push(own.at[last], own.at[first], halo_s.at[1], halo_r.at[1], span(later, h))
-    push(own.at[last], oth.at[first], halo_s.at[2], halo_r.at[2], span(later, n))
-
-    causal = lax.broadcasted_iota(jnp.int32, (BLOCK, BLOCK), 0)
-    summing = jnp.where(causal <= lax.broadcasted_iota(jnp.int32, (BLOCK, BLOCK), 1), 1.0, 0.0)
-
-    @pl.loop(0, 4)
-    def _(b):
+    deep = lax.broadcasted_iota(jnp.int32, (BLOCK, BLOCK), 0)
+    summing = jnp.where(deep <= lax.broadcasted_iota(jnp.int32, (BLOCK, BLOCK), 1), 1.0, 0.0)
+
+    def steps(b):
         rows = pl.ds(pl.multiple_of(b * BLOCK, BLOCK), BLOCK)
         turned = small[rows, :].T
         raw = jnp.where(c == 0, turned[64:72], turned[0:8]) + bias_r
@@ -321,78 +216,195 @@
         total = jnp.sum(jnp.where(head_sub == head_lane, end, 0.0), axis=0, keepdims=True)
         a_x[b] = jnp.broadcast_to(total, (8, COLS))
 
+    def convolve(src, row, lanes, taps, count):
+        v = src[pl.ds(row, count + 16), lanes].astype(F32)
+        acc = taps[0:1] * v[13 : 13 + count]
+        for k in (1, 2, 3):
+            acc = acc + taps[k : k + 1] * v[13 + k : 13 + k + count]
+        return silu(acc).astype(BF16)
+
+    def over_lanes(column, q, j):
+        lane = lax.broadcasted_iota(jnp.int32, (column.shape[0], 128), 1)
+        low = q * 8 + 2 * j
+        return jnp.where(lane < HEAD_DIM, column[:, low : low + 1], column[:, low + 1 : low + 2])
+
+    taps_x = cx[...].astype(F32)
+    head_rows, body_rows = 16, 80
+
+    def conv_x(row, count):
+        rows = pl.ds(row, count)
+        column = cols[rows, :]
+        for j in range(4):
+            lanes = slice(128 * j, 128 * j + 128)
+            done = convolve(xp, row, lanes, taps_x[:, lanes], count)
+            xc[rows, lanes] = done
+            value = done.astype(F32)
+            dtx[rows, lanes] = (value * over_lanes(column, 1, j)).astype(BF16)
+            xt[rows, lanes] = (value * over_lanes(column, 2, j)).astype(BF16)
+
+    def conv_map(index, row, count):
+        taps = mp[index, tap_own, :][0:4].astype(F32)
+        maps[index, pl.ds(row, count), :] = convolve(mp.at[index], row, slice(0, 128), taps, count)
+
+    def bodies(b, one):
+        @pl.loop(0, 3)
+        def _(i):
+            one(pl.multiple_of(b * BLOCK + 16 + i * body_rows, 16), body_rows)
+
+    def heads(one, low=0, high=4):
+        @pl.loop(low, high)
+        def _(b):
+            one(pl.multiple_of(b * BLOCK, BLOCK), head_rows)
+
+    locals_[1].wait()
+    locals_[2].wait()
+    st_w[pl.ds(pl.multiple_of((1 - c) * 64, 64), 16), :] = (
+        jnp.concatenate([st_dt[...].astype(F32), jnp.zeros((8, D), F32)], axis=0).astype(BF16)
+    )
+
+    @pl.loop(0, D // 128)
+    def _(j):
+        part = pl.ds(pl.multiple_of(j * 128, 128), 128)
+        w_small[part, :] = st_w[:, part].T
+
+    landed(bcs.at[tap_rows], sib_s.at[8], sib_r.at[8])
+    mp[h, tap_own, :] = bco[tap_rows, :] + bcs[tap_rows, :]
+    push(mp.at[h, tap_own], mp.at[h, tap_own], z_s.at[8, 0], z_r.at[8, 0], dev_z)
+    locals_[0].wait()
+    locals_[3].wait()
+    locals_[4].wait()
+    arrive(3, y, h, whole, sib=True)
+    project(0)
+    arrive(1, down, h, part_q)
+    send(8, down, h, part_q, dev_z)
+    send(9, down, h, part_q, dev_sib)
+    arrive(2, up, h, part_q)
+    send(11, up, h, part_q, dev_z)
+    send(12, up, h, part_q, dev_sib)
+    arrive(0, y, n, part_p)
+    send(13, y, n, part_p, dev_up)
+    send(14, y, n, part_p, dev_down)
+    send(7, down, h, q_a, dev_up)
+    send(10, up, h, q_b, dev_down)
+    send(15, y, n, part_p, dev_sib)
+    merge(0)
+    arrive(9, down, h, part_q, sib=True)
+    project(2, part_q, keep=2)
+    arrive(12, up, h, part_q, sib=True)
+    project(3, part_q, keep=3)
+    arrive(15, y, n, part_p, sib=True)
+    project(1, part_p, keep=0)
+    arrive(4, y, n, part_q)
+    send(16, y, n, part_q, dev_sib)
+    arrive(5, down, h, part_p)
+    send(21, down, h, p_a, dev_up)
+    send(22, down, h, part_p, dev_sib)
+    arrive(6, up, h, part_p)
+    send(23, up, h, p_b, dev_down)
+    send(24, up, h, part_p, dev_sib)
+    arrive(16, y, n, part_q, sib=True)
+    project(1, part_q, add=0)
+    arrive(22, down, h, part_p, sib=True)
+    project(2, part_p, add=2)
+    arrive(24, up, h, part_p, sib=True)
+    project(3, part_p, add=3)
+    merge(1)
+    steps(y)
+    bodies(y, conv_x)
+    merge(2)
+    merge(3)
+    arrive(8, down, n, part_q)
+    send(25, down, n, part_q, dev_sib)
+    arrive(13, down, n, part_p)
+    send(27, down, n, p_a, dev_up)
+    send(28, down, n, part_p, dev_sib)
+    arrive(14, up, n, part_p)
+    send(29, up, n, p_b, dev_down)
+    send(30, up, n, part_p, dev_sib)
+    arrive(25, down, n, part_q, sib=True)
+    arrive(28, down, n, part_p, sib=True)
+    project(4)
+    arrive(7, far, h, q_a)
+    send(17, far, h, q_a, dev_z)
+    send(18, far, h, q_a, dev_sib)
+    arrive(10, far, h, q_b)
+    send(19, far, h, q_b, dev_z)
+    send(20, far, h, q_b, dev_sib)
+    arrive(30, up, n, part_p, sib=True)
+    project(5, part_p, keep=0)
+    arrive(11, up, n, part_q)
+    send(26, up, n, part_q, dev_sib)
+    merge(4)
+    arrive(18, far, h, q_a, sib=True)
+    arrive(20, far, h, q_b, sib=True)
+    project(6, part_q, keep=1)
+    arrive(21, far, h, p_a)
+    send(33, far, h, p_a, dev_sib)
+    arrive(23, far, h, p_b)
+    send(34, far, h, p_b, dev_sib)
+    arrive(26, up, n, part_q, sib=True)
+    project(5, part_q, add=0)
+    steps(down)
+    bodies(down, conv_x)
+    merge(5)
+    arrive(17, far, n, q_a)
+    send(31, far, n, q_a, dev_sib)
+    arrive(33, far, h, p_a, sib=True)
+    arrive(34, far, h, p_b, sib=True)
+    project(6, part_p, add=1)
+    arrive(19, far, n, q_b)
+    send(32, far, n, q_b, dev_sib)
+    steps(up)
+    bodies(up, conv_x)
+    merge(6)
+    arrive(31, far, n, q_a, sib=True)
+    arrive(32, far, n, q_b, sib=True)
+    project(7, part_q, keep=1)
+    arrive(27, far, n, p_a)
+    send(35, far, n, p_a, dev_sib)
+    arrive(29, far, n, p_b)
+    send(36, far, n, p_b, dev_sib)
+    landed(mp.at[n, tap_own], z_s.at[8, 0], z_r.at[8, 0])
+    for k in range(6):
+        merged_there(k)
+    for b in (y, up, down):
+        bodies(b, lambda row, count: conv_map(0, row, count))
+    arrive(35, far, n, p_a, sib=True)
+    arrive(36, far, n, p_b, sib=True)
+
+    project_small(7, part_p, add=1)
+    unit = pl.ds(unit_row(7), 2 * ROWS)
+    push(bco.at[unit], bcs.at[unit], sib_s.at[7], sib_r.at[7], dev_sib)
+    push(bco.at[unit], direct.at[0], z_s.at[7, 0], z_r.at[7, 0], dev_z)
+    push(bco.at[unit], direct.at[1], z_s.at[7, 1], z_r.at[7, 1], dev_zsib)
+    ending = pl.ds(SPAN - 16, 16)
+    for k, (hh, cc) in enumerate(((h, c), (h, 1 - c), (n, c), (n, 1 - c))):
+        push(bco.at[ending], halo_in.at[k], halo_s.at[1 + k], halo_r.at[1 + k], span(later, hh, cc))
+    project_wide(7, 0, part_p, add=1)
+    last, first = pl.ds(SPAN, 16), pl.ds(0, 16)
+    push(xp.at[last], xp.at[first], halo_s.at[0], halo_r.at[0], span(later, h, c))
+    steps(far)
     decays[x] = a_x[0] + a_x[1] + a_x[2] + a_x[3]
     for d in (1, 2, 3):
-        push(decays.at[x], decays.at[x], line_s.at[5 + d], line_r.at[5 + d], on_line[d - 1])
-
-    taps_x = cx[...].astype(F32)
-    step = 64
-
-    def convolve(src, row, lanes, taps):
-        v = src[pl.ds(row, step + 16), lanes].astype(F32)
-        acc = taps[0:1] * v[13 : 13 + step]
-        for k in (1, 2, 3):
-            acc = acc + taps[k : k + 1] * v[13 + k : 13 + k + step]
-        return silu(acc).astype(BF16)
-
-    def split(exact):
-        high = exact.astype(BF16)
-        return jnp.concatenate([high, (exact - high.astype(F32)).astype(BF16)], axis=1)
-
-    def conv_x(low, high):
-        @pl.loop(low // step, high // step)
-        def _(i):
-            row = pl.multiple_of(i * step, step)
-            for j in range(4):
-                lanes = slice(128 * j, 128 * j + 128)
-                xc[pl.ds(row, step), lanes] = convolve(xp, row, lanes, taps_x[:, lanes])
-
-    def conv_maps(src, index, taps, low, high):
-        @pl.loop(low // step, high // step)
-        def _(i):
-            row = pl.multiple_of(i * step, step)
-            maps[index, pl.ds(row, step), :] = convolve(src, row, slice(0, 128), taps)
-
-    conv_x(step, SPAN)
+        push(decays.at[x], decays.at[x], line_s.at[11 + d], line_r.at[11 + d], on_line[d - 1])
+    bodies(far, conv_x)
+    heads(conv_x, 1, 4)
+    merged_there(6)
+    landed(bcs.at[unit], sib_s.at[7], sib_r.at[7])
+    mp[h, pl.ds(pl.multiple_of(unit_row(7) + 16, 16), 2 * ROWS), :] = bco[unit, :] + bcs[unit, :]
+    landed(direct.at[0], z_s.at[7, 0], z_r.at[7, 0])
+    landed(direct.at[1], z_s.at[7, 1], z_r.at[7, 1])
+    mp[n, pl.ds(pl.multiple_of(unit_row(7, flip=True) + 16, 16), 2 * ROWS), :] = direct[0] + direct[1]
     landed(xp.at[first], halo_s.at[0], halo_r.at[0])
-
-    @pl.when(s == 0)
-    def _():
-        xp[first, :] = jnp.zeros((16, COLS), BF16)
-
-    conv_x(0, step)
-
-    @pl.loop(0, 4)
-    def _(b):
-        rows = pl.ds(pl.multiple_of(b * BLOCK, BLOCK), BLOCK)
-        both = split(cols[rows, :])
-        for j in range(4):
-            lanes = slice(128 * j, 128 * j + 128)
-            value = xc[rows, lanes].astype(F32)
-            grown = [
-                jnp.dot(both, spread[:, q * COLS + 128 * j : q * COLS + 128 * j + 128], preferred_element_type=F32)
-                for q in range(2)
-            ]
-            dtx[rows, lanes] = (value * grown[0]).astype(BF16)
-            xt[rows, lanes] = (value * grown[1]).astype(BF16)
-
-    tap_o = own[tap_own, :][0:4].astype(F32)
-    conv_maps(own, h, tap_o, step, SPAN)
-    landed(oth.at[tap_own], z_s.at[8, 0], z_r.at[8, 0])
-    for k in range(8):
-        merged_there(k)
-    tap_t = oth[tap_own, :][0:4].astype(F32)
-    conv_maps(oth, n, tap_t, step, SPAN)
-    landed(own.at[first], halo_s.at[1], halo_r.at[1])
-    landed(oth.at[first], halo_s.at[2], halo_r.at[2])
-
-    @pl.when(s == 0)
-    def _():
-        own[first, :] = jnp.zeros((16, 128), BF16)
-        oth[first, :] = jnp.zeros((16, 128), BF16)
-
-    conv_maps(own, h, tap_o, 0, step)
-    conv_maps(oth, n, tap_t, 0, step)
+    for k in range(4):
+        landed(halo_in.at[k], halo_s.at[1 + k], halo_r.at[1 + k])
+    begun = s > 0
+    xp[first, :] = jnp.where(begun, xp[first, :].astype(F32), 0.0).astype(BF16)
+    mp[h, first, :] = jnp.where(begun, halo_in[0].astype(F32) + halo_in[1].astype(F32), 0.0).astype(BF16)
+    mp[n, first, :] = jnp.where(begun, halo_in[2].astype(F32) + halo_in[3].astype(F32), 0.0).astype(BF16)
+    bodies(far, lambda row, count: conv_map(0, row, count))
+    heads(conv_x, 0, 1)
+    heads(lambda row, count: conv_map(0, row, count))
 
     state[...] = jnp.zeros_like(state)
 
@@ -406,13 +418,18 @@
             turned, xt[rows, :], preferred_element_type=F32
         )
 
+    earlier = list(started)
     states[x] = state[...].astype(BF16)
-    halves = [pl.ds(0, COLS // 2), pl.ds(COLS // 2, COLS // 2)]
-    for part, lanes in enumerate(halves):
+    quarters = [pl.ds(128 * q, 128) for q in range(4)]
+    for part, lanes in enumerate(quarters):
         for d in (1, 3, 2):
             ref = states.at[x, :, lanes]
             push(ref, ref, line_s.at[part * 3 + d - 1], line_r.at[part * 3 + d - 1], on_line[d - 1])
 
+    project_wide(7, 1, part_p, add=1)
+    for b in (y, up, down, far):
+        bodies(b, lambda row, count: conv_map(1, row, count))
+    heads(lambda row, count: conv_map(1, row, count))
     pair_lane = lax.broadcasted_iota(jnp.int32, (128, 128), 1)
 
     @pl.loop(0, 4)
@@ -449,24 +466,23 @@
                     + skip_x[:, lanes] * xc[here, lanes].astype(F32)
                 )
 
-    sent(*list(started))
-
     for d in (1, 2, 3):
         index = (x + 4 - d) % 4
-        landed(decays.at[index], line_s.at[5 + d], line_r.at[5 + d])
-    for part, lanes in enumerate(halves):
+        landed(decays.at[index], line_s.at[11 + d], line_r.at[11 + d])
+    for part, lanes in enumerate(quarters):
         for d in (1, 3, 2):
             landed(
                 states.at[(x + 4 - d) % 4, :, lanes], line_s.at[part * 3 + d - 1], line_r.at[part * 3 + d - 1]
             )
-        total = jnp.zeros((STATE, COLS // 2), F32)
+        total = jnp.zeros((STATE, 128), F32)
         for j in range(4):
             total = jnp.exp(-decays[j, 0:1, lanes]) * total + states[j, :, lanes].astype(F32)
         t_out[:, lanes] = total.astype(BF16)
         push(t_out.at[:, lanes], t_in.at[:, lanes], t_s.at[part], t_r.at[part], across)
-    for part, lanes in enumerate(halves):
-        total = jnp.zeros((STATE, COLS // 2), F32)
-        passed = jnp.zeros((1, COLS // 2), F32)
+    sent(*earlier)
+    for part, lanes in enumerate(quarters):
+        total = jnp.zeros((STATE, 128), F32)
+        passed = jnp.zeros((1, 128), F32)
         for j in range(4):
             taken = jnp.where(j < x, 1.0, 0.0)
             through = jnp.where(j < x, jnp.exp(-decays[j, 0:1, lanes]), 1.0)
@@ -478,33 +494,29 @@
     sent(*list(started))
     gain_r = gain[...].astype(F32).reshape(1, COLS)
 
-    @pl.loop(0, 4)
-    def _(b):
-        rows = pl.ds(pl.multiple_of(b * BLOCK, BLOCK), BLOCK)
+    def gate(b, half):
+        rows = pl.ds(pl.multiple_of(b * BLOCK + half * 128, 128), 128)
         ahead = sum(jnp.where(i < b, 1.0, 0.0) * a_x[i][0:1] for i in range(3))
-        squares = jnp.zeros((BLOCK, 128), F32)
-        both = split(cols[rows, :])
+        squares = jnp.zeros((128, 128), F32)
+        column = cols[rows, :]
         for j in range(4):
             lanes = slice(128 * j, 128 * j + 128)
             entering = entry[b, :, lanes] + jnp.exp(-ahead[:, lanes]) * state[:, lanes]
             far_y = jnp.dot(maps[1, rows, :], entering.astype(BF16), preferred_element_type=F32)
-            shrink = jnp.dot(
-                both, spread[:, 2 * COLS + 128 * j : 2 * COLS + 128 * j + 128], preferred_element_type=F32
-            )
-            value = yloc[rows, lanes] + far_y * shrink
+            value = yloc[rows, lanes] + far_y * over_lanes(column, 3, j)
             value = value * silu(zs[rows, lanes].astype(F32))
             squares = squares + value * value
             g[rows, lanes] = (value * gain_r[:, lanes]).astype(BF16)
         buf[rows, pl.ds(D, 128)] = jnp.broadcast_to(
-            jnp.sum(squares, axis=1, keepdims=True), (BLOCK, 128)
+            jnp.sum(squares, axis=1, keepdims=True), (128, 128)
         ).astype(BF16)
 
     locals_[5].wait()
-    reduce_stage(g, w_o, out, buf, *reduce_refs)
+    reduce_stage(gate, g, w_o, out, buf, *reduce_refs)
 
 
 def reduce_stage(
-    g, w_out, out, o, sib, zq, pa, pb, qa, qb, pf, qf, zp, sends, recvs
+    gate, g, w_out, out, o, sib, zq, pa, pb, qa, qb, pf, qf, zp, sends, recvs
 ):
     s, y, h, c = place()
     up, down, far = (y + 1) % 4, (y + 3) % 4, (y + 2) % 4
@@ -546,21 +558,22 @@
     def chip(yy, hh):
         return yy * 2 + hh
 
-    def partial(yy, hh, k):
+    def partial(yy, hh, k, cols=(0, WIDE)):
         row = pl.multiple_of((yy * 4 + hh * 2) * ROWS, 2 * ROWS)
         rows = pl.ds(row, 2 * ROWS)
         left = g[rows, :]
-
-        for j in range(D // 1536):
-            cols = pl.ds(j * 1536, 1536)
-            o[rows, cols] = jnp.dot(left, w_out[:, cols], preferred_element_type=F32).astype(BF16)
-
-        send(k, at(yy, hh, 1 - c, (0, WIDE)), sib.at[chip(yy, hh)], dev_sib)
-
-    def joined(yy, hh, k):
-        ref = sib.at[chip(yy, hh)]
+        low, high = cols[0], min(D, cols[0] + cols[1])
+        pieces = -(-(high - low) // 1792)
+        width = (high - low) // pieces
+        for j in range(pieces):
+            part = pl.ds(low + j * width, width)
+            o[rows, part] = jnp.dot(left, w_out[:, part], preferred_element_type=F32).astype(BF16)
+        send(k, at(yy, hh, 1 - c, cols), sib.at[chip(yy, hh), :, pl.ds(cols[0], cols[1])], dev_sib)
+
+    def joined(yy, hh, k, cols=(0, WIDE)):
+        ref = sib.at[chip(yy, hh), :, pl.ds(cols[0], cols[1])]
         arrive(k, ref)
-        add(yy, hh, (0, WIDE), ref)
+        add(yy, hh, cols, ref)
 
     def in_q(cols):
         return pl.ds(cols[0] - SPLIT, cols[1])
@@ -569,20 +582,29 @@
         return pl.ds(cols[0], cols[1])
 
     n = 1 - h
-    partial(far, n, 0)
+    gate(far, n)
+    partial(far, n, 0, p_a)
+    partial(far, n, 32, p_b)
+    partial(far, n, 31, part_q)
+    gate(up, n)
+    joined(far, n, 0, p_a)
+    send(8, at(far, n, c, p_a), pa.at[n], dev_up)
+    joined(far, n, 32, p_b)
+    send(9, at(far, n, c, p_b), pb.at[n], dev_down)
     partial(up, n, 2)
-    joined(far, n, 0)
-    send(8, at(far, n, c, p_a), pa.at[n], dev_up)
-    send(9, at(far, n, c, p_b), pb.at[n], dev_down)
+    gate(down, n)
+    joined(far, n, 31, part_q)
     send(10, at(far, n, c, part_q), zq.at[far], dev_z)
     partial(down, n, 3)
     joined(up, n, 2)
     send(11, at(up, n, c, p_b), pf.at[0, n, :, in_p(p_b)], dev_up)
     send(13, at(up, n, c, part_q), zq.at[up], dev_z)
+    gate(far, h)
     partial(far, h, 1)
     joined(down, n, 3)
     send(12, at(down, n, c, p_a), pf.at[1, n, :, in_p(p_a)], dev_down)
     send(14, at(down, n, c, part_q), zq.at[down], dev_z)
+    gate(up, h)
     partial(up, h, 4)
     joined(far, h, 1)
     arrive(8, pa.at[n])
@@ -593,12 +615,15 @@
     send(16, at(down, n, c, p_b), pf.at[1, n, :, in_p(p_b)], dev_down)
     send(17, at(far, h, c, p_a), pa.at[h], dev_up)
     send(18, at(far, h, c, p_b), pb.at[h], dev_down)
+    gate(down, h)
     partial(down, h, 5)
     joined(up, h, 4)
     send(19, at(up, h, c, p_b), pf.at[0, h, :, in_p(p_b)], dev_up)
+    gate(y, n)
     partial(y, n, 6)
     joined(down, h, 5)
     send(20, at(down, h, c, p_a), pf.at[1, h, :, in_p(p_a)], dev_down)
+    gate(y, h)
     partial(y, h, 7)
     joined(y, n, 6)
     send(21, at(y, n, c, part_q), zq.at[y], dev_z)
@@ -681,7 +706,7 @@
         out_specs=vmem,
         scratch_shapes=[
             pltpu.VMEM((SPAN, WIDE), BF16),
-            pltpu.VMEM((2, 2 * ROWS, 2 * COLS + 128), F32),
+            pltpu.VMEM((4, 2 * ROWS, 2 * COLS + 128), F32),
             pltpu.VMEM((D, 2 * COLS), BF16),
             pltpu.VMEM((D, 128), BF16),
             pltpu.VMEM((128, D), BF16),
@@ -691,8 +716,9 @@
             pltpu.VMEM((SPAN, 128), F32),
             pltpu.VMEM((SPAN + 16, 128), BF16),
             pltpu.VMEM((SPAN + 16, 128), BF16),
-            pltpu.VMEM((SPAN + 32, 128), BF16),
-            pltpu.VMEM((SPAN + 32, 128), BF16),
+            pltpu.VMEM((2, SPAN + 32, 128), BF16),
+            pltpu.VMEM((2, 2 * ROWS, 128), BF16),
+            pltpu.VMEM((4, 16, 128), BF16),
             pltpu.VMEM((2, SPAN, 128), BF16),
             pltpu.VMEM((STATE, SPAN), BF16),
             pltpu.VMEM((SPAN, COLS), BF16),
@@ -702,7 +728,6 @@
             pltpu.VMEM((SPAN, 128), F32),
             pltpu.VMEM((4, 8, BLOCK), F32),
             pltpu.VMEM((4, 8, COLS), F32),
-            pltpu.VMEM((256, 3 * COLS), BF16),
             pltpu.VMEM((BLOCK, BLOCK), F32),
             pltpu.VMEM((4, STATE, COLS), F32),
             pltpu.VMEM((STATE, COLS), F32),
@@ -711,7 +736,7 @@
             pltpu.VMEM((STATE, COLS), BF16),
             pltpu.VMEM((STATE, COLS), BF16),
             dma((37,)), dma((37,)), dma((6,)), dma((9,)), dma((9,)), dma((9, 2)), dma((9, 2)),
-            dma((3,)), dma((3,)), dma((9,)), dma((9,)), dma((2,)), dma((2,)),
+            dma((5,)), dma((5,)), dma((15,)), dma((15,)), dma((4,)), dma((4,)),
             pltpu.VMEM((SPAN, COLS), BF16),
             pltpu.VMEM((COLS, D), BF16),
             pltpu.VMEM((8, ROWS, WIDE), BF16),
@@ -723,8 +748,8 @@
             pltpu.VMEM((2, 2, ROWS, SPLIT), BF16),
             pltpu.VMEM((2, ROWS, wide_q), BF16),
             pltpu.VMEM((ROWS, SPLIT), BF16),
-            pltpu.SemaphoreType.DMA((31,)),
-            pltpu.SemaphoreType.DMA((31,)),
+            pltpu.SemaphoreType.DMA((33,)),
+            pltpu.SemaphoreType.DMA((33,)),
         ],
         compiler_params=pltpu.CompilerParams(
             collective_id=1, has_side_effects=True, vmem_limit_bytes=63 << 20

time: 133 us -> 126 us (0.947)
  Pallas kernels: 131 us -> 124 us
    pallas_call x1, Pallas kernels: 131 us -> 124 us  [mix(): pl.pallas_call(mixer_kernel, out_shape=jax.ShapeDtypeStruct((ROWS, D), BF...]
where the time goes in v5:
time: 126 us
  Pallas kernels  124 us (98%)
  local copies, waits for them, and re-layouts  2.06 us (2%)
    pallas_call x1, Pallas kernels, mix(): pl.pallas_call(mixer_kernel, out_shape=jax.ShapeDtypeStruct((ROWS, D), BF...  124 us

profile of v5, /device:TPU:1, one launch (start us, length us, event | category | flops | bytes accessed | tf_op | source)
XLA Modules:
  0.0 125.7 jit_solution(123700548286180185)
XLA Ops:
  0.0 123.7 %mix.1 = bf16[64,6144]{1,0:T(8,128)(2,1)} custom-call(bf16[64,6144]{1,0:T(8,128)(2,1)} %tok.1, bf16[6144,512]{1,0:T(8,128)(2,1)} %wx.1, bf16[6144,512]{1,0:T(8,128)(2,1)} %wz.1, bf16[64,6144]{1,0:T(8,128)(2,1)} %bitcast.2, bf16[8,6144]{1,0:T(8,128)(2,1)} %bitcast.3, bf16[4,512]{1,0:T(4,128)(2,1)} %cx.1, bf16[4,64]{1,0:T(4,128)(2,1)} %cbc.1, f32[8]{0:T(128)} %bias.1, ...), custom_call_target="tpu_custom_call" | custom-call | tf_op jit(solution)/shard_map/mix/pallas_call | solution.py:702
  123.7 2.1 %copy.14 = bf16[64,6144]{1,0:T(8,128)(2,1)} copy(bf16[64,6144]{1,0:T(8,128)(2,1)} %mix.1) | data formatting | bytes 1572864

commit v6 on v5

--- a/solution.py
+++ b/solution.py
@@ -20,6 +20,9 @@
 HALF_P = SPLIT // 2
 HALF_Q = 1280
 WIDE = D + 128
+SPLIT_IN = 3840
+HALF_P_IN = SPLIT_IN // 2
+HALF_Q_IN = (D - SPLIT_IN) // 2
 
 
 def place():
@@ -56,10 +59,12 @@
     later, before = (s + 1) % 8, (s + 7) % 8
     on_line = [span(line * 4 + (x + d) % 4, h, c) for d in (1, 2, 3)]
     across = span((1 - line) * 4 + x, h, c)
-    part_p, part_q = (0, SPLIT), (SPLIT, D - SPLIT)
-    p_a, p_b = (0, HALF_P), (HALF_P, SPLIT - HALF_P)
-    q_a, q_b = (SPLIT, HALF_Q), (SPLIT + HALF_Q, D - SPLIT - HALF_Q)
+    part_p, part_q = (0, SPLIT_IN), (SPLIT_IN, D - SPLIT_IN)
+    p_a, p_b = (0, HALF_P_IN), (HALF_P_IN, HALF_P_IN)
+    q_a, q_b = (SPLIT_IN, HALF_Q_IN), (SPLIT_IN + HALF_Q_IN, HALF_Q_IN)
     whole = (0, D)
+    p_one, p_two, p_rest = (0, 1280), (2560, 1280), (1280, 1280)
+    rest_a, rest_b = (1280, 640), (1920, 640)
 
     def at(yy, hh, cc, cols_):
         row = pl.multiple_of((yy * 4 + hh * 2 + cc) * ROWS, ROWS)
@@ -316,10 +321,12 @@
     arrive(8, down, n, part_q)
     send(25, down, n, part_q, dev_sib)
     arrive(13, down, n, part_p)
-    send(27, down, n, p_a, dev_up)
+    send(27, down, n, p_one, dev_up)
+    send(37, down, n, rest_a, dev_up)
     send(28, down, n, part_p, dev_sib)
     arrive(14, up, n, part_p)
-    send(29, up, n, p_b, dev_down)
+    send(29, up, n, p_two, dev_down)
+    send(38, up, n, rest_b, dev_down)
     send(30, up, n, part_p, dev_sib)
     arrive(25, down, n, part_q, sib=True)
     arrive(28, down, n, part_p, sib=True)
@@ -360,19 +367,27 @@
     arrive(31, far, n, q_a, sib=True)
     arrive(32, far, n, q_b, sib=True)
     project(7, part_q, keep=1)
-    arrive(27, far, n, p_a)
-    send(35, far, n, p_a, dev_sib)
-    arrive(29, far, n, p_b)
-    send(36, far, n, p_b, dev_sib)
+    arrive(27, far, n, p_one)
+    send(35, far, n, p_one, dev_sib)
+    arrive(29, far, n, p_two)
+    send(36, far, n, p_two, dev_sib)
     landed(mp.at[n, tap_own], z_s.at[8, 0], z_r.at[8, 0])
     for k in range(6):
         merged_there(k)
     for b in (y, up, down):
         bodies(b, lambda row, count: conv_map(0, row, count))
-    arrive(35, far, n, p_a, sib=True)
-    arrive(36, far, n, p_b, sib=True)
-
-    project_small(7, part_p, add=1)
+    arrive(37, far, n, rest_a)
+    send(39, far, n, rest_a, dev_sib)
+    arrive(38, far, n, rest_b)
+    send(40, far, n, rest_b, dev_sib)
+    arrive(35, far, n, p_one, sib=True)
+    project(7, p_one, keep=1, add=1)
+    arrive(36, far, n, p_two, sib=True)
+    project(7, p_two, keep=1, add=1)
+    arrive(39, far, n, rest_a, sib=True)
+    arrive(40, far, n, rest_b, sib=True)
+
+    project_small(7, p_rest, add=1)
     unit = pl.ds(unit_row(7), 2 * ROWS)
     push(bco.at[unit], bcs.at[unit], sib_s.at[7], sib_r.at[7], dev_sib)
     push(bco.at[unit], direct.at[0], z_s.at[7, 0], z_r.at[7, 0], dev_z)
@@ -380,7 +395,7 @@
     ending = pl.ds(SPAN - 16, 16)
     for k, (hh, cc) in enumerate(((h, c), (h, 1 - c), (n, c), (n, 1 - c))):
         push(bco.at[ending], halo_in.at[k], halo_s.at[1 + k], halo_r.at[1 + k], span(later, hh, cc))
-    project_wide(7, 0, part_p, add=1)
+    project_wide(7, 0, p_rest, add=1)
     last, first = pl.ds(SPAN, 16), pl.ds(0, 16)
     push(xp.at[last], xp.at[first], halo_s.at[0], halo_r.at[0], span(later, h, c))
     steps(far)
@@ -389,6 +404,9 @@
         push(decays.at[x], decays.at[x], line_s.at[11 + d], line_r.at[11 + d], on_line[d - 1])
     bodies(far, conv_x)
     heads(conv_x, 1, 4)
+    project_wide(7, 1, p_rest, add=1)
+    for b in (y, up, down):
+        bodies(b, lambda row, count: conv_map(1, row, count))
     merged_there(6)
     landed(bcs.at[unit], sib_s.at[7], sib_r.at[7])
     mp[h, pl.ds(pl.multiple_of(unit_row(7) + 16, 16), 2 * ROWS), :] = bco[unit, :] + bcs[unit, :]
@@ -426,9 +444,7 @@
             ref = states.at[x, :, lanes]
             push(ref, ref, line_s.at[part * 3 + d - 1], line_r.at[part * 3 + d - 1], on_line[d - 1])
 
-    project_wide(7, 1, part_p, add=1)
-    for b in (y, up, down, far):
-        bodies(b, lambda row, count: conv_map(1, row, count))
+    bodies(far, lambda row, count: conv_map(1, row, count))
     heads(lambda row, count: conv_map(1, row, count))
     pair_lane = lax.broadcasted_iota(jnp.int32, (128, 128), 1)
 
@@ -664,31 +680,33 @@
     add(down, h, q_b, qb)
     send(30, at(down, h, c, q_b), qf.at[1, :, in_q(q_b)], dev_down)
     arrive(21, zq.at[y])
+    add(y, h, part_q, zq.at[y])
     arrive(27, qf.at[0, :, in_q(q_b)])
+    add(y, h, q_b, qf.at[0, :, in_q(q_b)])
     arrive(28, qf.at[1, :, in_q(q_a)])
+    add(y, h, q_a, qf.at[1, :, in_q(q_a)])
+    arrive(30, qf.at[1, :, in_q(q_b)])
+    mine = at(y, h, c, (0, WIDE))
+    squares = mine[:, D:WIDE].astype(F32) + qf[1, :, D - SPLIT : WIDE - SPLIT].astype(F32)
+    scale = lax.rsqrt(squares / (COLS * 16) + 1e-05)
+
+    def deliver(cols, other, begin):
+        width = 256 if cols[1] % 512 else 512
+        wide = jnp.concatenate([scale] * (width // 128), axis=1)
+
+        @pl.loop(0, cols[1] // width)
+        def _(j):
+            here = pl.ds(pl.multiple_of(cols[0] + j * width, 128), width)
+            total = mine[:, here].astype(F32)
+            there = pl.ds(pl.multiple_of(cols[0] - begin + j * width, 128), width)
+            total = total + other[:, there].astype(F32)
+            out[:, here] = (total * wide).astype(BF16)
+
+    deliver((q_b[0], D - q_b[0]), qf.at[1], SPLIT)
     arrive(29, qf.at[0, :, in_q(q_a)])
-    arrive(30, qf.at[1, :, in_q(q_b)])
-    mine_q = at(y, h, c, part_q)
-    mine_p = at(y, h, c, part_p)
-    terms = (mine_q, zq.at[y], qf.at[0], qf.at[1])
-    lane = pl.ds(D - SPLIT, 128)
-    squares = sum(t[:, lane].astype(F32) for t in terms)
-    scale = lax.rsqrt(squares / (COLS * 16) + 1e-05)
-
-    @pl.loop(0, (D - SPLIT) // 128)
-    def _(j):
-        cols = pl.ds(pl.multiple_of(j * 128, 128), 128)
-        total = sum(t[:, cols].astype(F32) for t in terms)
-        out[:, pl.ds(pl.multiple_of(SPLIT + j * 128, 128), 128)] = (total * scale).astype(BF16)
-
+    deliver(q_a, qf.at[0], SPLIT)
     arrive(24, zp)
-
-    @pl.loop(0, SPLIT // 128)
-    def _(j):
-        cols = pl.ds(pl.multiple_of(j * 128, 128), 128)
-        total = mine_p[:, cols].astype(F32) + zp[:, cols].astype(F32)
-        out[:, cols] = (total * scale).astype(BF16)
-
+    deliver(part_p, zp, 0)
     for copy in started:
         copy.wait_send()
 
@@ -735,7 +753,7 @@
             pltpu.VMEM((4, 8, COLS), F32),
             pltpu.VMEM((STATE, COLS), BF16),
             pltpu.VMEM((STATE, COLS), BF16),
-            dma((37,)), dma((37,)), dma((6,)), dma((9,)), dma((9,)), dma((9, 2)), dma((9, 2)),
+            dma((41,)), dma((41,)), dma((6,)), dma((9,)), dma((9,)), dma((9, 2)), dma((9, 2)),
             dma((5,)), dma((5,)), dma((15,)), dma((15,)), dma((4,)), dma((4,)),
             pltpu.VMEM((SPAN, COLS), BF16),
             pltpu.VMEM((COLS, D), BF16),

time: 126 us -> 127 us (level)
  no operation moved by 1% of the time
where the time goes in v6:
time: 127 us; the launch traced here: 126 us
  Pallas kernels  124 us (98%)
  local copies, waits for them, and re-layouts  2.06 us (2%)
    pallas_call x1, Pallas kernels, mix(): pl.pallas_call(mixer_kernel, out_shape=jax.ShapeDtypeStruct((ROWS, D), BF...  124 us

profile of v6, /device:TPU:1, one launch (start us, length us, event | category | flops | bytes accessed | tf_op | source)
XLA Modules:
  0.0 126.4 jit_solution(17906099408806039259)
XLA Ops:
  0.0 124.4 %mix.1 = bf16[64,6144]{1,0:T(8,128)(2,1)} custom-call(bf16[64,6144]{1,0:T(8,128)(2,1)} %tok.1, bf16[6144,512]{1,0:T(8,128)(2,1)} %wx.1, bf16[6144,512]{1,0:T(8,128)(2,1)} %wz.1, bf16[64,6144]{1,0:T(8,128)(2,1)} %bitcast.2, bf16[8,6144]{1,0:T(8,128)(2,1)} %bitcast.3, bf16[4,512]{1,0:T(4,128)(2,1)} %cx.1, bf16[4,64]{1,0:T(4,128)(2,1)} %cbc.1, f32[8]{0:T(128)} %bias.1, ...), custom_call_target="tpu_custom_call" | custom-call | tf_op jit(solution)/shard_map/mix/pallas_call | solution.py:720
  124.4 2.1 %copy.14 = bf16[64,6144]{1,0:T(8,128)(2,1)} copy(bf16[64,6144]{1,0:T(8,128)(2,1)} %mix.1) | data formatting | bytes 1572864

commit v7 on v6

--- a/solution.py
+++ b/solution.py
@@ -20,7 +20,7 @@
 HALF_P = SPLIT // 2
 HALF_Q = 1280
 WIDE = D + 128
-SPLIT_IN = 3840
+SPLIT_IN = 3584
 HALF_P_IN = SPLIT_IN // 2
 HALF_Q_IN = (D - SPLIT_IN) // 2
 
@@ -63,8 +63,8 @@
     p_a, p_b = (0, HALF_P_IN), (HALF_P_IN, HALF_P_IN)
     q_a, q_b = (SPLIT_IN, HALF_Q_IN), (SPLIT_IN + HALF_Q_IN, HALF_Q_IN)
     whole = (0, D)
-    p_one, p_two, p_rest = (0, 1280), (2560, 1280), (1280, 1280)
-    rest_a, rest_b = (1280, 640), (1920, 640)
+    p_one, p_two, p_rest = (0, 1280), (2304, 1280), (1280, 1024)
+    rest_a, rest_b = (1280, 512), (1792, 512)
 
     def at(yy, hh, cc, cols_):
         row = pl.multiple_of((yy * 4 + hh * 2 + cc) * ROWS, ROWS)

time: 127 us -> 126 us (level)
  no operation moved by 1% of the time
where the time goes in v7:
time: 126 us
  Pallas kernels  124 us (98%)
  local copies, waits for them, and re-layouts  2.06 us (2%)
    pallas_call x1, Pallas kernels, mix(): pl.pallas_call(mixer_kernel, out_shape=jax.ShapeDtypeStruct((ROWS, D), BF...  124 us

profile of v7, /device:TPU:1, one launch (start us, length us, event | category | flops | bytes accessed | tf_op | source)
XLA Modules:
  0.0 126.0 jit_solution(10060963879412211053)
XLA Ops:
  0.0 123.9 %mix.1 = bf16[64,6144]{1,0:T(8,128)(2,1)} custom-call(bf16[64,6144]{1,0:T(8,128)(2,1)} %tok.1, bf16[6144,512]{1,0:T(8,128)(2,1)} %wx.1, bf16[6144,512]{1,0:T(8,128)(2,1)} %wz.1, bf16[64,6144]{1,0:T(8,128)(2,1)} %bitcast.2, bf16[8,6144]{1,0:T(8,128)(2,1)} %bitcast.3, bf16[4,512]{1,0:T(4,128)(2,1)} %cx.1, bf16[4,64]{1,0:T(4,128)(2,1)} %cbc.1, f32[8]{0:T(128)} %bias.1, ...), custom_call_target="tpu_custom_call" | custom-call | tf_op jit(solution)/shard_map/mix/pallas_call | solution.py:720
  123.9 2.1 %copy.14 = bf16[64,6144]{1,0:T(8,128)(2,1)} copy(bf16[64,6144]{1,0:T(8,128)(2,1)} %mix.1) | data formatting | bytes 1572864
